TPU v7x, 256 devices: a whole 4x4x8 slice. The times are simulated.
256 devices in a mesh: band: 32 (over z, x_lo, core), mem: 8 (over x_hi, y).
Axes of the slice: x: 4 (x_hi: 2, x_lo: 2; x = x_hi * 2 + x_lo), y: 4, z: 8, core: 2. Of those that a mesh axis runs over, the one named last changes fastest.
Arguments:
- hidden: bfloat16 [8, 16384, 1024], P('mem', 'band'), may hold values from -6 to 6
- gain: float32 [1024], replicated, may hold values from 0.5 to 1.5
- w_first: bfloat16 [1024, 1024], replicated, may hold values from -0.1875 to 0.1875
- w_second: bfloat16 [1024, 100], replicated, may hold values from -0.1875 to 0.1875
- target: float32 [100, 16384], P(None, 'band'), may hold values from -20 to 20
- patch_ids: int32 [16384], P('band'), may hold values from 0 to 63, as said below
- neighbours: int32 [6, 16384], P(None, 'band'), may hold values from 0 to 767, as said below
Outputs:
- loss: float32 [], replicated
- grad_hidden: bfloat16 [8, 16384, 1024], P('mem', 'band')
- grad_first: float32 [1024, 1024], P('band')
- grad_second: float32 [1024, 100], P('band')
Inputs may be any that keep to these rules, and one draw needn't show every extreme that they name: `patch_ids`: patches of band b are numbered b * 2 onward; every patch holds exactly 256 cells, all of one band. Index j stands for local cell j - 128; values under 128 are the previous band's last cells, values of 640 and over are the next band's first cells. A cell's neighbours lie within 128 cells of it.
All inputs are finite; a program needn't handle non-finite values.
Results may differ from a plain program's by a relative error of at most 0.02.
Values may be sent and summed in bfloat16 or wider, within the bound.
No kernel may reach another device: no remote copies, remote signals or barrier semaphores. Data moves between devices by JAX's collectives and lax.ppermute only.
A program may use at most 64 MiB of HBM per device.

v0:
```python
import functools
import math

import jax
import jax.numpy as jnp
from jax import lax
from jax.experimental import pallas as pl
from jax.experimental.pallas import tpu as pltpu
from jax.sharding import PartitionSpec as P

PATCH = 256
NEIGH = 6
HALO = 128
EPS_NORM = 1e-05
EPS_DIST = 1e-06
LANES = 128
F32 = jnp.float32
BF16 = jnp.bfloat16
VMEM = pl.BlockSpec(memory_space=pltpu.VMEM)


def dot(a, b, ca=1, cb=0):
    return lax.dot_general(a, b, (((ca,), (cb,)), ((), ())), preferred_element_type=F32)


def call(kernel, outs, args, flops, scratch=(), aliases=None):
    moved = sum(math.prod(a.shape) * a.dtype.itemsize for a in list(args) + list(outs))
    return pl.pallas_call(
        kernel,
        out_shape=outs,
        in_specs=[VMEM] * len(args),
        out_specs=[VMEM] * len(outs),
        scratch_shapes=list(scratch),
        input_output_aliases=aliases or {},
        compiler_params=pltpu.CompilerParams(vmem_limit_bytes=48 * 2**20),
        cost_estimate=pl.CostEstimate(flops=flops, bytes_accessed=moved, transcendentals=0),
    )(*args)


def shape(dims, kind):
    return jax.ShapeDtypeStruct(dims, kind)


def count_kernel(near_ref, counts_ref, turned_ref):
    near = near_ref[...]
    cells = near.shape[1]
    rows = cells + 2 * HALO
    for start in range(0, rows, HALO):
        place = lax.broadcasted_iota(jnp.int32, (HALO, cells), 0) + start
        total = jnp.zeros((HALO, cells), F32)
        for k in range(NEIGH):
            total = total + jnp.where(near[k : k + 1, :] == place, 1.0, 0.0)
        turned_ref[start : start + HALO, :] = total.astype(BF16)
        counts_ref[:, start : start + HALO] = total.T.astype(BF16)


def forward_kernel(
    before_ref, states_ref, after_ref, counts_ref, gain_ref, first_ref, second_ref,
    copies_ref, slope_ref, active_ref, normed_ref, inv_ref,
):
    cells, width = states_ref.shape
    rows = 128
    gain = gain_ref[...]
    for r in range(0, cells, rows):
        own = slice(r, r + rows)
        total = dot(counts_ref[own, HALO : HALO + cells], states_ref[...])
        total = total + dot(counts_ref[own, :HALO], before_ref[...])
        total = total + dot(counts_ref[own, HALO + cells :], after_ref[...])
        summed = states_ref[own, :].astype(F32) + total * (1.0 / NEIGH)
        centred = summed - jnp.mean(summed, -1, keepdims=True)
        inv_root = lax.rsqrt(jnp.mean(centred * centred, -1, keepdims=True) + EPS_NORM)
        normed_ref[own, :] = (centred * inv_root * gain).astype(BF16)
        inv_ref[own, :] = jnp.broadcast_to(inv_root, (rows, LANES))
    cols = 256
    for n in range(0, width, cols):
        part = slice(n, n + cols)
        preact = dot(normed_ref[...], first_ref[:, part])
        share = 0.5 * (1.0 + lax.erf(preact * math.sqrt(0.5)))
        active_ref[:, part] = (preact * share).astype(BF16)
        bell = jnp.exp(-0.5 * preact * preact) * (1.0 / math.sqrt(2.0 * math.pi))
        slope_ref[:, part] = (share + preact * bell).astype(BF16)
    predicted = dot(second_ref[...], active_ref[...], 0, 1).astype(BF16)
    for m in range(copies_ref.shape[0]):
        copies_ref[m] = predicted


def split_loss(tile, loss, fields):
    lane = lax.broadcasted_iota(jnp.int32, tile.shape, 1)
    high = loss.astype(BF16).astype(F32)
    low = loss - high
    return jnp.where(lane == fields, high, jnp.where(lane == fields + 1, low, tile))


def read_loss(tile, fields):
    lane = lax.broadcasted_iota(jnp.int32, tile.shape, 1)
    here = (lane == fields) | (lane == fields + 1)
    return jnp.sum(jnp.where(here, tile, 0.0), axis=1, keepdims=True)


def score_kernel(
    everyone_ref, target_ref, patch_ref, second_ref, slope_ref, active_ref, normed_ref,
    keep_ref, send_ref, dpre_ref, held_ref,
):
    members, fields, cells = everyone_ref.shape
    width = slope_ref.shape[1]
    me = lax.axis_index("mem")
    core = lax.axis_index("band") % 2
    entries = fields * PATCH
    own = everyone_ref[me].astype(F32)
    error = own - target_ref[...]
    sums = [jnp.sum(error * error, axis=0, keepdims=True)]
    for n in range(members):
        differ = own - everyone_ref[n].astype(F32)
        sums.append(jnp.sum(differ * differ, axis=0, keepdims=True))
    sums.append(jnp.zeros((16 - len(sums), cells), F32))
    sums = jnp.concatenate(sums, 0)
    even = (patch_ref[...] & 1) == 0
    spread_even = jnp.sqrt(jnp.sum(jnp.where(even, sums, 0.0), 1, keepdims=True) / entries + EPS_DIST)
    spread_odd = jnp.sqrt(jnp.sum(jnp.where(even, 0.0, sums), 1, keepdims=True) / entries + EPS_DIST)
    row = lax.broadcasted_iota(jnp.int32, (16, 1), 0)
    weight = jnp.where(row == 0, 1.0 / members, 1.0 / (members * (members - 1)))
    scale = jnp.where(even, weight / spread_even, weight / spread_odd)
    gradient = error * scale[0:1]
    for n in range(members):
        differ = own - everyone_ref[n].astype(F32)
        gradient = gradient - differ * scale[n + 1 : n + 2]
    both = spread_even + spread_odd
    used = jnp.where(row == 0, 1.0 / members, -0.5 / (members * (members - 1)))
    used = jnp.where((row == me + 1) | (row > members), 0.0, used)
    loss = jnp.sum(both * used, axis=0, keepdims=True)

    gradient = jnp.concatenate([gradient, jnp.zeros((LANES - fields, cells), F32)], 0)
    outer = gradient.T.astype(BF16)
    cols = 256
    for n in range(0, width, cols):
        part = slice(n, n + cols)
        d_active = dot(outer[:, :fields], second_ref[part, :], 1, 1)
        d_pre = (d_active * slope_ref[:, part].astype(F32)).astype(BF16)
        dpre_ref[:, part] = d_pre
        grad = dot(normed_ref[...], d_pre, 0, 0).astype(BF16)
        held_ref[:, :, part] = grad.reshape(held_ref.shape[0], -1, cols)
    second = dot(active_ref[...], outer, 0, 0)
    second = split_loss(second, loss, fields).astype(BF16)
    held_ref[:, :, width:] = second.reshape(held_ref.shape[0], -1, LANES)
    for k in range(keep_ref.shape[0]):
        keep_ref[k] = held_ref[2 * k + core]
        send_ref[k] = held_ref[2 * k + 1 - core]


def backward_kernel(
    dpre_ref, first_ref, normed_ref, gain_ref, inv_ref, turned_ref,
    grad_ref, edge_ref, up_ref, down_ref, total_ref, low_ref,
):
    cells, width = dpre_ref.shape
    rows = 128
    gain = gain_ref[...]
    for r in range(0, cells, rows):
        own = slice(r, r + rows)
        d_normed = dot(dpre_ref[own, :], first_ref[...], 1, 1)
        scaled = d_normed * gain
        normed = normed_ref[own, :].astype(F32)
        mean = jnp.mean(scaled, -1, keepdims=True)
        along = jnp.mean(d_normed * normed, -1, keepdims=True)
        inv_root = inv_ref[own, :1]
        d_summed = inv_root * (scaled - mean - normed / gain * along)
        total_ref[own, :] = d_summed
        low_ref[own, :] = d_summed.astype(BF16)
    up_ref[...] = (dot(turned_ref[:HALO, :], low_ref[...]) * (1.0 / NEIGH)).astype(BF16)
    down_ref[...] = (dot(turned_ref[cells + HALO :, :], low_ref[...]) * (1.0 / NEIGH)).astype(BF16)
    for r in range(0, cells, rows):
        own = slice(r, r + rows)
        back = dot(turned_ref[r + HALO : r + HALO + rows, :], low_ref[...]) * (1.0 / NEIGH)
        value = total_ref[own, :] + back
        grad_ref[own, :] = value.astype(BF16)
        if r == 0:
            edge_ref[0] = value
        if r + rows == cells:
            edge_ref[1] = value


def pair_kernel(fields, keep_ref, got_ref, out_ref):
    width = keep_ref.shape[2] - LANES
    for k in range(keep_ref.shape[0]):
        total = keep_ref[k].astype(F32) + got_ref[k].astype(F32)
        out_ref[k, :, :width] = total[:, :width].astype(BF16)
        tile = total[:, width:]
        out_ref[k, :, width:] = split_loss(tile, read_loss(tile, fields), fields).astype(BF16)


def fold_kernel(fields, parts_ref, out_ref):
    width = parts_ref.shape[2] - LANES
    total = parts_ref[0].astype(F32)
    for k in range(1, parts_ref.shape[0]):
        total = total + parts_ref[k].astype(F32)
    tile = total[:, width:]
    tile = split_loss(tile, read_loss(tile, fields), fields)
    total = jnp.concatenate([total[:, :width], tile], 1).astype(BF16)
    for m in range(out_ref.shape[0]):
        out_ref[m] = total


def last_kernel(fields, patches, parts_ref, first_ref, second_ref, loss_ref):
    width = first_ref.shape[1]
    total = parts_ref[0].astype(F32)
    for k in range(1, parts_ref.shape[0]):
        total = total + parts_ref[k].astype(F32)
    first_ref[...] = total[:, :width]
    tile = total[:, width:]
    second_ref[...] = tile[:, :fields]
    loss_ref[...] = read_loss(tile, fields)[:1, :] * (1.0 / patches)


def edge_kernel(grad_in_ref, edge_ref, before_ref, after_ref, grad_ref):
    del grad_in_ref
    step = pl.program_id(0)

    @pl.when(step == 0)
    def _():
        grad_ref[...] = (edge_ref[0] + before_ref[...].astype(F32)).astype(BF16)

    @pl.when(step == 1)
    def _():
        grad_ref[...] = (edge_ref[0] + after_ref[...].astype(F32)).astype(BF16)


def per_device(hidden, gain, w_first, w_second, target, patch_ids, neighbours):
    states = hidden[0]
    cells, width = states.shape
    fields = w_second.shape[1]
    bands, members = lax.axis_size("band"), lax.axis_size("mem")
    peers = bands // 2
    share = width // bands
    up = [(i, i + 1) for i in range(bands - 1)]
    down = [(j, i) for i, j in up]
    before = lax.ppermute(states[cells - HALO :], "band", up)
    after = lax.ppermute(states[:HALO], "band", down)
    gain = gain[None]
    counts, turned = call(
        count_kernel,
        [shape((cells, cells + 2 * HALO), BF16), shape((cells + 2 * HALO, cells), BF16)],
        [neighbours],
        10**8,
    )
    copies, slope, active, normed, inv_root = call(
        forward_kernel,
        [
            shape((members, fields, cells), BF16),
            shape((cells, width), BF16),
            shape((cells, width), BF16),
            shape((cells, width), BF16),
            shape((cells, LANES), F32),
        ],
        [before, states, after, counts, gain, w_first, w_second],
        2 * 10**9,
    )
    everyone = lax.all_to_all(copies, "mem", 0, 0)
    message = (peers, share, width + LANES)
    keep, send, d_pre = call(
        score_kernel,
        [shape(message, BF16), shape(message, BF16), shape((cells, width), BF16)],
        [everyone, target, patch_ids[None], w_second, slope, active, normed],
        2 * 10**9,
        scratch=[pltpu.VMEM((bands, share, width + LANES), BF16)],
    )
    got = lax.ppermute(send, "band", [(i, i ^ 1) for i in range(bands)])
    grad, edge, rim_up, rim_down = call(
        backward_kernel,
        [
            shape((cells, width), BF16),
            shape((2, HALO, width), F32),
            shape((HALO, width), BF16),
            shape((HALO, width), BF16),
        ],
        [d_pre, w_first, normed, gain, inv_root, turned],
        2 * 10**9,
        scratch=[pltpu.VMEM((cells, width), F32), pltpu.VMEM((cells, width), BF16)],
    )
    rim_after = lax.ppermute(rim_up, "band", down)
    rim_before = lax.ppermute(rim_down, "band", up)
    (mine,) = call(
        functools.partial(pair_kernel, fields), [shape(message, BF16)], [keep, got], 10**6
    )
    groups = [[2 * k + c for k in range(peers)] for c in range(2)]
    parts = lax.all_to_all(mine, "band", 0, 0, axis_index_groups=groups)
    (shared,) = call(
        functools.partial(fold_kernel, fields),
        [shape((members,) + message[1:], BF16)],
        [parts],
        10**6,
    )
    parts = lax.all_to_all(shared, "mem", 0, 0)
    grad_first, grad_second, loss = call(
        functools.partial(last_kernel, fields, cells // PATCH * bands),
        [shape((share, width), F32), shape((share, fields), F32), shape((1, 1), F32)],
        [parts],
        10**6,
    )
    last = cells // HALO - 1
    grad_hidden = pl.pallas_call(
        edge_kernel,
        grid=(2,),
        out_shape=shape((cells, width), BF16),
        in_specs=[
            pl.BlockSpec(memory_space=pl.ANY),
            pl.BlockSpec((1, HALO, width), lambda i: (i, 0, 0)),
            pl.BlockSpec((HALO, width), lambda i: (0, 0)),
            pl.BlockSpec((HALO, width), lambda i: (0, 0)),
        ],
        out_specs=pl.BlockSpec((HALO, width), lambda i: (i * last, 0)),
        input_output_aliases={0: 0},
        compiler_params=pltpu.CompilerParams(vmem_limit_bytes=16 * 2**20),
    )(grad, edge, rim_before, rim_after)
    return (loss[0, 0], grad_hidden[None], grad_first, grad_second)


def solution(mesh):
    return jax.shard_map(
        per_device,
        mesh=mesh,
        in_specs=(
            P("mem", "band", None),
            P(),
            P(),
            P(),
            P(None, "band"),
            P("band"),
            P(None, "band"),
        ),
        out_specs=(P(), P("mem", "band", None), P("band", None), P("band", None)),
        check_vma=False,
    )
```

profile of v0, /device:TPU:7, one launch (start us, length us, event | category | flops | bytes accessed | tf_op | source)
XLA Modules:
  0.0 117.5 jit_solution(11932513288159938551)
XLA Ops:
  0.6 0.0 copy-start.7
  0.6 0.0 copy-start.2
  0.7 0.0 copy-start.3
  0.7 1.1 slice_bitcast_fusion
  1.8 2.6 %collective-permute-start.1 = (bf16[128,1024]{1,0:T(8,128)(2,1)S(1)}, bf16[128,1024]{1,0:T(8,128)(2,1)S(1)}, u32[]{:S(2)}, u32[]{:S(2)}) collective-permute-start(bf16[128,1024]{1,0:T(8,128)(2,1)S(1)} %get-tuple-element.38), channel_id=1, source_target_pairs={{8,0},{16,8},{24,16},{32,24},{40,32},{48,40},{56,48},{64,56},{72,6... | collective-permute-start | bytes 786440 | tf_op jit(solution)/shard_map/ppermute | solution.py:236
  4.4 3.9 %collective-permute-start = (bf16[128,1024]{1,0:T(8,128)(2,1)S(1)}, bf16[128,1024]{1,0:T(8,128)(2,1)S(1)}, u32[]{:S(2)}, u32[]{:S(2)}) collective-permute-start(bf16[128,1024]{1,0:T(8,128)(2,1)S(1)} %get-tuple-element.39), channel_id=1, source_target_pairs={{0,8},{8,16},{16,24},{24,32},{32,40},{40,48},{48,56},{56,64},{64,7... | collective-permute-start | bytes 786440 | tf_op jit(solution)/shard_map/ppermute | solution.py:235
  8.3 0.0 copy-done.7
  8.3 0.2 copy.12.second_ref
  8.4 0.0 copy-done.2
  8.5 1.1 shard_map.102
  9.5 0.9 collective-permute-done.1.after_ref
  10.5 1.1 collective-permute-done.before_ref
  11.5 0.0 copy-done.3
  11.6 5.6 %shard_map.103 = (bf16[8,100,512]{2,1,0:T(8,128)(2,1)S(1)}, bf16[512,1024]{1,0:T(8,128)(2,1)S(1)}, bf16[512,1024]{1,0:T(8,128)(2,1)S(1)}, bf16[512,1024]{1,0:T(8,128)(2,1)S(1)}, f32[512,128]{1,0:T(8,128)S(1)}) custom-call(bf16[128,1024]{1,0:T(8,128)(2,1)S(1)} %collective-permute-done.before_ref, bf16[512,1024]{1,0:T(8,128)(2,1)} %bitcast.13, ...), custom_call_target="tpu_custom_call" | custom-call | flops 2000000000 | bytes 8892416 | tf_op jit(solution)/shard_map/pallas_call | solution.py:28
  17.2 0.0 copy-start.1
  17.2 0.0 copy-start.4
  17.2 16.4 %all_to_all.15.everyone_ref = bf16[8,100,512]{2,1,0:T(8,128)(2,1)S(1)} all-to-all(bf16[8,100,512]{2,1,0:T(8,128)(2,1)S(1)} %get-tuple-element.22), channel_id=1, replica_groups=mesh['band'=32,'mem'=8] {'mem'}, dimensions={0} | all-to-all | bytes 1638400 | tf_op jit(solution)/shard_map/all_to_all | solution.py:256
  33.6 0.0 copy-done.1
  33.6 0.0 copy-done.4
  33.6 5.1 %shard_map.104 = (bf16[16,32,1152]{2,1,0:T(8,128)(2,1)}, bf16[16,32,1152]{2,1,0:T(8,128)(2,1)}, bf16[512,1024]{1,0:T(8,128)(2,1)S(1)}) custom-call(bf16[8,100,512]{2,1,0:T(8,128)(2,1)S(1)} %all_to_all.15.everyone_ref, f32[100,512]{1,0:T(8,128)S(1)} %copy-done.1, s32[1,512]{1,0:T(1,128)S(1)} %bitcast.11, bf16[1024,100]{1,0:T(8,128)(2,1)S(1)} %copy.12.second_ref, ...), custom_call_target="tpu_custom_call" | custom-call | flops 2000000000 | bytes 7784448 | tf_op jit(solution)/shard_map/pallas_call | solution.py:28
  38.7 0.0 copy-start.5
  38.7 1.0 copy-done.5
  39.6 3.9 %collective-permute-start.2 = (bf16[16,32,1152]{2,1,0:T(8,128)(2,1)}, bf16[16,32,1152]{2,1,0:T(8,128)(2,1)S(1)}, u32[]{:S(2)}, u32[]{:S(2)}) collective-permute-start(bf16[16,32,1152]{2,1,0:T(8,128)(2,1)} %get-tuple-element.27), channel_id=1, source_target_pairs={{0,8},{8,0},{16,24},{24,16},{32,40},{40,32},{48,56},{56,48},{64,72... | collective-permute-start | bytes 3538952 | tf_op jit(solution)/shard_map/ppermute | solution.py:265
  43.5 2.7 %collective-permute-done.2.got_ref = bf16[16,32,1152]{2,1,0:T(8,128)(2,1)S(1)} collective-permute-done((bf16[16,32,1152]{2,1,0:T(8,128)(2,1)}, bf16[16,32,1152]{2,1,0:T(8,128)(2,1)S(1)}, u32[]{:S(2)}, u32[]{:S(2)}) %collective-permute-start.2) | collective-permute-done | bytes 1179680 | tf_op jit(solution)/shard_map/ppermute | solution.py:265
  46.2 0.0 copy-start
  46.2 1.3 %copy-done = bf16[16,32,1152]{2,1,0:T(8,128)(2,1)S(1)} copy-done((bf16[16,32,1152]{2,1,0:T(8,128)(2,1)S(1)}, bf16[16,32,1152]{2,1,0:T(8,128)(2,1)}, u32[]{:S(2)}) %copy-start) | copy-done | bytes 1179672
  47.5 0.4 shard_map.105
  47.9 38.8 %all_to_all.16.parts_ref = bf16[16,32,1152]{2,1,0:T(8,128)(2,1)S(1)} all-to-all(bf16[16,32,1152]{2,1,0:T(8,128)(2,1)S(1)} %shard_map.105), channel_id=1, replica_groups={{0,16,32,48,64,80,96,112,128,144,160,176,192,208,224,240},{8,24,40,56,7..., dimensions={0} | all-to-all | bytes 2359296 | tf_op jit(solution)/shard_map/all_to_all | solution.py:284
  86.7 1.0 shard_map.106
  87.7 6.7 %all-to-all-start.2 = ((bf16[8,32,1152]{2,1,0:T(8,128)(2,1)}), bf16[8,32,1152]{2,1,0:T(8,128)(2,1)S(1)}, u32[]{:S(2)}, u32[]{:S(2)}) async-start(bf16[8,32,1152]{2,1,0:T(8,128)(2,1)} %shard_map.106), calls=%async_computation.2 | async-start | bytes 1179648 | tf_op jit(solution)/shard_map/all_to_all | solution.py:291
  94.4 0.0 copy-start.6
  94.4 1.2 %copy-done.6 = bf16[512,1024]{1,0:T(8,128)(2,1)S(1)} copy-done((bf16[512,1024]{1,0:T(8,128)(2,1)S(1)}, bf16[512,1024]{1,0:T(8,128)(2,1)}, u32[]{:S(2)}) %copy-start.6) | copy-done | bytes 1048600
  95.7 6.9 %shard_map.108 = (bf16[512,1024]{1,0:T(8,128)(2,1)}, f32[2,128,1024]{2,1,0:T(8,128)S(1)}, bf16[128,1024]{1,0:T(8,128)(2,1)S(1)}, bf16[128,1024]{1,0:T(8,128)(2,1)S(1)}) custom-call(bf16[512,1024]{1,0:T(8,128)(2,1)S(1)} %copy-done.6, bf16[1024,1024]{1,0:T(8,128)(2,1)} %first_ref.3, bf16[512,1024]{1,0:T(8,128)(2,1)S(1)} %get-tuple-element.25.normed_ref, ...), custom_call_target="tpu_custom_call" | custom-call | flops 2000000000 | bytes 7868416 | tf_op jit(solution)/shard_map/pallas_call | solution.py:28
  102.5 4.8 %collective-permute-start.3 = (bf16[128,1024]{1,0:T(8,128)(2,1)S(1)}, bf16[128,1024]{1,0:T(8,128)(2,1)S(1)}, u32[]{:S(2)}, u32[]{:S(2)}) collective-permute-start(bf16[128,1024]{1,0:T(8,128)(2,1)S(1)} %get-tuple-element.34), channel_id=1, source_target_pairs={{0,8},{8,16},{16,24},{24,32},{32,40},{40,48},{48,56},{56,64},{64,7... | collective-permute-start | bytes 786440 | tf_op jit(solution)/shard_map/ppermute | solution.py:279
  107.3 1.9 %collective-permute-start.4 = (bf16[128,1024]{1,0:T(8,128)(2,1)S(1)}, bf16[128,1024]{1,0:T(8,128)(2,1)S(1)}, u32[]{:S(2)}, u32[]{:S(2)}) collective-permute-start(bf16[128,1024]{1,0:T(8,128)(2,1)S(1)} %get-tuple-element.35), channel_id=1, source_target_pairs={{8,0},{16,8},{24,16},{32,24},{40,32},{48,40},{56,48},{64,56},{72,6... | collective-permute-start | bytes 786440 | tf_op jit(solution)/shard_map/ppermute | solution.py:278
  109.2 1.4 %collective-permute-done.3.before_ref = bf16[128,1024]{1,0:T(8,128)(2,1)S(1)} collective-permute-done((bf16[128,1024]{1,0:T(8,128)(2,1)S(1)}, bf16[128,1024]{1,0:T(8,128)(2,1)S(1)}, u32[]{:S(2)}, u32[]{:S(2)}) %collective-permute-start.3) | collective-permute-done | bytes 262176 | tf_op jit(solution)/shard_map/ppermute | solution.py:279
  110.6 5.3 %collective-permute-done.4.after_ref = bf16[128,1024]{1,0:T(8,128)(2,1)S(1)} collective-permute-done((bf16[128,1024]{1,0:T(8,128)(2,1)S(1)}, bf16[128,1024]{1,0:T(8,128)(2,1)S(1)}, u32[]{:S(2)}, u32[]{:S(2)}) %collective-permute-start.4) | collective-permute-done | bytes 262176 | tf_op jit(solution)/shard_map/ppermute | solution.py:278
  115.9 0.9 shard_map.109
  116.7 0.0 all-to-all-done.2.parts_ref
  116.7 0.7 shard_map.107
Async XLA Ops:
  0.6 7.6 %copy-start.7 = (bf16[1024,100]{0,1:T(8,128)(2,1)S(1)}, bf16[1024,100]{0,1:T(8,128)(2,1)}, u32[]{:S(2)}) copy-start(bf16[1024,100]{0,1:T(8,128)(2,1)} %param.10) | copy-start | bytes 614404
  0.6 7.8 %copy-start.2 = (s32[6,512]{1,0:T(8,128)S(1)}, s32[6,512]{1,0:T(8,128)}, u32[]{:S(2)}) copy-start(s32[6,512]{1,0:T(8,128)} %near_ref.1) | copy-start | bytes 36868
  0.7 10.9 %copy-start.3 = (f32[1024]{0:T(1024)S(1)}, f32[1024]{0:T(1024)}, u32[]{:S(2)}) copy-start(f32[1024]{0:T(1024)} %param.8) | copy-start | bytes 12292
  1.8 8.7 %collective-permute-start.1 = (bf16[128,1024]{1,0:T(8,128)(2,1)S(1)}, bf16[128,1024]{1,0:T(8,128)(2,1)S(1)}, u32[]{:S(2)}, u32[]{:S(2)}) collective-permute-start(bf16[128,1024]{1,0:T(8,128)(2,1)S(1)} %get-tuple-element.38), channel_id=1, source_target_pairs={{8,0},{16,8},{24,16},{32,24},{40,32},{48,40},{56,48},{64,56},{72,6... | collective-permute-start | bytes 786440 | tf_op jit(solution)/shard_map/ppermute | solution.py:236
  4.4 7.2 %collective-permute-start = (bf16[128,1024]{1,0:T(8,128)(2,1)S(1)}, bf16[128,1024]{1,0:T(8,128)(2,1)S(1)}, u32[]{:S(2)}, u32[]{:S(2)}) collective-permute-start(bf16[128,1024]{1,0:T(8,128)(2,1)S(1)} %get-tuple-element.39), channel_id=1, source_target_pairs={{0,8},{8,16},{16,24},{24,32},{32,40},{40,48},{48,56},{56,64},{64,7... | collective-permute-start | bytes 786440 | tf_op jit(solution)/shard_map/ppermute | solution.py:235
  17.2 16.4 %copy-start.1 = (f32[100,512]{1,0:T(8,128)S(1)}, f32[100,512]{1,0:T(8,128)}, u32[]{:S(2)}) copy-start(f32[100,512]{1,0:T(8,128)} %target_ref.1) | copy-start | bytes 614404
  17.2 16.4 %copy-start.4 = (s32[512]{0:T(512)S(1)}, s32[512]{0:T(512)}, u32[]{:S(2)}) copy-start(s32[512]{0:T(512)} %param.12) | copy-start | bytes 6148
  38.7 1.0 copy-start.5
  39.6 6.6 %collective-permute-start.2 = (bf16[16,32,1152]{2,1,0:T(8,128)(2,1)}, bf16[16,32,1152]{2,1,0:T(8,128)(2,1)S(1)}, u32[]{:S(2)}, u32[]{:S(2)}) collective-permute-start(bf16[16,32,1152]{2,1,0:T(8,128)(2,1)} %get-tuple-element.27), channel_id=1, source_target_pairs={{0,8},{8,0},{16,24},{24,16},{32,40},{40,32},{48,56},{56,48},{64,72... | collective-permute-start | bytes 3538952 | tf_op jit(solution)/shard_map/ppermute | solution.py:265
  46.2 1.3 %copy-start = (bf16[16,32,1152]{2,1,0:T(8,128)(2,1)S(1)}, bf16[16,32,1152]{2,1,0:T(8,128)(2,1)}, u32[]{:S(2)}) copy-start(bf16[16,32,1152]{2,1,0:T(8,128)(2,1)} %get-tuple-element.26.keep_ref) | copy-start | bytes 3538948
  87.7 29.0 %all-to-all-start.2 = ((bf16[8,32,1152]{2,1,0:T(8,128)(2,1)}), bf16[8,32,1152]{2,1,0:T(8,128)(2,1)S(1)}, u32[]{:S(2)}, u32[]{:S(2)}) async-start(bf16[8,32,1152]{2,1,0:T(8,128)(2,1)} %shard_map.106), calls=%async_computation.2 | async-start | bytes 1179648 | tf_op jit(solution)/shard_map/all_to_all | solution.py:291
  94.4 1.2 %copy-start.6 = (bf16[512,1024]{1,0:T(8,128)(2,1)S(1)}, bf16[512,1024]{1,0:T(8,128)(2,1)}, u32[]{:S(2)}) copy-start(bf16[512,1024]{1,0:T(8,128)(2,1)} %copy-done.5) | copy-start | bytes 3145732
  102.5 8.1 %collective-permute-start.3 = (bf16[128,1024]{1,0:T(8,128)(2,1)S(1)}, bf16[128,1024]{1,0:T(8,128)(2,1)S(1)}, u32[]{:S(2)}, u32[]{:S(2)}) collective-permute-start(bf16[128,1024]{1,0:T(8,128)(2,1)S(1)} %get-tuple-element.34), channel_id=1, source_target_pairs={{0,8},{8,16},{16,24},{24,32},{32,40},{40,48},{48,56},{56,64},{64,7... | collective-permute-start | bytes 786440 | tf_op jit(solution)/shard_map/ppermute | solution.py:279
  107.3 8.6 %collective-permute-start.4 = (bf16[128,1024]{1,0:T(8,128)(2,1)S(1)}, bf16[128,1024]{1,0:T(8,128)(2,1)S(1)}, u32[]{:S(2)}, u32[]{:S(2)}) collective-permute-start(bf16[128,1024]{1,0:T(8,128)(2,1)S(1)} %get-tuple-element.35), channel_id=1, source_target_pairs={{8,0},{16,8},{24,16},{32,24},{40,32},{48,40},{56,48},{64,56},{72,6... | collective-permute-start | bytes 786440 | tf_op jit(solution)/shard_map/ppermute | solution.py:278
where the time goes:
time: 118 us; the launch traced here: 117 us
  blocking collectives  55.2 us (47%)
  starting transfers between devices  23.7 us (20%)
  Pallas kernels  21.6 us (18%)
  waiting for transfers between devices  11.4 us (10%)
  local copies, waits for them, and re-layouts  4.78 us (4%)
    all_to_all x1, blocking collectives, per_device(): parts = lax.all_to_all(mine, 'band', 0, 0, axis_index_groups=groups)  38.8 us
    pallas_call x7, Pallas kernels, call(): pl.pallas_call(kernel, out_shape=outs, in_specs=[VMEM] * len(args), out_s...  20.8 us
    all_to_all x1, blocking collectives, per_device(): everyone = lax.all_to_all(copies, 'mem', 0, 0)  16.4 us
    all_to_all x1, starting transfers between devices, per_device(): parts = lax.all_to_all(shared, 'mem', 0, 0)  6.71 us
    ppermute x1, waiting for transfers between devices, per_device(): rim_after = lax.ppermute(rim_up, 'band', down)  5.29 us
    ppermute x1, starting transfers between devices, per_device(): rim_before = lax.ppermute(rim_down, 'band', up)  4.76 us
    ppermute x1, starting transfers between devices, per_device(): got = lax.ppermute(send, 'band', [(i, i ^ 1) for i in range(bands)])  3.89 us
    ppermute x1, starting transfers between devices, per_device(): before = lax.ppermute(states[cells - HALO:], 'band', up)  3.88 us
  transfers between devices with their start and end apart: 6, of which 5 were waited for; matrix products, arithmetic and copies ran while one was open for 0% of the time, Pallas kernels for 7%

commit v1 on v0

v1 whole, which is shorter than its diff:
```python
import functools
import math

import jax
import jax.numpy as jnp
from jax import lax
from jax.experimental import pallas as pl
from jax.experimental.pallas import tpu as pltpu
from jax.sharding import PartitionSpec as P

PATCH = 256
NEIGH = 6
HALO = 128
EPS_NORM = 1e-05
EPS_DIST = 1e-06
LANES = 128
F32 = jnp.float32
BF16 = jnp.bfloat16
VMEM = pl.BlockSpec(memory_space=pltpu.VMEM)
ANY = pl.BlockSpec(memory_space=pl.ANY)


def dot(a, b, ca=1, cb=0):
    return lax.dot_general(a, b, (((ca,), (cb,)), ((), ())), preferred_element_type=F32)


def call(kernel, outs, args, flops, limit, scratch=(), anywhere=(), stored=(), held=()):
    args = [
        pltpu.with_memory_space_constraint(a, pltpu.HBM) if i in anywhere else a
        for i, a in enumerate(args)
    ]
    moved = sum(math.prod(a.shape) * a.dtype.itemsize for a in list(args) + list(outs))
    return pl.pallas_call(
        kernel,
        out_shape=[
            pltpu.HBM(o.shape, o.dtype) if i in stored else pltpu.VMEM(o.shape, o.dtype) if i in held else o
            for i, o in enumerate(outs)
        ],
        in_specs=[ANY if i in anywhere else VMEM for i in range(len(args))],
        out_specs=[ANY if i in stored else VMEM for i in range(len(outs))],
        scratch_shapes=list(scratch),
        compiler_params=pltpu.CompilerParams(vmem_limit_bytes=limit * 2**20),
        cost_estimate=pl.CostEstimate(flops=flops, bytes_accessed=moved, transcendentals=0),
    )(*args)


def shape(dims, kind):
    return jax.ShapeDtypeStruct(dims, kind)


def count_rows(near, block):
    near = near[:, block * HALO : (block + 1) * HALO]
    place = lax.broadcasted_iota(jnp.int32, (3 * HALO, HALO), 0) + block * HALO
    total = jnp.zeros((3 * HALO, HALO), F32)
    for k in range(NEIGH):
        total = total + jnp.where(near[k : k + 1, :] == place, 1.0, 0.0)
    return total


def normalise(summed, gain):
    centred = summed - jnp.mean(summed, -1, keepdims=True)
    inv_root = lax.rsqrt(jnp.mean(centred * centred, -1, keepdims=True) + EPS_NORM)
    normed = (centred * inv_root * gain).astype(BF16)
    return normed, jnp.broadcast_to(inv_root, (summed.shape[0], LANES))


def head(normed_ref, first_ref, part):
    preact = dot(normed_ref[...], first_ref[:, part])
    share = 0.5 * (1.0 + lax.erf(preact * math.sqrt(0.5)))
    bell = jnp.exp(-0.5 * preact * preact) * (1.0 / math.sqrt(2.0 * math.pi))
    return (preact * share).astype(BF16), (share + preact * bell).astype(BF16)


def inner_kernel(
    near_ref, states_ref, gain_ref, second_ref, first_hbm,
    predicted_ref, slope_ref, active_ref, normed_ref, inv_ref, first_ref,
    done,
):
    load = pltpu.make_async_copy(first_hbm, first_ref, done)
    load.start()
    near = near_ref[...]
    for block in (1, 2):
        reach = states_ref[(block - 1) * HALO : (block + 2) * HALO, :]
        counts = count_rows(near, block).T.astype(BF16)
        own = states_ref[block * HALO : (block + 1) * HALO, :].astype(F32)
        summed = own + dot(counts, reach) * (1.0 / NEIGH)
        to = slice((block - 1) * HALO, block * HALO)
        normed_ref[to, :], inv_ref[to, :] = normalise(summed, gain_ref[...])
    load.wait()
    cols = 256
    for n in range(0, normed_ref.shape[1], cols):
        part = slice(n, n + cols)
        active_ref[:, part], slope_ref[:, part] = head(normed_ref, first_ref, part)
    predicted_ref[...] = dot(second_ref[...], active_ref[...], 1, 1).astype(BF16)


def prepare_kernel(near_ref, states_ref, partial_ref, outside_ref, turned_ref):
    near = near_ref[...]
    blocks = states_ref.shape[0] // HALO
    for block in range(blocks):
        cells = slice(block * HALO, (block + 1) * HALO)
        total = count_rows(near, block)
        turned_ref[block * HALO : (block + 3) * HALO, cells] = total.astype(BF16)
        if block in (0, blocks - 1):
            edge = 0 if block == 0 else 1
            to = slice(edge * HALO, (edge + 1) * HALO)
            counts = total.T.astype(BF16)
            inside = slice(HALO, 3 * HALO) if edge == 0 else slice(0, 2 * HALO)
            outside = slice(0, HALO) if edge == 0 else slice(2 * HALO, 3 * HALO)
            start = 0 if edge == 0 else (blocks - 2) * HALO
            reach = states_ref[start : start + 2 * HALO, :]
            partial_ref[to, :] = states_ref[cells, :].astype(F32) + dot(counts[:, inside], reach) * (
                1.0 / NEIGH
            )
            outside_ref[edge] = counts[:, outside]


def outer_kernel(
    before_ref, after_ref, partial_ref, outside_ref, gain_ref, second_ref,
    predicted_in_ref, slope_in_ref, active_in_ref, normed_in_ref, inv_in_ref, first_ref,
    copies_ref, slope_ref, active_ref, normed_ref, inv_ref,
    own_ref,
):
    cells, width = normed_ref.shape
    top, inner, bottom = slice(0, HALO), slice(HALO, cells - HALO), slice(cells - HALO, cells)
    for edge, (rows_ref, place) in enumerate(((before_ref, top), (after_ref, bottom))):
        to = slice(edge * HALO, (edge + 1) * HALO)
        summed = partial_ref[to, :] + dot(outside_ref[edge], rows_ref[...]) * (1.0 / NEIGH)
        normed, inv_ref[place, :] = normalise(summed, gain_ref[...])
        normed_ref[place, :] = normed
        own_ref[to, :] = normed
    normed_ref[inner, :] = normed_in_ref[...]
    inv_ref[inner, :] = inv_in_ref[...]
    active_ref[inner, :] = active_in_ref[...]
    slope_ref[inner, :] = slope_in_ref[...]
    cols = 256
    for n in range(0, width, cols):
        part = slice(n, n + cols)
        active, slope = head(own_ref, first_ref, part)
        active_ref[top, part] = active[:HALO]
        active_ref[bottom, part] = active[HALO:]
        slope_ref[top, part] = slope[:HALO]
        slope_ref[bottom, part] = slope[HALO:]
    own = jnp.concatenate([active_ref[top, :], active_ref[bottom, :]], 0)
    predicted = dot(second_ref[...], own, 1, 1).astype(BF16)
    for m in range(copies_ref.shape[0]):
        copies_ref[m, :, top] = predicted[:, :HALO]
        copies_ref[m, :, inner] = predicted_in_ref[...]
        copies_ref[m, :, bottom] = predicted[:, HALO:]


def split_loss(tile, loss, fields):
    lane = lax.broadcasted_iota(jnp.int32, tile.shape, 1)
    high = loss.astype(BF16).astype(F32)
    low = loss - high
    return jnp.where(lane == fields, high, jnp.where(lane == fields + 1, low, tile))


def read_loss(tile, fields):
    lane = lax.broadcasted_iota(jnp.int32, tile.shape, 1)
    here = (lane == fields) | (lane == fields + 1)
    return jnp.sum(jnp.where(here, tile, 0.0), axis=1, keepdims=True)


def score_kernel(
    everyone_ref, target_ref, patch_ref, second_ref, slope_ref, active_ref, normed_ref,
    keep_ref, send_ref, dpre_ref, held_ref,
):
    members, fields, cells = everyone_ref.shape
    width = slope_ref.shape[1]
    me = lax.axis_index("xh") * lax.axis_size("y") + lax.axis_index("y")
    core = lax.axis_index("co")
    entries = fields * PATCH
    share = held_ref.shape[3]

    def target_of(xl, member):
        return (member % 4) * 4 + (member // 4) * 2 + xl

    places = [(b, ((b // 2) % 2, b // 4)) for b in range(width // share)]
    own = everyone_ref[me].astype(F32)
    error = own - target_ref[...]
    sums = [jnp.sum(error * error, axis=0, keepdims=True)]
    for n in range(members):
        differ = own - everyone_ref[n].astype(F32)
        sums.append(jnp.sum(differ * differ, axis=0, keepdims=True))
    sums.append(jnp.zeros((16 - len(sums), cells), F32))
    sums = jnp.concatenate(sums, 0)
    even = (patch_ref[...] & 1) == 0
    spread_even = jnp.sqrt(jnp.sum(jnp.where(even, sums, 0.0), 1, keepdims=True) / entries + EPS_DIST)
    spread_odd = jnp.sqrt(jnp.sum(jnp.where(even, 0.0, sums), 1, keepdims=True) / entries + EPS_DIST)
    row = lax.broadcasted_iota(jnp.int32, (16, 1), 0)
    weight = jnp.where(row == 0, 1.0 / members, 1.0 / (members * (members - 1)))
    scale = jnp.where(even, weight / spread_even, weight / spread_odd)
    gradient = error * scale[0:1]
    for n in range(members):
        differ = own - everyone_ref[n].astype(F32)
        gradient = gradient - differ * scale[n + 1 : n + 2]
    both = spread_even + spread_odd
    used = jnp.where(row == 0, 1.0 / members, -0.5 / (members * (members - 1)))
    used = jnp.where((row == me + 1) | (row > members), 0.0, used)
    loss = jnp.sum(both * used, axis=0, keepdims=True)

    gradient = jnp.concatenate([gradient, jnp.zeros((LANES - fields, cells), F32)], 0)
    outer = gradient.T.astype(BF16)
    cols = 256
    for n in range(0, width, cols):
        part = slice(n, n + cols)
        d_active = dot(outer[:, :fields], second_ref[:, part])
        d_pre = (d_active * slope_ref[:, part].astype(F32)).astype(BF16)
        dpre_ref[:, part] = d_pre
        grad = dot(normed_ref[...], d_pre, 0, 0).astype(BF16)
        for band, slot in places:
            rows = grad[band * share : (band + 1) * share]
            for c in range(0, cols, LANES):
                block = (n + c) // LANES
                held_ref[band % 2, target_of(slot[0], block), slot[1]] = rows[:, c : c + LANES]
    second = dot(active_ref[...], outer, 0, 0)
    second = split_loss(second, loss, fields).astype(BF16)
    for band, slot in places:
        rows = second[band * share : (band + 1) * share]
        held_ref[band % 2, target_of(slot[0], slot[1]), members] = rows
    keep_ref[...] = held_ref[core]
    send_ref[...] = held_ref[1 - core]


def backward_kernel(
    first_ref, dpre_ref, normed_ref, inv_ref, turned_ref, gain_ref,
    grad_hbm, edge_hbm, up_hbm, down_hbm,
    total_ref, low_ref, grad_ref, edge_ref, rim_ref, done,
):
    cells, width = low_ref.shape
    blocks = cells // HALO
    gain = gain_ref[...]
    inverse = 1.0 / gain
    saves = [
        pltpu.make_async_copy(source, place, done.at[i])
        for i, (source, place) in enumerate(
            [
                (rim_ref.at[0], up_hbm),
                (rim_ref.at[1], down_hbm),
                (edge_ref, edge_hbm),
                (grad_ref, grad_hbm),
            ]
        )
    ]
    for block in range(blocks):
        own = slice(block * HALO, (block + 1) * HALO)
        d_normed = dot(dpre_ref[own, :], first_ref[...], 1, 1)
        scaled = d_normed * gain
        normed = normed_ref[own, :].astype(F32)
        mean = jnp.mean(scaled, -1, keepdims=True)
        along = jnp.mean(d_normed * normed, -1, keepdims=True)
        d_summed = inv_ref[own, :1] * (scaled - mean - normed * inverse * along)
        total_ref[own, :] = d_summed
        low_ref[own, :] = d_summed.astype(BF16)
    for row in (0, blocks + 1, 1, blocks, *range(2, blocks)):
        near = slice(max(row - 2, 0) * HALO, min(row + 1, blocks) * HALO)
        back = dot(turned_ref[row * HALO : (row + 1) * HALO, near], low_ref[near, :]) * (1.0 / NEIGH)
        if row in (0, blocks + 1):
            rim = 0 if row == 0 else 1
            rim_ref[rim] = back.astype(BF16)
            saves[rim].start()
            continue
        own = slice((row - 1) * HALO, row * HALO)
        value = total_ref[own, :] + back
        grad_ref[own, :] = value.astype(BF16)
        if row in (1, blocks):
            edge_ref[0 if row == 1 else 1] = value
        if row == blocks:
            saves[2].start()
    saves[3].start()
    for save in saves:
        save.wait()


def pair_kernel(fields, keep_ref, got_ref, out_ref):
    last = keep_ref.shape[1] - 1
    for k in range(keep_ref.shape[0]):
        total = keep_ref[k, :last].astype(F32) + got_ref[k, :last].astype(F32)
        out_ref[k, :last] = total.astype(BF16)
        tile = keep_ref[k, last].astype(F32) + got_ref[k, last].astype(F32)
        out_ref[k, last] = split_loss(tile, read_loss(tile, fields), fields).astype(BF16)


def plane_kernel(fields, parts_ref, out_ref):
    me = lax.axis_index("xh") * lax.axis_size("y") + lax.axis_index("y")
    blocks = parts_ref.shape[1] - 1
    for j in range(blocks + 1):
        total = parts_ref[0, j].astype(F32)
        for k in range(1, parts_ref.shape[0]):
            total = total + parts_ref[k, j].astype(F32)
        if j < blocks:
            out_ref[j, 0] = total.astype(BF16)
    loss = read_loss(total, fields)
    for j in range(blocks):
        tile = jnp.where(me == j, total, 0.0)
        out_ref[j, 1] = split_loss(tile, loss, fields).astype(BF16)


def fold_kernel(fields, parts_ref, out_ref):
    total = parts_ref[0].astype(F32)
    for k in range(1, parts_ref.shape[0]):
        total = total + parts_ref[k].astype(F32)
    first = total[0].astype(BF16)
    second = split_loss(total[1], read_loss(total[1], fields), fields).astype(BF16)
    for m in range(out_ref.shape[0]):
        out_ref[m, 0] = first
        out_ref[m, 1] = second


def last_kernel(fields, patches, parts_ref, first_ref, second_ref, loss_ref):
    for k in range(parts_ref.shape[0]):
        first_ref[:, k * LANES : (k + 1) * LANES] = parts_ref[k, 0].astype(F32)
    tile = parts_ref[lax.axis_index("z"), 1].astype(F32)
    second_ref[...] = tile[:, :fields]
    loss_ref[...] = read_loss(tile, fields)[:1, :] * (1.0 / patches)


def edge_kernel(grad_in_ref, edge_ref, before_ref, after_ref, grad_ref):
    del grad_in_ref
    step = pl.program_id(0)

    @pl.when(step == 0)
    def _():
        grad_ref[...] = (edge_ref[0] + before_ref[...].astype(F32)).astype(BF16)

    @pl.when(step == 1)
    def _():
        grad_ref[...] = (edge_ref[0] + after_ref[...].astype(F32)).astype(BF16)


BAND = ("z", "xl", "co")
MEM = ("xh", "y")
PLANE = ("y", "xh", "xl")


def per_device(hidden, gain, w_first, w_second, target, patch_ids, neighbours):
    states = hidden[0]
    cells, width = states.shape
    fields = w_second.shape[1]
    bands, members = lax.axis_size(BAND), lax.axis_size(MEM)
    share = width // bands
    up = [(i, i + 1) for i in range(bands - 1)]
    down = [(j, i) for i, j in up]
    before = lax.ppermute(states[cells - HALO :], BAND, up)
    after = lax.ppermute(states[:HALO], BAND, down)
    gain = gain[None]
    second = w_second.T
    half = cells // 2
    saved = [shape((half, width), BF16)] * 3 + [shape((half, LANES), F32)]
    inside = call(
        inner_kernel,
        [shape((fields, half), BF16)] + saved + [shape(w_first.shape, BF16)],
        [neighbours, states, gain, second, w_first],
        10**9,
        16,
        [pltpu.SemaphoreType.DMA],
        anywhere=(4,),
        held=(5,),
    )
    partial, outside, turned = call(
        prepare_kernel,
        [
            shape((half, width), F32),
            shape((2, HALO, HALO), BF16),
            shape((cells + 2 * HALO, cells), BF16),
        ],
        [neighbours, states],
        10**8,
        12,
    )
    saved = [shape((cells, width), BF16)] * 3 + [shape((cells, LANES), F32)]
    copies, slope, active, normed, inv_root = call(
        outer_kernel,
        [shape((members, fields, cells), BF16)] + saved,
        [before, after, partial, outside, gain, second, *inside],
        10**9,
        20,
        [pltpu.VMEM((half, width), BF16)],
    )
    everyone = lax.all_to_all(copies, MEM, 0, 0)
    message = (2 * members, members + 1, share, LANES)
    keep, send, d_pre = call(
        score_kernel,
        [shape(message, BF16), shape(message, BF16), shape((cells, width), BF16)],
        [everyone, target, patch_ids[None], second, slope, active, normed],
        2 * 10**9,
        20,
        [pltpu.VMEM((2,) + message, BF16)],
    )
    got = lax.ppermute(send, "co", [(0, 1), (1, 0)])
    grad, edge, rim_up, rim_down = call(
        backward_kernel,
        [
            shape((cells, width), BF16),
            shape((2, HALO, width), F32),
            shape((HALO, width), BF16),
            shape((HALO, width), BF16),
        ],
        [inside[-1], d_pre, normed, inv_root, turned, gain],
        2 * 10**9,
        20,
        [
            pltpu.VMEM((cells, width), F32),
            pltpu.VMEM((cells, width), BF16),
            pltpu.VMEM((cells, width), BF16),
            pltpu.VMEM((2, HALO, width), F32),
            pltpu.VMEM((2, HALO, width), BF16),
            pltpu.SemaphoreType.DMA((4,)),
        ],
        stored=(0, 1, 2, 3),
    )
    got, grad = lax.optimization_barrier((got, grad))
    (mine,) = call(
        functools.partial(pair_kernel, fields), [shape(message, BF16)], [keep, got], 10**6, 8
    )
    parts = lax.all_to_all(mine, PLANE, 0, 0)
    parts, rim_up, rim_down, grad = lax.optimization_barrier((parts, rim_up, rim_down, grad))
    rim_after = lax.ppermute(rim_up, BAND, down)
    rim_before = lax.ppermute(rim_down, BAND, up)
    last = cells // HALO - 1
    grad_hidden = pl.pallas_call(
        edge_kernel,
        grid=(2,),
        out_shape=shape((cells, width), BF16),
        in_specs=[
            pl.BlockSpec(memory_space=pl.ANY),
            pl.BlockSpec((1, HALO, width), lambda i: (i, 0, 0)),
            pl.BlockSpec((HALO, width), lambda i: (0, 0)),
            pl.BlockSpec((HALO, width), lambda i: (0, 0)),
        ],
        out_specs=pl.BlockSpec((HALO, width), lambda i: (i * last, 0)),
        input_output_aliases={0: 0},
        compiler_params=pltpu.CompilerParams(vmem_limit_bytes=8 * 2**20),
    )(grad, edge, rim_before, rim_after)
    message = (members, 2, share, LANES)
    (planed,) = call(
        functools.partial(plane_kernel, fields), [shape(message, BF16)], [parts], 10**6, 8
    )
    parts = lax.all_to_all(planed, "z", 0, 0)
    (folded,) = call(
        functools.partial(fold_kernel, fields), [shape(message, BF16)], [parts], 10**6, 8
    )
    parts = lax.all_to_all(folded, MEM, 0, 0)
    grad_first, grad_second, loss = call(
        functools.partial(last_kernel, fields, cells // PATCH * bands),
        [shape((share, width), F32), shape((share, fields), F32), shape((1, 1), F32)],
        [parts],
        10**6,
        8,
    )
    return (loss[0, 0], grad_hidden[None], grad_first, grad_second)


def solution(mesh):
    split = jax.sharding.Mesh(mesh.devices.reshape(8, 2, 2, 2, 4), BAND + MEM)
    return jax.shard_map(
        per_device,
        mesh=split,
        in_specs=(
            P(MEM, BAND, None),
            P(),
            P(),
            P(),
            P(None, BAND),
            P(BAND),
            P(None, BAND),
        ),
        out_specs=(P(), P(MEM, BAND, None), P(BAND, None), P(BAND, None)),
        check_vma=False,
    )
```

time: 118 us -> 98.5 us (0.83)
  the two profiles are of different devices: /device:TPU:7 before, /device:TPU:2 now
where the time goes in v1:
time: 98.5 us; the launch traced here: 97.9 us
  blocking collectives  42.8 us (43%)
  starting transfers between devices  21.8 us (22%)
  Pallas kernels  16.9 us (17%)
  waiting for transfers between devices  12.9 us (13%)
  local copies, waits for them, and re-layouts  2.59 us (3%)
    all_to_all x1, blocking collectives, per_device(): parts = lax.all_to_all(mine, PLANE, 0, 0)  21.6 us
    all_to_all x1, blocking collectives, per_device(): everyone = lax.all_to_all(copies, MEM, 0, 0)  21.2 us
    pallas_call x9, Pallas kernels, call(): pl.pallas_call(kernel, out_shape=[pltpu.HBM(o.shape, o.dtype) if i in sto...  16.1 us
    all_to_all x1, starting transfers between devices, per_device(): parts = lax.all_to_all(planed, 'z', 0, 0)  8.47 us
    all_to_all x1, waiting for transfers between devices, per_device(): parts = lax.all_to_all(folded, MEM, 0, 0)  7.12 us
    ppermute x1, starting transfers between devices, per_device(): rim_after = lax.ppermute(rim_up, BAND, down)  3.64 us
    all_to_all x1, waiting for transfers between devices, per_device(): parts = lax.all_to_all(planed, 'z', 0, 0)  3.59 us
    all_to_all x1, starting transfers between devices, per_device(): parts = lax.all_to_all(folded, MEM, 0, 0)  3.37 us
  transfers between devices with their start and end apart: 7, of which 3 were waited for; matrix products, arithmetic and copies ran while one was open for 0% of the time, Pallas kernels for 11%

profile of v1, /device:TPU:2, one launch (start us, length us, event | category | flops | bytes accessed | tf_op | source)
XLA Modules:
  0.0 97.9 jit_solution(6398881440414737452)
XLA Ops:
  0.6 0.0 copy-start
  0.6 0.0 copy-start.2
  0.7 1.2 %slice_bitcast_fusion = (bf16[128,1024]{1,0:T(8,128)(2,1)S(1)}, bf16[128,1024]{1,0:T(8,128)(2,1)S(1)}) fusion(bf16[1,512,1024]{2,1,0:T(8,128)(2,1)} %param.7), kind=kLoop, calls=%fused_computation | loop fusion | bytes 1048576 | tf_op jit(solution)/shard_map/slice | solution.py:346
  1.8 1.9 %collective-permute-start.1 = (bf16[128,1024]{1,0:T(8,128)(2,1)S(1)}, bf16[128,1024]{1,0:T(8,128)(2,1)S(1)}, u32[]{:S(2)}, u32[]{:S(2)}) collective-permute-start(bf16[128,1024]{1,0:T(8,128)(2,1)S(1)} %get-tuple-element.64), channel_id=1, source_target_pairs={{8,0},{16,8},{24,16},{32,24},{40,32},{48,40},{56,48},{64,56},{72,6... | collective-permute-start | bytes 786440 | tf_op jit(solution)/shard_map/ppermute | solution.py:346
  3.7 2.4 %collective-permute-start = (bf16[128,1024]{1,0:T(8,128)(2,1)S(1)}, bf16[128,1024]{1,0:T(8,128)(2,1)S(1)}, u32[]{:S(2)}, u32[]{:S(2)}) collective-permute-start(bf16[128,1024]{1,0:T(8,128)(2,1)S(1)} %get-tuple-element.65), channel_id=1, source_target_pairs={{0,8},{8,16},{16,24},{24,32},{32,40},{40,48},{48,56},{56,64},{64,7... | collective-permute-start | bytes 786440 | tf_op jit(solution)/shard_map/ppermute | solution.py:345
  6.2 0.0 copy-done
  6.2 0.0 copy-start.3
  6.2 0.7 copy-done.3
  6.9 0.7 shard_map.102
  7.6 0.0 copy-done.2
  7.6 0.0 copy-start.4
  7.6 0.7 copy-done.4
  8.3 2.7 %shard_map.103 = (bf16[100,256]{1,0:T(8,128)(2,1)S(1)}, bf16[256,1024]{1,0:T(8,128)(2,1)S(1)}, bf16[256,1024]{1,0:T(8,128)(2,1)S(1)}, bf16[256,1024]{1,0:T(8,128...) custom-call(s32[6,512]{1,0:T(8,128)S(1)} %copy-done.3, bf16[512,1024]{1,0:T(8,128)(2,1)S(1)} %bitcast.11, ...), custom_call_target="tpu_custom_call" | custom-call | flops 1000000000 | bytes 7219200 | tf_op jit(solution)/shard_map/pallas_call | solution.py:33
  11.1 0.0 collective-permute-done.1.after_ref
  11.1 2.1 %collective-permute-done.before_ref = bf16[128,1024]{1,0:T(8,128)(2,1)S(1)} collective-permute-done((bf16[128,1024]{1,0:T(8,128)(2,1)S(1)}, bf16[128,1024]{1,0:T(8,128)(2,1)S(1)}, u32[]{:S(2)}, u32[]{:S(2)}) %collective-permute-start) | collective-permute-done | bytes 262176 | tf_op jit(solution)/shard_map/ppermute | solution.py:345
  13.2 1.7 %shard_map.104 = (bf16[8,100,512]{2,1,0:T(8,128)(2,1)S(1)}, bf16[512,1024]{1,0:T(8,128)(2,1)S(1)}, bf16[512,1024]{1,0:T(8,128)(2,1)S(1)}, bf16[512,1024]{1,0:T(8,128)(2,1)S(1)}, f32[512,128]{1,0:T(8,128)S(1)}) custom-call(bf16[128,1024]{1,0:T(8,128)(2,1)S(1)} %collective-permute-done.before_ref, bf16[128,1024]{1,0:T(8,128)(2,1)S(1)} %collective-permute-done.1.after_ref, ...), custom_call_target="tpu_custom_call" | custom-call | flops 1000000000 | bytes 9926656 | tf_op jit(solution)/shard_map/pallas_call | solution.py:33
  15.0 0.0 copy-start.6
  15.0 0.0 copy-start.7
  15.0 21.2 %all_to_all.20.everyone_ref = bf16[8,100,512]{2,1,0:T(8,128)(2,1)S(1)} all-to-all(bf16[8,100,512]{2,1,0:T(8,128)(2,1)S(1)} %get-tuple-element.42), channel_id=1, replica_groups=mesh['z'=8,'xl'=2,'co'=2,'xh'=2,'y'=4] {'xh','y'}, dimensions={0} | all-to-all | bytes 1638400 | tf_op jit(solution)/shard_map/all_to_all | solution.py:381
  36.2 0.0 copy-done.6
  36.2 0.0 copy-done.7
  36.2 0.0 copy-start.5
  36.2 2.8 %shard_map.105 = (bf16[16,9,32,128]{3,2,1,0:T(8,128)(2,1)S(1)}, bf16[16,9,32,128]{3,2,1,0:T(8,128)(2,1)S(1)}, bf16[512,1024]{1,0:T(8,128)(2,1)S(1)}) custom-call(bf16[8,100,512]{2,1,0:T(8,128)(2,1)S(1)} %all_to_all.20.everyone_ref, f32[100,512]{1,0:T(8,128)S(1)} %copy-done.6, s32[1,512]{1,0:T(1,128)S(1)} %bitcast.18, bf16[100,1024]{1,0:T(8,128)(2,1)S(1)} %bitcast.14, ...), custom_call_target="tpu_custom_call" | custom-call | flops 2000000000 | bytes 7784448 | tf_op jit(solution)/shard_map/pallas_call | solution.py:33
  39.1 0.1 collective-permute-start.2
  39.2 0.0 copy-done.5
  39.2 5.4 %shard_map.106 = (bf16[512,1024]{1,0:T(8,128)(2,1)}, f32[2,128,1024]{2,1,0:T(8,128)}, bf16[128,1024]{1,0:T(8,128)(2,1)}, bf16[128,1024]{1,0:T(8,128)(2,1)}) custom-call(bf16[1024,1024]{1,0:T(8,128)(2,1)S(1)} %get-tuple-element.41.first_ref, bf16[512,1024]{1,0:T(8,128)(2,1)S(1)} %get-tuple-element.48.dpre_ref, ...), custom_call_target="tpu_custom_call" | custom-call | flops 2000000000 | bytes 7868416 | tf_op jit(solution)/shard_map/pallas_call | solution.py:33
  44.6 0.0 collective-permute-done.2.got_ref
  44.6 0.4 shard_map.107
  45.0 21.6 %all_to_all.21.parts_ref = bf16[16,9,32,128]{3,2,1,0:T(8,128)(2,1)S(1)} all-to-all(bf16[16,9,32,128]{3,2,1,0:T(8,128)(2,1)S(1)} %shard_map.107), channel_id=1, replica_groups=mesh['z'=8,'xl'=2,'co'=2,'xh'=2,'y'=4] {'y','xh','xl'}, dimensions={0} | all-to-all | bytes 2359296 | tf_op jit(solution)/shard_map/all_to_all | solution.py:417
  66.6 0.0 copy-start.9
  66.6 0.0 copy-start.8
  66.6 0.0 copy-start.1
  66.6 0.8 shard_map.108
  67.4 8.5 %all-to-all-start.2 = ((bf16[8,2,32,128]{3,2,1,0:T(8,128)(2,1)}), bf16[8,2,32,128]{3,2,1,0:T(8,128)(2,1)S(1)}, u32[]{:S(2)}, u32[]{:S(2)}) async-start(bf16[8,2,32,128]{3,2,1,0:T(8,128)(2,1)} %shard_map.108), calls=%async_computation.2 | async-start | bytes 262144 | tf_op jit(solution)/shard_map/all_to_all | solution.py:440
  75.9 0.0 copy-done.9
  75.9 1.9 %collective-permute-start.3 = (bf16[128,1024]{1,0:T(8,128)(2,1)S(1)}, bf16[128,1024]{1,0:T(8,128)(2,1)S(1)}, u32[]{:S(2)}, u32[]{:S(2)}) collective-permute-start(bf16[128,1024]{1,0:T(8,128)(2,1)S(1)} %copy-done.9), channel_id=1, source_target_pairs={{0,8},{8,16},{16,24},{24,32},{32,40},{40,48},{48,56},{56,64},{64,7... | collective-permute-start | bytes 786440 | tf_op jit(solution)/shard_map/ppermute | solution.py:420
  77.8 0.0 copy-done.8
  77.8 3.6 %collective-permute-start.4 = (bf16[128,1024]{1,0:T(8,128)(2,1)S(1)}, bf16[128,1024]{1,0:T(8,128)(2,1)S(1)}, u32[]{:S(2)}, u32[]{:S(2)}) collective-permute-start(bf16[128,1024]{1,0:T(8,128)(2,1)S(1)} %copy-done.8), channel_id=1, source_target_pairs={{8,0},{16,8},{24,16},{32,24},{40,32},{48,40},{56,48},{64,56},{72,6... | collective-permute-start | bytes 786440 | tf_op jit(solution)/shard_map/ppermute | solution.py:419
  81.5 3.6 %all-to-all-done.2.parts_ref = bf16[8,2,32,128]{3,2,1,0:T(8,128)(2,1)S(1)} async-done(((bf16[8,2,32,128]{3,2,1,0:T(8,128)(2,1)}), bf16[8,2,32,128]{3,2,1,0:T(8,128)(2,1)S(1)}, u32[]{:S(2)}, u32[]{:S(2)}) %all-to-all-start.2) | async-done | bytes 131104 | tf_op jit(solution)/shard_map/all_to_all | solution.py:440
  85.1 0.8 shard_map.109
  85.8 3.4 %all-to-all-start.3 = ((bf16[8,2,32,128]{3,2,1,0:T(8,128)(2,1)}), bf16[8,2,32,128]{3,2,1,0:T(8,128)(2,1)S(1)}, u32[]{:S(2)}, u32[]{:S(2)}) async-start(bf16[8,2,32,128]{3,2,1,0:T(8,128)(2,1)} %shard_map.109), calls=%async_computation.3 | async-start | bytes 262144 | tf_op jit(solution)/shard_map/all_to_all | solution.py:444
  89.2 0.0 collective-permute-done.3.before_ref
  89.2 0.0 collective-permute-done.4.after_ref
  89.2 0.0 copy-done.1
  89.2 0.9 shard_map.111
  90.1 7.1 %all-to-all-done.3.parts_ref = bf16[8,2,32,128]{3,2,1,0:T(8,128)(2,1)S(1)} async-done(((bf16[8,2,32,128]{3,2,1,0:T(8,128)(2,1)}), bf16[8,2,32,128]{3,2,1,0:T(8,128)(2,1)S(1)}, u32[]{:S(2)}, u32[]{:S(2)}) %all-to-all-start.3) | async-done | bytes 131104 | tf_op jit(solution)/shard_map/all_to_all | solution.py:444
  97.2 0.7 shard_map.110
Async XLA Ops:
  0.6 5.5 %copy-start = (bf16[1,512,1024]{2,1,0:T(8,128)(2,1)S(1)}, bf16[1,512,1024]{2,1,0:T(8,128)(2,1)}, u32[]{:S(2)}) copy-start(bf16[1,512,1024]{2,1,0:T(8,128)(2,1)} %param.7) | copy-start | bytes 3145732
  0.6 7.0 %copy-start.2 = (bf16[1024,100]{0,1:T(8,128)(2,1)S(1)}, bf16[1024,100]{0,1:T(8,128)(2,1)}, u32[]{:S(2)}) copy-start(bf16[1024,100]{0,1:T(8,128)(2,1)} %param.10) | copy-start | bytes 614404
  1.8 9.3 %collective-permute-start.1 = (bf16[128,1024]{1,0:T(8,128)(2,1)S(1)}, bf16[128,1024]{1,0:T(8,128)(2,1)S(1)}, u32[]{:S(2)}, u32[]{:S(2)}) collective-permute-start(bf16[128,1024]{1,0:T(8,128)(2,1)S(1)} %get-tuple-element.64), channel_id=1, source_target_pairs={{8,0},{16,8},{24,16},{32,24},{40,32},{48,40},{56,48},{64,56},{72,6... | collective-permute-start | bytes 786440 | tf_op jit(solution)/shard_map/ppermute | solution.py:346
  3.7 9.5 %collective-permute-start = (bf16[128,1024]{1,0:T(8,128)(2,1)S(1)}, bf16[128,1024]{1,0:T(8,128)(2,1)S(1)}, u32[]{:S(2)}, u32[]{:S(2)}) collective-permute-start(bf16[128,1024]{1,0:T(8,128)(2,1)S(1)} %get-tuple-element.65), channel_id=1, source_target_pairs={{0,8},{8,16},{16,24},{24,32},{32,40},{40,48},{48,56},{56,64},{64,7... | collective-permute-start | bytes 786440 | tf_op jit(solution)/shard_map/ppermute | solution.py:345
  6.2 0.7 copy-start.3
  7.6 0.7 copy-start.4
  15.0 21.2 %copy-start.6 = (f32[100,512]{1,0:T(8,128)S(1)}, f32[100,512]{1,0:T(8,128)}, u32[]{:S(2)}) copy-start(f32[100,512]{1,0:T(8,128)} %target_ref.1) | copy-start | bytes 614404
  15.0 21.2 %copy-start.7 = (s32[512]{0:T(512)S(1)}, s32[512]{0:T(512)}, u32[]{:S(2)}) copy-start(s32[512]{0:T(512)} %param.12) | copy-start | bytes 6148
  36.2 2.9 %copy-start.5 = (f32[1024]{0:T(1024)S(1)}, f32[1024]{0:T(1024)}, u32[]{:S(2)}) copy-start(f32[1024]{0:T(1024)} %param.8) | copy-start | bytes 12292
  39.1 5.5 %collective-permute-start.2 = (bf16[16,9,32,128]{3,2,1,0:T(8,128)(2,1)S(1)}, bf16[16,9,32,128]{3,2,1,0:T(8,128)(2,1)S(1)}, u32[]{:S(2)}, u32[]{:S(2)}) collective-permute-start(bf16[16,9,32,128]{3,2,1,0:T(8,128)(2,1)S(1)} %get-tuple-element.47), channel_id=1, source_target_pairs={{0,8},{8,0},{1,9},{9,1},{2,10},{10,2},{3,11},{11,3},{4,12},{12,4},... | collective-permute-start | bytes 3538952 | tf_op jit(solution)/shard_map/ppermute | solution.py:391
  66.6 9.3 %copy-start.9 = (bf16[128,1024]{1,0:T(8,128)(2,1)S(1)}, bf16[128,1024]{1,0:T(8,128)(2,1)}, u32[]{:S(2)}) copy-start(bf16[128,1024]{1,0:T(8,128)(2,1)} %get-tuple-element.60) | copy-start | bytes 786436
  66.6 11.2 %copy-start.8 = (bf16[128,1024]{1,0:T(8,128)(2,1)S(1)}, bf16[128,1024]{1,0:T(8,128)(2,1)}, u32[]{:S(2)}) copy-start(bf16[128,1024]{1,0:T(8,128)(2,1)} %get-tuple-element.61) | copy-start | bytes 786436
  66.6 22.6 %copy-start.1 = (f32[2,128,1024]{2,1,0:T(8,128)S(1)}, f32[2,128,1024]{2,1,0:T(8,128)}, u32[]{:S(2)}) copy-start(f32[2,128,1024]{2,1,0:T(8,128)} %get-tuple-element.59.edge_ref) | copy-start | bytes 3145732
  67.4 17.7 %all-to-all-start.2 = ((bf16[8,2,32,128]{3,2,1,0:T(8,128)(2,1)}), bf16[8,2,32,128]{3,2,1,0:T(8,128)(2,1)S(1)}, u32[]{:S(2)}, u32[]{:S(2)}) async-start(bf16[8,2,32,128]{3,2,1,0:T(8,128)(2,1)} %shard_map.108), calls=%async_computation.2 | async-start | bytes 262144 | tf_op jit(solution)/shard_map/all_to_all | solution.py:440
  75.9 13.3 %collective-permute-start.3 = (bf16[128,1024]{1,0:T(8,128)(2,1)S(1)}, bf16[128,1024]{1,0:T(8,128)(2,1)S(1)}, u32[]{:S(2)}, u32[]{:S(2)}) collective-permute-start(bf16[128,1024]{1,0:T(8,128)(2,1)S(1)} %copy-done.9), channel_id=1, source_target_pairs={{0,8},{8,16},{16,24},{24,32},{32,40},{40,48},{48,56},{56,64},{64,7... | collective-permute-start | bytes 786440 | tf_op jit(solution)/shard_map/ppermute | solution.py:420
  77.8 11.4 %collective-permute-start.4 = (bf16[128,1024]{1,0:T(8,128)(2,1)S(1)}, bf16[128,1024]{1,0:T(8,128)(2,1)S(1)}, u32[]{:S(2)}, u32[]{:S(2)}) collective-permute-start(bf16[128,1024]{1,0:T(8,128)(2,1)S(1)} %copy-done.8), channel_id=1, source_target_pairs={{8,0},{16,8},{24,16},{32,24},{40,32},{48,40},{56,48},{64,56},{72,6... | collective-permute-start | bytes 786440 | tf_op jit(solution)/shard_map/ppermute | solution.py:419
  85.8 11.4 %all-to-all-start.3 = ((bf16[8,2,32,128]{3,2,1,0:T(8,128)(2,1)}), bf16[8,2,32,128]{3,2,1,0:T(8,128)(2,1)S(1)}, u32[]{:S(2)}, u32[]{:S(2)}) async-start(bf16[8,2,32,128]{3,2,1,0:T(8,128)(2,1)} %shard_map.109), calls=%async_computation.3 | async-start | bytes 262144 | tf_op jit(solution)/shard_map/all_to_all | solution.py:444

commit v2 on v1

--- a/solution.py
+++ b/solution.py
@@ -48,6 +48,20 @@
     return jax.ShapeDtypeStruct(dims, kind)
 
 
+def rims_kernel(states_hbm, same_ref, other_ref, done):
+    rows = states_hbm.shape[0]
+    core = lax.axis_index("co")
+    low, high = core * (rows - HALO), (1 - core) * (rows - HALO)
+    moves = [
+        pltpu.make_async_copy(states_hbm.at[pl.ds(low, HALO)], other_ref, done.at[0]),
+        pltpu.make_async_copy(states_hbm.at[pl.ds(high, HALO)], same_ref, done.at[1]),
+    ]
+    for move in moves:
+        move.start()
+    for move in moves:
+        move.wait()
+
+
 def count_rows(near, block):
     near = near[:, block * HALO : (block + 1) * HALO]
     place = lax.broadcasted_iota(jnp.int32, (3 * HALO, HALO), 0) + block * HALO
@@ -72,21 +86,50 @@
 
 
 def inner_kernel(
-    near_ref, states_ref, gain_ref, second_ref, first_hbm,
-    predicted_ref, slope_ref, active_ref, normed_ref, inv_ref, first_ref,
-    done,
+    near_hbm, states_hbm, gain_hbm, first_hbm, second_hbm,
+    predicted_ref, slope_ref, active_ref, normed_ref, inv_ref, gain_ref, first_ref, second_ref,
+    partial_ref, outside_ref, turned_ref,
+    near_ref, states_ref, done,
 ):
-    load = pltpu.make_async_copy(first_hbm, first_ref, done)
-    load.start()
+    loads = [
+        pltpu.make_async_copy(source, place, done.at[i])
+        for i, (source, place) in enumerate(
+            [
+                (near_hbm, near_ref),
+                (states_hbm, states_ref),
+                (gain_hbm, gain_ref),
+                (first_hbm, first_ref),
+                (second_hbm, second_ref),
+            ]
+        )
+    ]
+    for load in loads:
+        load.start()
+    loads[0].wait()
     near = near_ref[...]
-    for block in (1, 2):
+    blocks = states_ref.shape[0] // HALO
+    counts = []
+    for block in range(blocks):
+        total = count_rows(near, block)
+        turned_ref[block * HALO : (block + 3) * HALO, block * HALO : (block + 1) * HALO] = total.astype(BF16)
+        counts.append(total.T.astype(BF16))
+    outside_ref[0] = counts[0][:, :HALO]
+    outside_ref[1] = counts[-1][:, 2 * HALO :]
+    loads[1].wait()
+    loads[2].wait()
+    for block in range(1, blocks - 1):
         reach = states_ref[(block - 1) * HALO : (block + 2) * HALO, :]
-        counts = count_rows(near, block).T.astype(BF16)
         own = states_ref[block * HALO : (block + 1) * HALO, :].astype(F32)
-        summed = own + dot(counts, reach) * (1.0 / NEIGH)
+        summed = own + dot(counts[block], reach) * (1.0 / NEIGH)
         to = slice((block - 1) * HALO, block * HALO)
         normed_ref[to, :], inv_ref[to, :] = normalise(summed, gain_ref[...])
-    load.wait()
+    for edge, block, reach in ((0, 0, counts[0][:, HALO:]), (1, blocks - 1, counts[-1][:, : 2 * HALO])):
+        start = 0 if edge == 0 else (blocks - 2) * HALO
+        own = states_ref[block * HALO : (block + 1) * HALO, :].astype(F32)
+        inside = dot(reach, states_ref[start : start + 2 * HALO, :])
+        partial_ref[edge * HALO : (edge + 1) * HALO, :] = own + inside * (1.0 / NEIGH)
+    loads[3].wait()
+    loads[4].wait()
     cols = 256
     for n in range(0, normed_ref.shape[1], cols):
         part = slice(n, n + cols)
@@ -94,38 +137,19 @@
     predicted_ref[...] = dot(second_ref[...], active_ref[...], 1, 1).astype(BF16)
 
 
-def prepare_kernel(near_ref, states_ref, partial_ref, outside_ref, turned_ref):
-    near = near_ref[...]
-    blocks = states_ref.shape[0] // HALO
-    for block in range(blocks):
-        cells = slice(block * HALO, (block + 1) * HALO)
-        total = count_rows(near, block)
-        turned_ref[block * HALO : (block + 3) * HALO, cells] = total.astype(BF16)
-        if block in (0, blocks - 1):
-            edge = 0 if block == 0 else 1
-            to = slice(edge * HALO, (edge + 1) * HALO)
-            counts = total.T.astype(BF16)
-            inside = slice(HALO, 3 * HALO) if edge == 0 else slice(0, 2 * HALO)
-            outside = slice(0, HALO) if edge == 0 else slice(2 * HALO, 3 * HALO)
-            start = 0 if edge == 0 else (blocks - 2) * HALO
-            reach = states_ref[start : start + 2 * HALO, :]
-            partial_ref[to, :] = states_ref[cells, :].astype(F32) + dot(counts[:, inside], reach) * (
-                1.0 / NEIGH
-            )
-            outside_ref[edge] = counts[:, outside]
-
-
 def outer_kernel(
-    before_ref, after_ref, partial_ref, outside_ref, gain_ref, second_ref,
+    same_ref, other_ref, partial_ref, outside_ref, gain_ref, second_ref,
     predicted_in_ref, slope_in_ref, active_in_ref, normed_in_ref, inv_in_ref, first_ref,
     copies_ref, slope_ref, active_ref, normed_ref, inv_ref,
     own_ref,
 ):
     cells, width = normed_ref.shape
     top, inner, bottom = slice(0, HALO), slice(HALO, cells - HALO), slice(cells - HALO, cells)
-    for edge, (rows_ref, place) in enumerate(((before_ref, top), (after_ref, bottom))):
+    core = lax.axis_index("co")
+    for edge, place in enumerate((top, bottom)):
         to = slice(edge * HALO, (edge + 1) * HALO)
-        summed = partial_ref[to, :] + dot(outside_ref[edge], rows_ref[...]) * (1.0 / NEIGH)
+        rows = jnp.where(core == edge, other_ref[...], same_ref[...])
+        summed = partial_ref[to, :] + dot(outside_ref[edge], rows) * (1.0 / NEIGH)
         normed, inv_ref[place, :] = normalise(summed, gain_ref[...])
         normed_ref[place, :] = normed
         own_ref[to, :] = normed
@@ -225,47 +249,56 @@
 
 def backward_kernel(
     first_ref, dpre_ref, normed_ref, inv_ref, turned_ref, gain_ref,
-    grad_hbm, edge_hbm, up_hbm, down_hbm,
+    grad_hbm, edge_hbm, same_hbm, other_hbm,
     total_ref, low_ref, grad_ref, edge_ref, rim_ref, done,
 ):
     cells, width = low_ref.shape
     blocks = cells // HALO
     gain = gain_ref[...]
     inverse = 1.0 / gain
+    core = lax.axis_index("co")
     saves = [
         pltpu.make_async_copy(source, place, done.at[i])
         for i, (source, place) in enumerate(
             [
-                (rim_ref.at[0], up_hbm),
-                (rim_ref.at[1], down_hbm),
+                (rim_ref.at[0], same_hbm),
+                (rim_ref.at[1], other_hbm),
                 (edge_ref, edge_hbm),
-                (grad_ref, grad_hbm),
+                (grad_ref, grad_hbm.at[HALO : cells - HALO]),
             ]
         )
     ]
+    cols = 256
+    mean = jnp.zeros((cells, 1), F32)
+    along = jnp.zeros((cells, 1), F32)
+    for n in range(0, width, cols):
+        part = slice(n, n + cols)
+        d_normed = dot(dpre_ref[...], first_ref[part, :], 1, 1)
+        total_ref[:, part] = d_normed
+        mean = mean + jnp.sum(d_normed * gain[:, part], -1, keepdims=True)
+        along = along + jnp.sum(d_normed * normed_ref[:, part].astype(F32), -1, keepdims=True)
     for block in range(blocks):
         own = slice(block * HALO, (block + 1) * HALO)
-        d_normed = dot(dpre_ref[own, :], first_ref[...], 1, 1)
-        scaled = d_normed * gain
-        normed = normed_ref[own, :].astype(F32)
-        mean = jnp.mean(scaled, -1, keepdims=True)
-        along = jnp.mean(d_normed * normed, -1, keepdims=True)
-        d_summed = inv_ref[own, :1] * (scaled - mean - normed * inverse * along)
+        inner = mean[own] * (1.0 / width) + normed_ref[own, :].astype(F32) * inverse * (
+            along[own] * (1.0 / width)
+        )
+        d_summed = inv_ref[own, :1] * (total_ref[own, :] * gain - inner)
         total_ref[own, :] = d_summed
         low_ref[own, :] = d_summed.astype(BF16)
     for row in (0, blocks + 1, 1, blocks, *range(2, blocks)):
         near = slice(max(row - 2, 0) * HALO, min(row + 1, blocks) * HALO)
         back = dot(turned_ref[row * HALO : (row + 1) * HALO, near], low_ref[near, :]) * (1.0 / NEIGH)
         if row in (0, blocks + 1):
-            rim = 0 if row == 0 else 1
-            rim_ref[rim] = back.astype(BF16)
-            saves[rim].start()
+            rim_ref[1 - core if row == 0 else core] = back.astype(BF16)
+            if row > 0:
+                saves[0].start()
+                saves[1].start()
             continue
-        own = slice((row - 1) * HALO, row * HALO)
-        value = total_ref[own, :] + back
-        grad_ref[own, :] = value.astype(BF16)
+        value = total_ref[(row - 1) * HALO : row * HALO, :] + back
         if row in (1, blocks):
             edge_ref[0 if row == 1 else 1] = value
+        else:
+            grad_ref[(row - 2) * HALO : (row - 1) * HALO, :] = value.astype(BF16)
         if row == blocks:
             saves[2].start()
     saves[3].start()
@@ -316,17 +349,10 @@
     loss_ref[...] = read_loss(tile, fields)[:1, :] * (1.0 / patches)
 
 
-def edge_kernel(grad_in_ref, edge_ref, before_ref, after_ref, grad_ref):
+def edge_kernel(grad_in_ref, edge_ref, same_ref, other_ref, grad_ref):
     del grad_in_ref
-    step = pl.program_id(0)
-
-    @pl.when(step == 0)
-    def _():
-        grad_ref[...] = (edge_ref[0] + before_ref[...].astype(F32)).astype(BF16)
-
-    @pl.when(step == 1)
-    def _():
-        grad_ref[...] = (edge_ref[0] + after_ref[...].astype(F32)).astype(BF16)
+    rim = jnp.where(pl.program_id(0) == lax.axis_index("co"), other_ref[...], same_ref[...])
+    grad_ref[...] = (edge_ref[0] + rim.astype(F32)).astype(BF16)
 
 
 BAND = ("z", "xl", "co")
@@ -340,40 +366,51 @@
     fields = w_second.shape[1]
     bands, members = lax.axis_size(BAND), lax.axis_size(MEM)
     share = width // bands
-    up = [(i, i + 1) for i in range(bands - 1)]
-    down = [(j, i) for i, j in up]
-    before = lax.ppermute(states[cells - HALO :], BAND, up)
-    after = lax.ppermute(states[:HALO], BAND, down)
-    gain = gain[None]
-    second = w_second.T
+    chips = [(i, i + 1) for i in range(1, bands - 1, 2)]
+    chips = chips + [(j, i) for i, j in chips]
+    cores = [(0, 1), (1, 0)]
+    rim_same, rim_other = call(
+        rims_kernel,
+        [shape((HALO, width), BF16), shape((HALO, width), BF16)],
+        [states],
+        0,
+        4,
+        [pltpu.SemaphoreType.DMA((2,))],
+        anywhere=(0,),
+        held=(0, 1),
+    )
+    other = lax.ppermute(rim_other, BAND, chips)
+    same = lax.ppermute(rim_same, "co", cores)
     half = cells // 2
     saved = [shape((half, width), BF16)] * 3 + [shape((half, LANES), F32)]
-    inside = call(
+    *inside, gain, first, second, partial, outside, turned = call(
         inner_kernel,
-        [shape((fields, half), BF16)] + saved + [shape(w_first.shape, BF16)],
-        [neighbours, states, gain, second, w_first],
-        10**9,
-        16,
-        [pltpu.SemaphoreType.DMA],
-        anywhere=(4,),
-        held=(5,),
-    )
-    partial, outside, turned = call(
-        prepare_kernel,
         [
+            shape((fields, half), BF16),
+            *saved,
+            shape((1, width), F32),
+            shape(w_first.shape, BF16),
+            shape((fields, width), BF16),
             shape((half, width), F32),
             shape((2, HALO, HALO), BF16),
             shape((cells + 2 * HALO, cells), BF16),
         ],
-        [neighbours, states],
-        10**8,
-        12,
+        [neighbours, states, gain[None], w_first, w_second.T],
+        10**9,
+        16,
+        [
+            pltpu.VMEM(neighbours.shape, jnp.int32),
+            pltpu.VMEM(states.shape, BF16),
+            pltpu.SemaphoreType.DMA((5,)),
+        ],
+        anywhere=(0, 1, 2, 3, 4),
+        held=(5, 6, 7),
     )
     saved = [shape((cells, width), BF16)] * 3 + [shape((cells, LANES), F32)]
     copies, slope, active, normed, inv_root = call(
         outer_kernel,
         [shape((members, fields, cells), BF16)] + saved,
-        [before, after, partial, outside, gain, second, *inside],
+        [same, other, partial, outside, gain, second, *inside, first],
         10**9,
         20,
         [pltpu.VMEM((half, width), BF16)],
@@ -388,8 +425,8 @@
         20,
         [pltpu.VMEM((2,) + message, BF16)],
     )
-    got = lax.ppermute(send, "co", [(0, 1), (1, 0)])
-    grad, edge, rim_up, rim_down = call(
+    got = lax.ppermute(send, "co", cores)
+    grad, edge, rim_same, rim_other = call(
         backward_kernel,
         [
             shape((cells, width), BF16),
@@ -397,13 +434,13 @@
             shape((HALO, width), BF16),
             shape((HALO, width), BF16),
         ],
-        [inside[-1], d_pre, normed, inv_root, turned, gain],
+        [first, d_pre, normed, inv_root, turned, gain],
         2 * 10**9,
         20,
         [
             pltpu.VMEM((cells, width), F32),
             pltpu.VMEM((cells, width), BF16),
-            pltpu.VMEM((cells, width), BF16),
+            pltpu.VMEM((cells - 2 * HALO, width), BF16),
             pltpu.VMEM((2, HALO, width), F32),
             pltpu.VMEM((2, HALO, width), BF16),
             pltpu.SemaphoreType.DMA((4,)),
@@ -415,9 +452,9 @@
         functools.partial(pair_kernel, fields), [shape(message, BF16)], [keep, got], 10**6, 8
     )
     parts = lax.all_to_all(mine, PLANE, 0, 0)
-    parts, rim_up, rim_down, grad = lax.optimization_barrier((parts, rim_up, rim_down, grad))
-    rim_after = lax.ppermute(rim_up, BAND, down)
-    rim_before = lax.ppermute(rim_down, BAND, up)
+    parts, rim_same, rim_other = lax.optimization_barrier((parts, rim_same, rim_other))
+    other = lax.ppermute(rim_other, BAND, chips)
+    same = lax.ppermute(rim_same, "co", cores)
     last = cells // HALO - 1
     grad_hidden = pl.pallas_call(
         edge_kernel,
@@ -432,7 +469,7 @@
         out_specs=pl.BlockSpec((HALO, width), lambda i: (i * last, 0)),
         input_output_aliases={0: 0},
         compiler_params=pltpu.CompilerParams(vmem_limit_bytes=8 * 2**20),
-    )(grad, edge, rim_before, rim_after)
+    )(grad, edge, same, other)
     message = (members, 2, share, LANES)
     (planed,) = call(
         functools.partial(plane_kernel, fields), [shape(message, BF16)], [parts], 10**6, 8

time: 98.5 us -> 97.1 us (0.986)
  waiting for transfers between devices: 12.9 us -> 16.2 us
  local copies, waits for them, and re-layouts: 2.59 us -> 0.02 us
  blocking collectives: 42.8 us -> 41 us
    all_to_all x1, starting transfers between devices: 8.47 us -> 10.8 us  [per_device(): parts = lax.all_to_all(planed, 'z', 0, 0)]
    all_to_all x1, waiting for transfers between devices: 3.59 us -> 5.61 us  [per_device(): parts = lax.all_to_all(planed, 'z', 0, 0)]
    ppermute x5, starting transfers between devices: 9.98 us -> 7.99 us  [the longest x2 7.72 us: per_device(): other = lax.ppermute(rim_other, BAND, chips)]
    all_to_all x1, blocking collectives: 21.2 us -> 19.4 us  [per_device(): everyone = lax.all_to_all(copies, MEM, 0, 0)]
    unnamed x20 -> x10, local copies, waits for them, and re-layouts: 1.43 us -> 0.02 us
    ppermute x5, waiting for transfers between devices: 2.16 us -> 3.5 us  [the longest x2 3.49 us: per_device(): other = lax.ppermute(rim_other, BAND, chips)]
    slice x1 -> x0, local copies, waits for them, and re-layouts: 1.16 us -> none  [per_device(): after = lax.ppermute(states[:HALO], BAND, down)]
  transfers between devices with their start and end apart: 7 -> 7, of which waited for: 3 -> 3; matrix products, arithmetic and copies ran while one was open for 0% -> 0% of each run, Pallas kernels for 11% -> 9%
where the time goes in v2:
time: 97.1 us; the launch traced here: 96.6 us
  blocking collectives  41 us (42%)
  starting transfers between devices  22.2 us (23%)
  Pallas kernels  16.4 us (17%)
  waiting for transfers between devices  16.2 us (17%)
    all_to_all x1, blocking collectives, per_device(): parts = lax.all_to_all(mine, PLANE, 0, 0)  21.6 us
    all_to_all x1, blocking collectives, per_device(): everyone = lax.all_to_all(copies, MEM, 0, 0)  19.4 us
    pallas_call x9, Pallas kernels, call(): pl.pallas_call(kernel, out_shape=[pltpu.HBM(o.shape, o.dtype) if i in sto...  15.5 us
    all_to_all x1, starting transfers between devices, per_device(): parts = lax.all_to_all(planed, 'z', 0, 0)  10.8 us
    ppermute x2, starting transfers between devices, per_device(): other = lax.ppermute(rim_other, BAND, chips)  7.72 us
    all_to_all x1, waiting for transfers between devices, per_device(): parts = lax.all_to_all(folded, MEM, 0, 0)  7.11 us
    all_to_all x1, waiting for transfers between devices, per_device(): parts = lax.all_to_all(planed, 'z', 0, 0)  5.61 us
    ppermute x2, waiting for transfers between devices, per_device(): other = lax.ppermute(rim_other, BAND, chips)  3.49 us
  transfers between devices with their start and end apart: 7, of which 3 were waited for; matrix products, arithmetic and copies ran while one was open for 0% of the time, Pallas kernels for 9%

profile of v2, /device:TPU:2, one launch (start us, length us, event | category | flops | bytes accessed | tf_op | source)
XLA Modules:
  0.0 96.6 jit_solution(2011237691245975613)
XLA Ops:
  0.6 1.1 %shard_map.102 = (bf16[128,1024]{1,0:T(8,128)(2,1)S(1)}, bf16[128,1024]{1,0:T(8,128)(2,1)S(1)}) custom-call(bf16[512,1024]{1,0:T(8,128)(2,1)} %bitcast.8), custom_call_target="tpu_custom_call" | custom-call | bytes 1572864 | tf_op jit(solution)/shard_map/pallas_call | solution.py:33
  1.7 0.1 collective-permute-start
  1.8 4.3 %collective-permute-start.1 = (bf16[128,1024]{1,0:T(8,128)(2,1)S(1)}, bf16[128,1024]{1,0:T(8,128)(2,1)S(1)}, u32[]{:S(2)}, u32[]{:S(2)}) collective-permute-start(bf16[128,1024]{1,0:T(8,128)(2,1)S(1)} %get-tuple-element.38), channel_id=1, source_target_pairs={{8,16},{24,32},{40,48},{56,64},{72,80},{88,96},{104,112},{120,128}... | collective-permute-start | bytes 786440 | tf_op jit(solution)/shard_map/ppermute | solution.py:382
  6.1 3.3 %shard_map.103 = (bf16[100,256]{1,0:T(8,128)(2,1)S(1)}, bf16[256,1024]{1,0:T(8,128)(2,1)S(1)}, bf16[256,1024]{1,0:T(8,128)(2,1)S(1)}, bf16[256,1024]{1,0:T(8,128...) custom-call(s32[6,512]{1,0:T(8,128)} %near_hbm.1, ...), custom_call_target="tpu_custom_call" | custom-call | flops 1000000000 | bytes 9328640 | tf_op jit(solution)/shard_map/pallas_call | solution.py:33
  9.4 0.0 collective-permute-done.same_ref
  9.4 3.5 %collective-permute-done.1.other_ref = bf16[128,1024]{1,0:T(8,128)(2,1)S(1)} collective-permute-done((bf16[128,1024]{1,0:T(8,128)(2,1)S(1)}, bf16[128,1024]{1,0:T(8,128)(2,1)S(1)}, u32[]{:S(2)}, u32[]{:S(2)}) %collective-permute-start.1) | collective-permute-done | bytes 262176 | tf_op jit(solution)/shard_map/ppermute | solution.py:382
  12.9 1.7 %shard_map.104 = (bf16[8,100,512]{2,1,0:T(8,128)(2,1)S(1)}, bf16[512,1024]{1,0:T(8,128)(2,1)S(1)}, bf16[512,1024]{1,0:T(8,128)(2,1)S(1)}, bf16[512,1024]{1,0:T(8,128)(2,1)S(1)}, f32[512,128]{1,0:T(8,128)S(1)}) custom-call(bf16[128,1024]{1,0:T(8,128)(2,1)S(1)} %collective-permute-done.same_ref, bf16[128,1024]{1,0:T(8,128)(2,1)S(1)} %collective-permute-done.1.other_ref, ...), custom_call_target="tpu_custom_call" | custom-call | flops 1000000000 | bytes 9926656 | tf_op jit(solution)/shard_map/pallas_call | solution.py:33
  14.7 0.0 copy-start.1
  14.7 0.0 copy-start.2
  14.7 19.4 %all_to_all.20.everyone_ref = bf16[8,100,512]{2,1,0:T(8,128)(2,1)S(1)} all-to-all(bf16[8,100,512]{2,1,0:T(8,128)(2,1)S(1)} %get-tuple-element.49), channel_id=1, replica_groups=mesh['z'=8,'xl'=2,'co'=2,'xh'=2,'y'=4] {'xh','y'}, dimensions={0} | all-to-all | bytes 1638400 | tf_op jit(solution)/shard_map/all_to_all | solution.py:418
  34.1 0.0 copy-done.1
  34.1 0.0 copy-done.2
  34.1 2.8 %shard_map.105 = (bf16[16,9,32,128]{3,2,1,0:T(8,128)(2,1)S(1)}, bf16[16,9,32,128]{3,2,1,0:T(8,128)(2,1)S(1)}, bf16[512,1024]{1,0:T(8,128)(2,1)S(1)}) custom-call(bf16[8,100,512]{2,1,0:T(8,128)(2,1)S(1)} %all_to_all.20.everyone_ref, f32[100,512]{1,0:T(8,128)S(1)} %copy-done.1, s32[1,512]{1,0:T(1,128)S(1)} %bitcast.6, ...), custom_call_target="tpu_custom_call" | custom-call | flops 2000000000 | bytes 7784448 | tf_op jit(solution)/shard_map/pallas_call | solution.py:33
  37.0 0.1 collective-permute-start.2
  37.1 3.9 %shard_map.106 = (bf16[512,1024]{1,0:T(8,128)(2,1)}, f32[2,128,1024]{2,1,0:T(8,128)}, bf16[128,1024]{1,0:T(8,128)(2,1)}, bf16[128,1024]{1,0:T(8,128)(2,1)}) custom-call(bf16[1024,1024]{1,0:T(8,128)(2,1)S(1)} %get-tuple-element.48.first_ref, bf16[512,1024]{1,0:T(8,128)(2,1)S(1)} %get-tuple-element.55.dpre_ref, ...), custom_call_target="tpu_custom_call" | custom-call | flops 2000000000 | bytes 7868416 | tf_op jit(solution)/shard_map/pallas_call | solution.py:33
  41.0 0.0 collective-permute-done.2.got_ref
  41.0 0.4 shard_map.107
  41.4 21.6 %all_to_all.21.parts_ref = bf16[16,9,32,128]{3,2,1,0:T(8,128)(2,1)S(1)} all-to-all(bf16[16,9,32,128]{3,2,1,0:T(8,128)(2,1)S(1)} %shard_map.107), channel_id=1, replica_groups=mesh['z'=8,'xl'=2,'co'=2,'xh'=2,'y'=4] {'y','xh','xl'}, dimensions={0} | all-to-all | bytes 2359296 | tf_op jit(solution)/shard_map/all_to_all | solution.py:454
  62.9 0.0 copy-start.4
  62.9 0.0 copy-start.3
  62.9 0.0 copy-start
  62.9 0.8 shard_map.108
  63.8 10.8 %all-to-all-start.2 = ((bf16[8,2,32,128]{3,2,1,0:T(8,128)(2,1)}), bf16[8,2,32,128]{3,2,1,0:T(8,128)(2,1)S(1)}, u32[]{:S(2)}, u32[]{:S(2)}) async-start(bf16[8,2,32,128]{3,2,1,0:T(8,128)(2,1)} %shard_map.108), calls=%async_computation.2 | async-start | bytes 262144 | tf_op jit(solution)/shard_map/all_to_all | solution.py:477
  74.6 0.0 copy-done.4
  74.6 0.1 collective-permute-start.3
  74.7 0.0 copy-done.3
  74.7 3.5 %collective-permute-start.4 = (bf16[128,1024]{1,0:T(8,128)(2,1)S(1)}, bf16[128,1024]{1,0:T(8,128)(2,1)S(1)}, u32[]{:S(2)}, u32[]{:S(2)}) collective-permute-start(bf16[128,1024]{1,0:T(8,128)(2,1)S(1)} %copy-done.3), channel_id=1, source_target_pairs={{8,16},{24,32},{40,48},{56,64},{72,80},{88,96},{104,112},{120,128}... | collective-permute-start | bytes 786440 | tf_op jit(solution)/shard_map/ppermute | solution.py:456
  78.1 5.6 %all-to-all-done.2.parts_ref = bf16[8,2,32,128]{3,2,1,0:T(8,128)(2,1)S(1)} async-done(((bf16[8,2,32,128]{3,2,1,0:T(8,128)(2,1)}), bf16[8,2,32,128]{3,2,1,0:T(8,128)(2,1)S(1)}, u32[]{:S(2)}, u32[]{:S(2)}) %all-to-all-start.2) | async-done | bytes 131104 | tf_op jit(solution)/shard_map/all_to_all | solution.py:477
  83.7 0.8 shard_map.109
  84.5 3.4 %all-to-all-start.3 = ((bf16[8,2,32,128]{3,2,1,0:T(8,128)(2,1)}), bf16[8,2,32,128]{3,2,1,0:T(8,128)(2,1)S(1)}, u32[]{:S(2)}, u32[]{:S(2)}) async-start(bf16[8,2,32,128]{3,2,1,0:T(8,128)(2,1)} %shard_map.109), calls=%async_computation.3 | async-start | bytes 262144 | tf_op jit(solution)/shard_map/all_to_all | solution.py:481
  87.9 0.0 collective-permute-done.3.same_ref
  87.9 0.0 collective-permute-done.4.other_ref
  87.9 0.0 copy-done
  87.9 0.9 shard_map.111
  88.8 7.1 %all-to-all-done.3.parts_ref = bf16[8,2,32,128]{3,2,1,0:T(8,128)(2,1)S(1)} async-done(((bf16[8,2,32,128]{3,2,1,0:T(8,128)(2,1)}), bf16[8,2,32,128]{3,2,1,0:T(8,128)(2,1)S(1)}, u32[]{:S(2)}, u32[]{:S(2)}) %all-to-all-start.3) | async-done | bytes 131104 | tf_op jit(solution)/shard_map/all_to_all | solution.py:481
  95.9 0.7 shard_map.110
Async XLA Ops:
  1.7 7.7 %collective-permute-start = (bf16[128,1024]{1,0:T(8,128)(2,1)S(1)}, bf16[128,1024]{1,0:T(8,128)(2,1)S(1)}, u32[]{:S(2)}, u32[]{:S(2)}) collective-permute-start(bf16[128,1024]{1,0:T(8,128)(2,1)S(1)} %get-tuple-element.37), channel_id=1, source_target_pairs={{0,8},{8,0},{1,9},{9,1},{2,10},{10,2},{3,11},{11,3},{4,12},{12,4},... | collective-permute-start | bytes 786440 | tf_op jit(solution)/shard_map/ppermute | solution.py:383
  1.8 11.1 %collective-permute-start.1 = (bf16[128,1024]{1,0:T(8,128)(2,1)S(1)}, bf16[128,1024]{1,0:T(8,128)(2,1)S(1)}, u32[]{:S(2)}, u32[]{:S(2)}) collective-permute-start(bf16[128,1024]{1,0:T(8,128)(2,1)S(1)} %get-tuple-element.38), channel_id=1, source_target_pairs={{8,16},{24,32},{40,48},{56,64},{72,80},{88,96},{104,112},{120,128}... | collective-permute-start | bytes 786440 | tf_op jit(solution)/shard_map/ppermute | solution.py:382
  14.7 19.5 %copy-start.1 = (f32[100,512]{1,0:T(8,128)S(1)}, f32[100,512]{1,0:T(8,128)}, u32[]{:S(2)}) copy-start(f32[100,512]{1,0:T(8,128)} %target_ref.1) | copy-start | bytes 614404
  14.7 19.5 %copy-start.2 = (s32[512]{0:T(512)S(1)}, s32[512]{0:T(512)}, u32[]{:S(2)}) copy-start(s32[512]{0:T(512)} %param.12) | copy-start | bytes 6148
  37.0 4.0 %collective-permute-start.2 = (bf16[16,9,32,128]{3,2,1,0:T(8,128)(2,1)S(1)}, bf16[16,9,32,128]{3,2,1,0:T(8,128)(2,1)S(1)}, u32[]{:S(2)}, u32[]{:S(2)}) collective-permute-start(bf16[16,9,32,128]{3,2,1,0:T(8,128)(2,1)S(1)} %get-tuple-element.54), channel_id=1, source_target_pairs={{0,8},{8,0},{1,9},{9,1},{2,10},{10,2},{3,11},{11,3},{4,12},{12,4},... | collective-permute-start | bytes 3538952 | tf_op jit(solution)/shard_map/ppermute | solution.py:428
  62.9 11.6 %copy-start.4 = (bf16[128,1024]{1,0:T(8,128)(2,1)S(1)}, bf16[128,1024]{1,0:T(8,128)(2,1)}, u32[]{:S(2)}) copy-start(bf16[128,1024]{1,0:T(8,128)(2,1)} %get-tuple-element.66) | copy-start | bytes 786436
  62.9 11.7 %copy-start.3 = (bf16[128,1024]{1,0:T(8,128)(2,1)S(1)}, bf16[128,1024]{1,0:T(8,128)(2,1)}, u32[]{:S(2)}) copy-start(bf16[128,1024]{1,0:T(8,128)(2,1)} %get-tuple-element.67) | copy-start | bytes 786436
  62.9 25.0 %copy-start = (f32[2,128,1024]{2,1,0:T(8,128)S(1)}, f32[2,128,1024]{2,1,0:T(8,128)}, u32[]{:S(2)}) copy-start(f32[2,128,1024]{2,1,0:T(8,128)} %get-tuple-element.65.edge_ref) | copy-start | bytes 3145732
  63.8 20.0 %all-to-all-start.2 = ((bf16[8,2,32,128]{3,2,1,0:T(8,128)(2,1)}), bf16[8,2,32,128]{3,2,1,0:T(8,128)(2,1)S(1)}, u32[]{:S(2)}, u32[]{:S(2)}) async-start(bf16[8,2,32,128]{3,2,1,0:T(8,128)(2,1)} %shard_map.108), calls=%async_computation.2 | async-start | bytes 262144 | tf_op jit(solution)/shard_map/all_to_all | solution.py:477
  74.6 13.3 %collective-permute-start.3 = (bf16[128,1024]{1,0:T(8,128)(2,1)S(1)}, bf16[128,1024]{1,0:T(8,128)(2,1)S(1)}, u32[]{:S(2)}, u32[]{:S(2)}) collective-permute-start(bf16[128,1024]{1,0:T(8,128)(2,1)S(1)} %copy-done.4), channel_id=1, source_target_pairs={{0,8},{8,0},{1,9},{9,1},{2,10},{10,2},{3,11},{11,3},{4,12},{12,4},... | collective-permute-start | bytes 786440 | tf_op jit(solution)/shard_map/ppermute | solution.py:457
  74.7 13.2 %collective-permute-start.4 = (bf16[128,1024]{1,0:T(8,128)(2,1)S(1)}, bf16[128,1024]{1,0:T(8,128)(2,1)S(1)}, u32[]{:S(2)}, u32[]{:S(2)}) collective-permute-start(bf16[128,1024]{1,0:T(8,128)(2,1)S(1)} %copy-done.3), channel_id=1, source_target_pairs={{8,16},{24,32},{40,48},{56,64},{72,80},{88,96},{104,112},{120,128}... | collective-permute-start | bytes 786440 | tf_op jit(solution)/shard_map/ppermute | solution.py:456
  84.5 11.4 %all-to-all-start.3 = ((bf16[8,2,32,128]{3,2,1,0:T(8,128)(2,1)}), bf16[8,2,32,128]{3,2,1,0:T(8,128)(2,1)S(1)}, u32[]{:S(2)}, u32[]{:S(2)}) async-start(bf16[8,2,32,128]{3,2,1,0:T(8,128)(2,1)} %shard_map.109), calls=%async_computation.3 | async-start | bytes 262144 | tf_op jit(solution)/shard_map/all_to_all | solution.py:481

commit v3 on v2

--- a/solution.py
+++ b/solution.py
@@ -64,10 +64,11 @@
 
 def count_rows(near, block):
     near = near[:, block * HALO : (block + 1) * HALO]
-    place = lax.broadcasted_iota(jnp.int32, (3 * HALO, HALO), 0) + block * HALO
-    total = jnp.zeros((3 * HALO, HALO), F32)
+    row = lax.broadcasted_iota(jnp.int32, (3 * HALO, HALO), 0)
+    own = lax.broadcasted_iota(jnp.int32, (3 * HALO, HALO), 1) + HALO
+    total = jnp.where(row == own, float(NEIGH), 0.0)
     for k in range(NEIGH):
-        total = total + jnp.where(near[k : k + 1, :] == place, 1.0, 0.0)
+        total = total + jnp.where(near[k : k + 1, :] == row + block * HALO, 1.0, 0.0)
     return total
 
 
@@ -86,9 +87,9 @@
 
 
 def inner_kernel(
-    near_hbm, states_hbm, gain_hbm, first_hbm, second_hbm,
+    same_ref, near_hbm, states_hbm, gain_hbm, first_hbm, second_hbm,
     predicted_ref, slope_ref, active_ref, normed_ref, inv_ref, gain_ref, first_ref, second_ref,
-    partial_ref, outside_ref, turned_ref,
+    partial_ref, outside_ref, turned_ref, first_turned_ref,
     near_ref, states_ref, done,
 ):
     loads = [
@@ -105,29 +106,34 @@
     ]
     for load in loads:
         load.start()
+    core = lax.axis_index("co")
     loads[0].wait()
     near = near_ref[...]
-    blocks = states_ref.shape[0] // HALO
+    cells = states_ref.shape[0]
+    blocks = cells // HALO
     counts = []
     for block in range(blocks):
         total = count_rows(near, block)
         turned_ref[block * HALO : (block + 3) * HALO, block * HALO : (block + 1) * HALO] = total.astype(BF16)
         counts.append(total.T.astype(BF16))
-    outside_ref[0] = counts[0][:, :HALO]
-    outside_ref[1] = counts[-1][:, 2 * HALO :]
+    outside = (counts[0][:, :HALO], counts[-1][:, 2 * HALO :])
+    inside = (counts[0][:, HALO:], counts[-1][:, : 2 * HALO])
     loads[1].wait()
     loads[2].wait()
+    gain = gain_ref[...]
     for block in range(1, blocks - 1):
         reach = states_ref[(block - 1) * HALO : (block + 2) * HALO, :]
-        own = states_ref[block * HALO : (block + 1) * HALO, :].astype(F32)
-        summed = own + dot(counts[block], reach) * (1.0 / NEIGH)
+        summed = dot(counts[block], reach) * (1.0 / NEIGH)
         to = slice((block - 1) * HALO, block * HALO)
-        normed_ref[to, :], inv_ref[to, :] = normalise(summed, gain_ref[...])
-    for edge, block, reach in ((0, 0, counts[0][:, HALO:]), (1, blocks - 1, counts[-1][:, : 2 * HALO])):
-        start = 0 if edge == 0 else (blocks - 2) * HALO
-        own = states_ref[block * HALO : (block + 1) * HALO, :].astype(F32)
-        inside = dot(reach, states_ref[start : start + 2 * HALO, :])
-        partial_ref[edge * HALO : (edge + 1) * HALO, :] = own + inside * (1.0 / NEIGH)
+        normed_ref[to, :], inv_ref[to, :] = normalise(summed, gain)
+    last = cells - 2 * HALO
+    rows = states_ref[pl.ds(pl.multiple_of((1 - core) * last, HALO), 2 * HALO), :]
+    summed = dot(jnp.where(core == 0, inside[1], inside[0]), rows)
+    summed = summed + dot(jnp.where(core == 0, outside[1], outside[0]), same_ref[...])
+    normed_ref[last:, :], inv_ref[last:, :] = normalise(summed * (1.0 / NEIGH), gain)
+    rows = states_ref[pl.ds(pl.multiple_of(core * last, HALO), 2 * HALO), :]
+    partial_ref[...] = dot(jnp.where(core == 0, inside[0], inside[1]), rows)
+    outside_ref[...] = jnp.where(core == 0, outside[0], outside[1])
     loads[3].wait()
     loads[4].wait()
     cols = 256
@@ -135,42 +141,43 @@
         part = slice(n, n + cols)
         active_ref[:, part], slope_ref[:, part] = head(normed_ref, first_ref, part)
     predicted_ref[...] = dot(second_ref[...], active_ref[...], 1, 1).astype(BF16)
+    for n in range(0, first_ref.shape[0], LANES):
+        first_turned_ref[:, n : n + LANES] = first_ref[n : n + LANES, :].T
 
 
 def outer_kernel(
-    same_ref, other_ref, partial_ref, outside_ref, gain_ref, second_ref,
+    other_ref, partial_ref, outside_ref, gain_ref, second_ref,
     predicted_in_ref, slope_in_ref, active_in_ref, normed_in_ref, inv_in_ref, first_ref,
     copies_ref, slope_ref, active_ref, normed_ref, inv_ref,
     own_ref,
 ):
     cells, width = normed_ref.shape
-    top, inner, bottom = slice(0, HALO), slice(HALO, cells - HALO), slice(cells - HALO, cells)
     core = lax.axis_index("co")
-    for edge, place in enumerate((top, bottom)):
-        to = slice(edge * HALO, (edge + 1) * HALO)
-        rows = jnp.where(core == edge, other_ref[...], same_ref[...])
-        summed = partial_ref[to, :] + dot(outside_ref[edge], rows) * (1.0 / NEIGH)
-        normed, inv_ref[place, :] = normalise(summed, gain_ref[...])
-        normed_ref[place, :] = normed
-        own_ref[to, :] = normed
-    normed_ref[inner, :] = normed_in_ref[...]
-    inv_ref[inner, :] = inv_in_ref[...]
-    active_ref[inner, :] = active_in_ref[...]
-    slope_ref[inner, :] = slope_in_ref[...]
+    last = cells - HALO
+    inner, held = slice(HALO, last), slice(0, last - HALO)
+    mine = pl.ds(pl.multiple_of(core * last, HALO), HALO)
+    done = pl.ds(pl.multiple_of((1 - core) * last, HALO), HALO)
+    summed = (partial_ref[...] + dot(outside_ref[...], other_ref[...])) * (1.0 / NEIGH)
+    normed, inv_ref[mine, :] = normalise(summed, gain_ref[...])
+    normed_ref[mine, :] = normed
+    own_ref[...] = normed
+    for full_ref, part_ref in (
+        (normed_ref, normed_in_ref),
+        (inv_ref, inv_in_ref),
+        (active_ref, active_in_ref),
+        (slope_ref, slope_in_ref),
+    ):
+        full_ref[inner, :] = part_ref[held, :]
+        full_ref[done, :] = part_ref[last - HALO :, :]
     cols = 256
     for n in range(0, width, cols):
         part = slice(n, n + cols)
-        active, slope = head(own_ref, first_ref, part)
-        active_ref[top, part] = active[:HALO]
-        active_ref[bottom, part] = active[HALO:]
-        slope_ref[top, part] = slope[:HALO]
-        slope_ref[bottom, part] = slope[HALO:]
-    own = jnp.concatenate([active_ref[top, :], active_ref[bottom, :]], 0)
-    predicted = dot(second_ref[...], own, 1, 1).astype(BF16)
+        active_ref[mine, part], slope_ref[mine, part] = head(own_ref, first_ref, part)
+    predicted = dot(second_ref[...], active_ref[mine, :], 1, 1).astype(BF16)
     for m in range(copies_ref.shape[0]):
-        copies_ref[m, :, top] = predicted[:, :HALO]
-        copies_ref[m, :, inner] = predicted_in_ref[...]
-        copies_ref[m, :, bottom] = predicted[:, HALO:]
+        copies_ref[m, :, inner] = predicted_in_ref[:, held]
+        copies_ref[m, :, done] = predicted_in_ref[:, last - HALO :]
+        copies_ref[m, :, mine] = predicted
 
 
 def split_loss(tile, loss, fields):
@@ -188,14 +195,13 @@
 
 def score_kernel(
     everyone_ref, target_ref, patch_ref, second_ref, slope_ref, active_ref, normed_ref,
-    keep_ref, send_ref, dpre_ref, held_ref,
+    keep_ref, send_ref, dpre_ref,
 ):
     members, fields, cells = everyone_ref.shape
     width = slope_ref.shape[1]
-    me = lax.axis_index("xh") * lax.axis_size("y") + lax.axis_index("y")
-    core = lax.axis_index("co")
+    me = member_place(lax.axis_index("xh") * lax.axis_size("y") + lax.axis_index("y"), members)
     entries = fields * PATCH
-    share = held_ref.shape[3]
+    share = keep_ref.shape[2]
 
     def target_of(xl, member):
         return (member % 4) * 4 + (member // 4) * 2 + xl
@@ -230,21 +236,25 @@
     for n in range(0, width, cols):
         part = slice(n, n + cols)
         d_active = dot(outer[:, :fields], second_ref[:, part])
-        d_pre = (d_active * slope_ref[:, part].astype(F32)).astype(BF16)
-        dpre_ref[:, part] = d_pre
-        grad = dot(normed_ref[...], d_pre, 0, 0).astype(BF16)
+        dpre_ref[:, part] = (d_active * slope_ref[:, part].astype(F32)).astype(BF16)
+
+    def weight_grads(kept):
+        for n in range(0, width, cols):
+            grad = dot(normed_ref[...], dpre_ref[:, n : n + cols], 0, 0).astype(BF16)
+            for band, slot in places:
+                to_ref = keep_ref if band % 2 == kept else send_ref
+                rows = grad[band * share : (band + 1) * share]
+                for c in range(0, cols, LANES):
+                    to_ref[target_of(slot[0], (n + c) // LANES), slot[1]] = rows[:, c : c + LANES]
+        grad = dot(active_ref[...], outer, 0, 0)
+        grad = split_loss(grad, loss, fields).astype(BF16)
         for band, slot in places:
-            rows = grad[band * share : (band + 1) * share]
-            for c in range(0, cols, LANES):
-                block = (n + c) // LANES
-                held_ref[band % 2, target_of(slot[0], block), slot[1]] = rows[:, c : c + LANES]
-    second = dot(active_ref[...], outer, 0, 0)
-    second = split_loss(second, loss, fields).astype(BF16)
-    for band, slot in places:
-        rows = second[band * share : (band + 1) * share]
-        held_ref[band % 2, target_of(slot[0], slot[1]), members] = rows
-    keep_ref[...] = held_ref[core]
-    send_ref[...] = held_ref[1 - core]
+            to_ref = keep_ref if band % 2 == kept else send_ref
+            to_ref[target_of(slot[0], slot[1]), members] = grad[band * share : (band + 1) * share]
+
+    core = lax.axis_index("co")
+    pl.when(core == 0)(lambda: weight_grads(0))
+    pl.when(core == 1)(lambda: weight_grads(1))
 
 
 def backward_kernel(
@@ -264,27 +274,33 @@
                 (rim_ref.at[0], same_hbm),
                 (rim_ref.at[1], other_hbm),
                 (edge_ref, edge_hbm),
-                (grad_ref, grad_hbm.at[HALO : cells - HALO]),
+                *(
+                    (grad_ref.at[i : i + HALO], grad_hbm.at[i + HALO : i + 2 * HALO])
+                    for i in range(0, cells - 2 * HALO, HALO)
+                ),
             ]
         )
     ]
     cols = 256
-    mean = jnp.zeros((cells, 1), F32)
-    along = jnp.zeros((cells, 1), F32)
+    mean = jnp.zeros((cells, LANES), F32)
+    along = jnp.zeros((cells, LANES), F32)
     for n in range(0, width, cols):
         part = slice(n, n + cols)
-        d_normed = dot(dpre_ref[...], first_ref[part, :], 1, 1)
-        total_ref[:, part] = d_normed
-        mean = mean + jnp.sum(d_normed * gain[:, part], -1, keepdims=True)
-        along = along + jnp.sum(d_normed * normed_ref[:, part].astype(F32), -1, keepdims=True)
+        d_normed = dot(dpre_ref[...], first_ref[:, part])
+        scaled = d_normed * gain[:, part]
+        total_ref[:, part] = scaled
+        shared = d_normed * normed_ref[:, part].astype(F32)
+        for c in range(0, cols, LANES):
+            mean = mean + scaled[:, c : c + LANES]
+            along = along + shared[:, c : c + LANES]
+    mean = jnp.sum(mean, -1, keepdims=True)
+    along = jnp.sum(along, -1, keepdims=True)
     for block in range(blocks):
         own = slice(block * HALO, (block + 1) * HALO)
         inner = mean[own] * (1.0 / width) + normed_ref[own, :].astype(F32) * inverse * (
             along[own] * (1.0 / width)
         )
-        d_summed = inv_ref[own, :1] * (total_ref[own, :] * gain - inner)
-        total_ref[own, :] = d_summed
-        low_ref[own, :] = d_summed.astype(BF16)
+        low_ref[own, :] = (inv_ref[own, :1] * (total_ref[own, :] - inner)).astype(BF16)
     for row in (0, blocks + 1, 1, blocks, *range(2, blocks)):
         near = slice(max(row - 2, 0) * HALO, min(row + 1, blocks) * HALO)
         back = dot(turned_ref[row * HALO : (row + 1) * HALO, near], low_ref[near, :]) * (1.0 / NEIGH)
@@ -294,14 +310,13 @@
                 saves[0].start()
                 saves[1].start()
             continue
-        value = total_ref[(row - 1) * HALO : row * HALO, :] + back
         if row in (1, blocks):
-            edge_ref[0 if row == 1 else 1] = value
+            edge_ref[0 if row == 1 else 1] = back
         else:
-            grad_ref[(row - 2) * HALO : (row - 1) * HALO, :] = value.astype(BF16)
+            grad_ref[(row - 2) * HALO : (row - 1) * HALO, :] = back.astype(BF16)
+            saves[row + 1].start()
         if row == blocks:
             saves[2].start()
-    saves[3].start()
     for save in saves:
         save.wait()
 
@@ -342,9 +357,10 @@
 
 
 def last_kernel(fields, patches, parts_ref, first_ref, second_ref, loss_ref):
-    for k in range(parts_ref.shape[0]):
-        first_ref[:, k * LANES : (k + 1) * LANES] = parts_ref[k, 0].astype(F32)
-    tile = parts_ref[lax.axis_index("z"), 1].astype(F32)
+    members = parts_ref.shape[0]
+    for m in range(members):
+        first_ref[:, m * LANES : (m + 1) * LANES] = parts_ref[member_place(m, members), 0].astype(F32)
+    tile = parts_ref[member_place(lax.axis_index("z"), members), 1].astype(F32)
     second_ref[...] = tile[:, :fields]
     loss_ref[...] = read_loss(tile, fields)[:1, :] * (1.0 / patches)
 
@@ -358,6 +374,18 @@
 BAND = ("z", "xl", "co")
 MEM = ("xh", "y")
 PLANE = ("y", "xh", "xl")
+
+
+def member_groups(bands, members):
+    groups = []
+    for band in range(bands):
+        group = [band * members + m for m in range(members)]
+        groups.append(group if band % 2 == 0 else group[::-1])
+    return groups
+
+
+def member_place(member, members):
+    return jnp.where(lax.axis_index("co") == 0, member, members - 1 - member)
 
 
 def per_device(hidden, gain, w_first, w_second, target, patch_ids, neighbours):
@@ -379,23 +407,24 @@
         anywhere=(0,),
         held=(0, 1),
     )
+    same = lax.ppermute(rim_same, "co", cores)
     other = lax.ppermute(rim_other, BAND, chips)
-    same = lax.ppermute(rim_same, "co", cores)
-    half = cells // 2
-    saved = [shape((half, width), BF16)] * 3 + [shape((half, LANES), F32)]
-    *inside, gain, first, second, partial, outside, turned = call(
+    held = cells - HALO
+    saved = [shape((held, width), BF16)] * 3 + [shape((held, LANES), F32)]
+    *inside, gain, first, second, partial, outside, turned, first_turned = call(
         inner_kernel,
         [
-            shape((fields, half), BF16),
+            shape((fields, held), BF16),
             *saved,
             shape((1, width), F32),
             shape(w_first.shape, BF16),
             shape((fields, width), BF16),
-            shape((half, width), F32),
-            shape((2, HALO, HALO), BF16),
+            shape((HALO, width), F32),
+            shape((HALO, HALO), BF16),
             shape((cells + 2 * HALO, cells), BF16),
+            shape(w_first.shape[::-1], BF16),
         ],
-        [neighbours, states, gain[None], w_first, w_second.T],
+        [same, neighbours, states, gain[None], w_first, w_second.T],
         10**9,
         16,
         [
@@ -403,19 +432,20 @@
             pltpu.VMEM(states.shape, BF16),
             pltpu.SemaphoreType.DMA((5,)),
         ],
-        anywhere=(0, 1, 2, 3, 4),
-        held=(5, 6, 7),
+        anywhere=(1, 2, 3, 4, 5),
+        held=(5, 6, 7, 10, 11),
     )
     saved = [shape((cells, width), BF16)] * 3 + [shape((cells, LANES), F32)]
     copies, slope, active, normed, inv_root = call(
         outer_kernel,
         [shape((members, fields, cells), BF16)] + saved,
-        [same, other, partial, outside, gain, second, *inside, first],
+        [other, partial, outside, gain, second, *inside, first],
         10**9,
         20,
-        [pltpu.VMEM((half, width), BF16)],
-    )
-    everyone = lax.all_to_all(copies, MEM, 0, 0)
+        [pltpu.VMEM((HALO, width), BF16)],
+    )
+    groups = member_groups(bands, members)
+    everyone = lax.all_to_all(copies, BAND + MEM, 0, 0, axis_index_groups=groups)
     message = (2 * members, members + 1, share, LANES)
     keep, send, d_pre = call(
         score_kernel,
@@ -423,7 +453,6 @@
         [everyone, target, patch_ids[None], second, slope, active, normed],
         2 * 10**9,
         20,
-        [pltpu.VMEM((2,) + message, BF16)],
     )
     got = lax.ppermute(send, "co", cores)
     grad, edge, rim_same, rim_other = call(
@@ -434,7 +463,7 @@
             shape((HALO, width), BF16),
             shape((HALO, width), BF16),
         ],
-        [first, d_pre, normed, inv_root, turned, gain],
+        [first_turned, d_pre, normed, inv_root, turned, gain],
         2 * 10**9,
         20,
         [
@@ -443,7 +472,7 @@
             pltpu.VMEM((cells - 2 * HALO, width), BF16),
             pltpu.VMEM((2, HALO, width), F32),
             pltpu.VMEM((2, HALO, width), BF16),
-            pltpu.SemaphoreType.DMA((4,)),
+            pltpu.SemaphoreType.DMA((3 + cells // HALO - 2,)),
         ],
         stored=(0, 1, 2, 3),
     )
@@ -453,8 +482,8 @@
     )
     parts = lax.all_to_all(mine, PLANE, 0, 0)
     parts, rim_same, rim_other = lax.optimization_barrier((parts, rim_same, rim_other))
+    same = lax.ppermute(rim_same, "co", cores)
     other = lax.ppermute(rim_other, BAND, chips)
-    same = lax.ppermute(rim_same, "co", cores)
     last = cells // HALO - 1
     grad_hidden = pl.pallas_call(
         edge_kernel,
@@ -478,7 +507,7 @@
     (folded,) = call(
         functools.partial(fold_kernel, fields), [shape(message, BF16)], [parts], 10**6, 8
     )
-    parts = lax.all_to_all(folded, MEM, 0, 0)
+    parts = lax.all_to_all(folded, BAND + MEM, 0, 0, axis_index_groups=groups)
     grad_first, grad_second, loss = call(
         functools.partial(last_kernel, fields, cells // PATCH * bands),
         [shape((share, width), F32), shape((share, fields), F32), shape((1, 1), F32)],

time: 97.1 us -> 95.9 us (0.988)
    all_to_all x1, blocking collectives: 21.6 us -> 24 us  [per_device(): parts = lax.all_to_all(mine, PLANE, 0, 0)]
    all_to_all x1, blocking collectives: 19.4 us -> 17.4 us  [per_device(): lax.all_to_all(copies, BAND + MEM, 0, 0, axis_index_groups=groups)]
    all_to_all x1, starting transfers between devices: 10.8 us -> 9.76 us  [per_device(): parts = lax.all_to_all(planed, 'z', 0, 0)]
  transfers between devices with their start and end apart: 7 -> 7, of which waited for: 3 -> 3; matrix products, arithmetic and copies ran while one was open for 0% -> 0% of each run, Pallas kernels for 9% -> 10%
where the time goes in v3:
time: 95.9 us; the launch traced here: 95.3 us
  blocking collectives  41.4 us (43%)
  starting transfers between devices  21.3 us (22%)
  Pallas kernels  16.4 us (17%)
  waiting for transfers between devices  15.4 us (16%)
    all_to_all x1, blocking collectives, per_device(): parts = lax.all_to_all(mine, PLANE, 0, 0)  24 us
    all_to_all x1, blocking collectives, per_device(): lax.all_to_all(copies, BAND + MEM, 0, 0, axis_index_groups=groups)  17.4 us
    pallas_call x9, Pallas kernels, call(): pl.pallas_call(kernel, out_shape=[pltpu.HBM(o.shape, o.dtype) if i in sto...  15.5 us
    all_to_all x1, starting transfers between devices, per_device(): parts = lax.all_to_all(planed, 'z', 0, 0)  9.76 us
    ppermute x2, starting transfers between devices, per_device(): other = lax.ppermute(rim_other, BAND, chips)  7.72 us
    all_to_all x1, waiting for transfers between devices, per_device(): parts = lax.all_to_all(folded, BAND + MEM, 0, 0, axis_index_groups=groups)  7.11 us
    all_to_all x1, waiting for transfers between devices, per_device(): parts = lax.all_to_all(planed, 'z', 0, 0)  5.61 us
    all_to_all x1, starting transfers between devices, per_device(): parts = lax.all_to_all(folded, BAND + MEM, 0, 0, axis_index_groups=groups)  3.37 us
  transfers between devices with their start and end apart: 7, of which 3 were waited for; matrix products, arithmetic and copies ran while one was open for 0% of the time, Pallas kernels for 10%

profile of v3, /device:TPU:2, one launch (start us, length us, event | category | flops | bytes accessed | tf_op | source)
XLA Modules:
  0.0 95.3 jit_solution(7772670162604286004)
XLA Ops:
  0.6 1.1 %shard_map.102 = (bf16[128,1024]{1,0:T(8,128)(2,1)S(1)}, bf16[128,1024]{1,0:T(8,128)(2,1)S(1)}) custom-call(bf16[512,1024]{1,0:T(8,128)(2,1)} %bitcast.8), custom_call_target="tpu_custom_call" | custom-call | bytes 1572864 | tf_op jit(solution)/shard_map/pallas_call | solution.py:33
  1.7 0.1 collective-permute-start.1
  1.8 4.3 %collective-permute-start = (bf16[128,1024]{1,0:T(8,128)(2,1)S(1)}, bf16[128,1024]{1,0:T(8,128)(2,1)S(1)}, u32[]{:S(2)}, u32[]{:S(2)}) collective-permute-start(bf16[128,1024]{1,0:T(8,128)(2,1)S(1)} %get-tuple-element.38), channel_id=1, source_target_pairs={{8,16},{24,32},{40,48},{56,64},{72,80},{88,96},{104,112},{120,128}... | collective-permute-start | bytes 786440 | tf_op jit(solution)/shard_map/ppermute | solution.py:411
  6.1 0.0 collective-permute-done.1.same_ref
  6.1 4.2 %shard_map.103 = (bf16[100,384]{1,0:T(8,128)(2,1)S(1)}, bf16[384,1024]{1,0:T(8,128)(2,1)S(1)}, bf16[384,1024]{1,0:T(8,128)(2,1)S(1)}, bf16[384,1024]{1,0:T(8,128...) custom-call(bf16[128,1024]{1,0:T(8,128)(2,1)S(1)} %collective-permut, ...), custom_call_target="tpu_custom_call" | custom-call | flops 1000000000 | bytes 12008448 | tf_op jit(solution)/shard_map/pallas_call | solution.py:33
  10.3 2.6 %collective-permute-done.other_ref = bf16[128,1024]{1,0:T(8,128)(2,1)S(1)} collective-permute-done((bf16[128,1024]{1,0:T(8,128)(2,1)S(1)}, bf16[128,1024]{1,0:T(8,128)(2,1)S(1)}, u32[]{:S(2)}, u32[]{:S(2)}) %collective-permute-start) | collective-permute-done | bytes 262176 | tf_op jit(solution)/shard_map/ppermute | solution.py:411
  12.9 1.2 %shard_map.104 = (bf16[8,100,512]{2,1,0:T(8,128)(2,1)S(1)}, bf16[512,1024]{1,0:T(8,128)(2,1)S(1)}, bf16[512,1024]{1,0:T(8,128)(2,1)S(1)}, bf16[512,1024]{1,0:T(8,128)(2,1)S(1)}, f32[512,128]{1,0:T(8,128)S(1)}) custom-call(bf16[128,1024]{1,0:T(8,128)(2,1)S(1)} %collective-permute-done.other_ref, f32[128,1024]{1,0:T(8,128)S(1)} %get-tuple-element.40.partial_ref, ...), custom_call_target="tpu_custom_call" | custom-call | flops 1000000000 | bytes 9985024 | tf_op jit(solution)/shard_map/pallas_call | solution.py:33
  14.2 0.0 copy-start.1
  14.2 0.0 copy-start.2
  14.2 17.4 %all_to_all.20.everyone_ref = bf16[8,100,512]{2,1,0:T(8,128)(2,1)S(1)} all-to-all(bf16[8,100,512]{2,1,0:T(8,128)(2,1)S(1)} %get-tuple-element.50), channel_id=1, replica_groups={{0,1,2,3,4,5,6,7},{15,14,13,12,11,10,9,8},{16,17,18,19,20,21,22,23},{31..., dimensions={0} | all-to-all | bytes 1638400 | tf_op jit(solution)/shard_map/all_to_all | solution.py:448
  31.6 0.0 copy-done.1
  31.6 0.0 copy-done.2
  31.6 2.7 %shard_map.105 = (bf16[16,9,32,128]{3,2,1,0:T(8,128)(2,1)S(1)}, bf16[16,9,32,128]{3,2,1,0:T(8,128)(2,1)S(1)}, bf16[512,1024]{1,0:T(8,128)(2,1)S(1)}) custom-call(bf16[8,100,512]{2,1,0:T(8,128)(2,1)S(1)} %all_to_all.20.everyone_ref, f32[100,512]{1,0:T(8,128)S(1)} %copy-done.1, s32[1,512]{1,0:T(1,128)S(1)} %bitcast.6, ...), custom_call_target="tpu_custom_call" | custom-call | flops 2000000000 | bytes 7784448 | tf_op jit(solution)/shard_map/pallas_call | solution.py:33
  34.3 0.3 collective-permute-start.2
  34.5 3.7 %shard_map.106 = (bf16[512,1024]{1,0:T(8,128)(2,1)}, f32[2,128,1024]{2,1,0:T(8,128)}, bf16[128,1024]{1,0:T(8,128)(2,1)}, bf16[128,1024]{1,0:T(8,128)(2,1)}) custom-call(bf16[1024,1024]{1,0:T(8,128)(2,1)S(1)} %get-tuple-element.56.first_ref, bf16[512,1024]{1,0:T(8,128)(2,1)S(1)} %get-tuple-element.57.dpre_ref, ...), custom_call_target="tpu_custom_call" | custom-call | flops 2000000000 | bytes 7868416 | tf_op jit(solution)/shard_map/pallas_call | solution.py:33
  38.3 0.0 collective-permute-done.2.got_ref
  38.3 0.4 shard_map.107
  38.7 24.0 %all_to_all.21.parts_ref = bf16[16,9,32,128]{3,2,1,0:T(8,128)(2,1)S(1)} all-to-all(bf16[16,9,32,128]{3,2,1,0:T(8,128)(2,1)S(1)} %shard_map.107), channel_id=1, replica_groups=mesh['z'=8,'xl'=2,'co'=2,'xh'=2,'y'=4] {'y','xh','xl'}, dimensions={0} | all-to-all | bytes 2359296 | tf_op jit(solution)/shard_map/all_to_all | solution.py:483
  62.7 0.0 copy-start.4
  62.7 0.0 copy-start.3
  62.7 0.0 copy-start
  62.7 0.8 shard_map.108
  63.5 9.8 %all-to-all-start.2 = ((bf16[8,2,32,128]{3,2,1,0:T(8,128)(2,1)}), bf16[8,2,32,128]{3,2,1,0:T(8,128)(2,1)S(1)}, u32[]{:S(2)}, u32[]{:S(2)}) async-start(bf16[8,2,32,128]{3,2,1,0:T(8,128)(2,1)} %shard_map.108), calls=%async_computation.2 | async-start | bytes 262144 | tf_op jit(solution)/shard_map/all_to_all | solution.py:506
  73.3 0.0 copy-done.4
  73.3 0.1 collective-permute-start.3
  73.4 0.0 copy-done.3
  73.4 3.5 %collective-permute-start.4 = (bf16[128,1024]{1,0:T(8,128)(2,1)S(1)}, bf16[128,1024]{1,0:T(8,128)(2,1)S(1)}, u32[]{:S(2)}, u32[]{:S(2)}) collective-permute-start(bf16[128,1024]{1,0:T(8,128)(2,1)S(1)} %copy-done.3), channel_id=1, source_target_pairs={{8,16},{24,32},{40,48},{56,64},{72,80},{88,96},{104,112},{120,128}... | collective-permute-start | bytes 786440 | tf_op jit(solution)/shard_map/ppermute | solution.py:486
  76.9 5.6 %all-to-all-done.2.parts_ref = bf16[8,2,32,128]{3,2,1,0:T(8,128)(2,1)S(1)} async-done(((bf16[8,2,32,128]{3,2,1,0:T(8,128)(2,1)}), bf16[8,2,32,128]{3,2,1,0:T(8,128)(2,1)S(1)}, u32[]{:S(2)}, u32[]{:S(2)}) %all-to-all-start.2) | async-done | bytes 131104 | tf_op jit(solution)/shard_map/all_to_all | solution.py:506
  82.5 0.8 shard_map.109
  83.2 3.4 %all-to-all-start.3 = ((bf16[8,2,32,128]{3,2,1,0:T(8,128)(2,1)}), bf16[8,2,32,128]{3,2,1,0:T(8,128)(2,1)S(1)}, u32[]{:S(2)}, u32[]{:S(2)}) async-start(bf16[8,2,32,128]{3,2,1,0:T(8,128)(2,1)} %shard_map.109), calls=%async_computation.3 | async-start | bytes 262144 | tf_op jit(solution)/shard_map/all_to_all | solution.py:510
  86.6 0.0 collective-permute-done.3.same_ref
  86.6 0.0 collective-permute-done.4.other_ref
  86.6 0.0 copy-done
  86.7 0.9 shard_map.111
  87.5 7.1 %all-to-all-done.3.parts_ref = bf16[8,2,32,128]{3,2,1,0:T(8,128)(2,1)S(1)} async-done(((bf16[8,2,32,128]{3,2,1,0:T(8,128)(2,1)}), bf16[8,2,32,128]{3,2,1,0:T(8,128)(2,1)S(1)}, u32[]{:S(2)}, u32[]{:S(2)}) %all-to-all-start.3) | async-done | bytes 131104 | tf_op jit(solution)/shard_map/all_to_all | solution.py:510
  94.6 0.7 shard_map.110
Async XLA Ops:
  1.7 4.4 %collective-permute-start.1 = (bf16[128,1024]{1,0:T(8,128)(2,1)S(1)}, bf16[128,1024]{1,0:T(8,128)(2,1)S(1)}, u32[]{:S(2)}, u32[]{:S(2)}) collective-permute-start(bf16[128,1024]{1,0:T(8,128)(2,1)S(1)} %get-tuple-element.39), channel_id=1, source_target_pairs={{0,8},{8,0},{1,9},{9,1},{2,10},{10,2},{3,11},{11,3},{4,12},{12,4},... | collective-permute-start | bytes 786440 | tf_op jit(solution)/shard_map/ppermute | solution.py:410
  1.8 11.1 %collective-permute-start = (bf16[128,1024]{1,0:T(8,128)(2,1)S(1)}, bf16[128,1024]{1,0:T(8,128)(2,1)S(1)}, u32[]{:S(2)}, u32[]{:S(2)}) collective-permute-start(bf16[128,1024]{1,0:T(8,128)(2,1)S(1)} %get-tuple-element.38), channel_id=1, source_target_pairs={{8,16},{24,32},{40,48},{56,64},{72,80},{88,96},{104,112},{120,128}... | collective-permute-start | bytes 786440 | tf_op jit(solution)/shard_map/ppermute | solution.py:411
  14.2 17.4 %copy-start.1 = (f32[100,512]{1,0:T(8,128)S(1)}, f32[100,512]{1,0:T(8,128)}, u32[]{:S(2)}) copy-start(f32[100,512]{1,0:T(8,128)} %target_ref.1) | copy-start | bytes 614404
  14.2 17.4 %copy-start.2 = (s32[512]{0:T(512)S(1)}, s32[512]{0:T(512)}, u32[]{:S(2)}) copy-start(s32[512]{0:T(512)} %param.12) | copy-start | bytes 6148
  34.3 4.0 %collective-permute-start.2 = (bf16[16,9,32,128]{3,2,1,0:T(8,128)(2,1)S(1)}, bf16[16,9,32,128]{3,2,1,0:T(8,128)(2,1)S(1)}, u32[]{:S(2)}, u32[]{:S(2)}) collective-permute-start(bf16[16,9,32,128]{3,2,1,0:T(8,128)(2,1)S(1)} %get-tuple-element.55), channel_id=1, source_target_pairs={{0,8},{8,0},{1,9},{9,1},{2,10},{10,2},{3,11},{11,3},{4,12},{12,4},... | collective-permute-start | bytes 3538952 | tf_op jit(solution)/shard_map/ppermute | solution.py:457
  62.7 10.6 %copy-start.4 = (bf16[128,1024]{1,0:T(8,128)(2,1)S(1)}, bf16[128,1024]{1,0:T(8,128)(2,1)}, u32[]{:S(2)}) copy-start(bf16[128,1024]{1,0:T(8,128)(2,1)} %get-tuple-element.68) | copy-start | bytes 786436
  62.7 10.7 %copy-start.3 = (bf16[128,1024]{1,0:T(8,128)(2,1)S(1)}, bf16[128,1024]{1,0:T(8,128)(2,1)}, u32[]{:S(2)}) copy-start(bf16[128,1024]{1,0:T(8,128)(2,1)} %get-tuple-element.69) | copy-start | bytes 786436
  62.7 23.9 %copy-start = (f32[2,128,1024]{2,1,0:T(8,128)S(1)}, f32[2,128,1024]{2,1,0:T(8,128)}, u32[]{:S(2)}) copy-start(f32[2,128,1024]{2,1,0:T(8,128)} %get-tuple-element.67.edge_ref) | copy-start | bytes 3145732
  63.5 18.9 %all-to-all-start.2 = ((bf16[8,2,32,128]{3,2,1,0:T(8,128)(2,1)}), bf16[8,2,32,128]{3,2,1,0:T(8,128)(2,1)S(1)}, u32[]{:S(2)}, u32[]{:S(2)}) async-start(bf16[8,2,32,128]{3,2,1,0:T(8,128)(2,1)} %shard_map.108), calls=%async_computation.2 | async-start | bytes 262144 | tf_op jit(solution)/shard_map/all_to_all | solution.py:506
  73.3 13.3 %collective-permute-start.3 = (bf16[128,1024]{1,0:T(8,128)(2,1)S(1)}, bf16[128,1024]{1,0:T(8,128)(2,1)S(1)}, u32[]{:S(2)}, u32[]{:S(2)}) collective-permute-start(bf16[128,1024]{1,0:T(8,128)(2,1)S(1)} %copy-done.4), channel_id=1, source_target_pairs={{0,8},{8,0},{1,9},{9,1},{2,10},{10,2},{3,11},{11,3},{4,12},{12,4},... | collective-permute-start | bytes 786440 | tf_op jit(solution)/shard_map/ppermute | solution.py:485
  73.4 13.2 %collective-permute-start.4 = (bf16[128,1024]{1,0:T(8,128)(2,1)S(1)}, bf16[128,1024]{1,0:T(8,128)(2,1)S(1)}, u32[]{:S(2)}, u32[]{:S(2)}) collective-permute-start(bf16[128,1024]{1,0:T(8,128)(2,1)S(1)} %copy-done.3), channel_id=1, source_target_pairs={{8,16},{24,32},{40,48},{56,64},{72,80},{88,96},{104,112},{120,128}... | collective-permute-start | bytes 786440 | tf_op jit(solution)/shard_map/ppermute | solution.py:486
  83.2 11.4 %all-to-all-start.3 = ((bf16[8,2,32,128]{3,2,1,0:T(8,128)(2,1)}), bf16[8,2,32,128]{3,2,1,0:T(8,128)(2,1)S(1)}, u32[]{:S(2)}, u32[]{:S(2)}) async-start(bf16[8,2,32,128]{3,2,1,0:T(8,128)(2,1)} %shard_map.109), calls=%async_computation.3 | async-start | bytes 262144 | tf_op jit(solution)/shard_map/all_to_all | solution.py:510

commit v4 on v3

--- a/solution.py
+++ b/solution.py
@@ -40,7 +40,9 @@
         out_specs=[ANY if i in stored else VMEM for i in range(len(outs))],
         scratch_shapes=list(scratch),
         compiler_params=pltpu.CompilerParams(vmem_limit_bytes=limit * 2**20),
-        cost_estimate=pl.CostEstimate(flops=flops, bytes_accessed=moved, transcendentals=0),
+        cost_estimate=pl.CostEstimate(flops=flops, bytes_accessed=moved, transcendentals=0)
+        if flops
+        else None,
     )(*args)
 
 
@@ -89,7 +91,7 @@
 def inner_kernel(
     same_ref, near_hbm, states_hbm, gain_hbm, first_hbm, second_hbm,
     predicted_ref, slope_ref, active_ref, normed_ref, inv_ref, gain_ref, first_ref, second_ref,
-    partial_ref, outside_ref, turned_ref, first_turned_ref,
+    partial_ref, outside_ref, turned_ref, first_turned_ref, turned_hbm,
     near_ref, states_ref, done,
 ):
     loads = [
@@ -116,6 +118,8 @@
         total = count_rows(near, block)
         turned_ref[block * HALO : (block + 3) * HALO, block * HALO : (block + 1) * HALO] = total.astype(BF16)
         counts.append(total.T.astype(BF16))
+    save = pltpu.make_async_copy(turned_ref, turned_hbm, done.at[5])
+    save.start()
     outside = (counts[0][:, :HALO], counts[-1][:, 2 * HALO :])
     inside = (counts[0][:, HALO:], counts[-1][:, : 2 * HALO])
     loads[1].wait()
@@ -143,6 +147,7 @@
     predicted_ref[...] = dot(second_ref[...], active_ref[...], 1, 1).astype(BF16)
     for n in range(0, first_ref.shape[0], LANES):
         first_turned_ref[:, n : n + LANES] = first_ref[n : n + LANES, :].T
+    save.wait()
 
 
 def outer_kernel(
@@ -259,8 +264,8 @@
 
 def backward_kernel(
     first_ref, dpre_ref, normed_ref, inv_ref, turned_ref, gain_ref,
-    grad_hbm, edge_hbm, same_hbm, other_hbm,
-    total_ref, low_ref, grad_ref, edge_ref, rim_ref, done,
+    low_hbm, same_hbm, other_hbm,
+    total_ref, low_ref, rim_ref, done,
 ):
     cells, width = low_ref.shape
     blocks = cells // HALO
@@ -273,11 +278,7 @@
             [
                 (rim_ref.at[0], same_hbm),
                 (rim_ref.at[1], other_hbm),
-                (edge_ref, edge_hbm),
-                *(
-                    (grad_ref.at[i : i + HALO], grad_hbm.at[i + HALO : i + 2 * HALO])
-                    for i in range(0, cells - 2 * HALO, HALO)
-                ),
+                (low_ref, low_hbm),
             ]
         )
     ]
@@ -295,28 +296,19 @@
             along = along + shared[:, c : c + LANES]
     mean = jnp.sum(mean, -1, keepdims=True)
     along = jnp.sum(along, -1, keepdims=True)
-    for block in range(blocks):
+    for block in (0, blocks - 1, *range(1, blocks - 1)):
         own = slice(block * HALO, (block + 1) * HALO)
         inner = mean[own] * (1.0 / width) + normed_ref[own, :].astype(F32) * inverse * (
             along[own] * (1.0 / width)
         )
         low_ref[own, :] = (inv_ref[own, :1] * (total_ref[own, :] - inner)).astype(BF16)
-    for row in (0, blocks + 1, 1, blocks, *range(2, blocks)):
-        near = slice(max(row - 2, 0) * HALO, min(row + 1, blocks) * HALO)
-        back = dot(turned_ref[row * HALO : (row + 1) * HALO, near], low_ref[near, :]) * (1.0 / NEIGH)
-        if row in (0, blocks + 1):
-            rim_ref[1 - core if row == 0 else core] = back.astype(BF16)
-            if row > 0:
-                saves[0].start()
-                saves[1].start()
-            continue
-        if row in (1, blocks):
-            edge_ref[0 if row == 1 else 1] = back
-        else:
-            grad_ref[(row - 2) * HALO : (row - 1) * HALO, :] = back.astype(BF16)
-            saves[row + 1].start()
-        if row == blocks:
-            saves[2].start()
+    saves[2].start()
+    up = dot(turned_ref[:HALO, :HALO], low_ref[:HALO, :]) * (1.0 / NEIGH)
+    rim_ref[1 - core] = up.astype(BF16)
+    down = dot(turned_ref[cells + HALO :, cells - HALO :], low_ref[cells - HALO :, :]) * (1.0 / NEIGH)
+    rim_ref[core] = down.astype(BF16)
+    saves[0].start()
+    saves[1].start()
     for save in saves:
         save.wait()
 
@@ -365,10 +357,25 @@
     loss_ref[...] = read_loss(tile, fields)[:1, :] * (1.0 / patches)
 
 
-def edge_kernel(grad_in_ref, edge_ref, same_ref, other_ref, grad_ref):
-    del grad_in_ref
-    rim = jnp.where(pl.program_id(0) == lax.axis_index("co"), other_ref[...], same_ref[...])
-    grad_ref[...] = (edge_ref[0] + rim.astype(F32)).astype(BF16)
+def gather_kernel(low_hbm, turned_hbm, same_ref, other_ref, grad_ref, low_ref, turned_ref, done):
+    loads = [
+        pltpu.make_async_copy(low_hbm, low_ref, done.at[0]),
+        pltpu.make_async_copy(turned_hbm, turned_ref, done.at[1]),
+    ]
+    for load in loads:
+        load.start()
+    for load in loads:
+        load.wait()
+    core = lax.axis_index("co")
+    blocks = low_ref.shape[0] // HALO
+    for row in range(1, blocks + 1):
+        near = slice(max(row - 2, 0) * HALO, min(row + 1, blocks) * HALO)
+        back = dot(turned_ref[row * HALO : (row + 1) * HALO, near], low_ref[near, :]) * (1.0 / NEIGH)
+        if row == 1:
+            back = back + jnp.where(core == 0, other_ref[...], same_ref[...]).astype(F32)
+        if row == blocks:
+            back = back + jnp.where(core == 0, same_ref[...], other_ref[...]).astype(F32)
+        grad_ref[(row - 1) * HALO : row * HALO, :] = back.astype(BF16)
 
 
 BAND = ("z", "xl", "co")
@@ -411,7 +418,7 @@
     other = lax.ppermute(rim_other, BAND, chips)
     held = cells - HALO
     saved = [shape((held, width), BF16)] * 3 + [shape((held, LANES), F32)]
-    *inside, gain, first, second, partial, outside, turned, first_turned = call(
+    *inside, gain, first, second, partial, outside, turned, first_turned, turned_saved = call(
         inner_kernel,
         [
             shape((fields, held), BF16),
@@ -423,6 +430,7 @@
             shape((HALO, HALO), BF16),
             shape((cells + 2 * HALO, cells), BF16),
             shape(w_first.shape[::-1], BF16),
+            shape((cells + 2 * HALO, cells), BF16),
         ],
         [same, neighbours, states, gain[None], w_first, w_second.T],
         10**9,
@@ -430,9 +438,10 @@
         [
             pltpu.VMEM(neighbours.shape, jnp.int32),
             pltpu.VMEM(states.shape, BF16),
-            pltpu.SemaphoreType.DMA((5,)),
+            pltpu.SemaphoreType.DMA((6,)),
         ],
         anywhere=(1, 2, 3, 4, 5),
+        stored=(12,),
         held=(5, 6, 7, 10, 11),
     )
     saved = [shape((cells, width), BF16)] * 3 + [shape((cells, LANES), F32)]
@@ -455,11 +464,10 @@
         20,
     )
     got = lax.ppermute(send, "co", cores)
-    grad, edge, rim_same, rim_other = call(
+    low, rim_same, rim_other = call(
         backward_kernel,
         [
             shape((cells, width), BF16),
-            shape((2, HALO, width), F32),
             shape((HALO, width), BF16),
             shape((HALO, width), BF16),
         ],
@@ -469,14 +477,12 @@
         [
             pltpu.VMEM((cells, width), F32),
             pltpu.VMEM((cells, width), BF16),
-            pltpu.VMEM((cells - 2 * HALO, width), BF16),
-            pltpu.VMEM((2, HALO, width), F32),
             pltpu.VMEM((2, HALO, width), BF16),
-            pltpu.SemaphoreType.DMA((3 + cells // HALO - 2,)),
+            pltpu.SemaphoreType.DMA((3,)),
         ],
-        stored=(0, 1, 2, 3),
-    )
-    got, grad = lax.optimization_barrier((got, grad))
+        stored=(0, 1, 2),
+    )
+    got, low = lax.optimization_barrier((got, low))
     (mine,) = call(
         functools.partial(pair_kernel, fields), [shape(message, BF16)], [keep, got], 10**6, 8
     )
@@ -484,21 +490,19 @@
     parts, rim_same, rim_other = lax.optimization_barrier((parts, rim_same, rim_other))
     same = lax.ppermute(rim_same, "co", cores)
     other = lax.ppermute(rim_other, BAND, chips)
-    last = cells // HALO - 1
-    grad_hidden = pl.pallas_call(
-        edge_kernel,
-        grid=(2,),
-        out_shape=shape((cells, width), BF16),
-        in_specs=[
-            pl.BlockSpec(memory_space=pl.ANY),
-            pl.BlockSpec((1, HALO, width), lambda i: (i, 0, 0)),
-            pl.BlockSpec((HALO, width), lambda i: (0, 0)),
-            pl.BlockSpec((HALO, width), lambda i: (0, 0)),
+    (grad_hidden,) = call(
+        gather_kernel,
+        [shape((cells, width), BF16)],
+        [low, turned_saved, same, other],
+        0,
+        16,
+        [
+            pltpu.VMEM((cells, width), BF16),
+            pltpu.VMEM(turned.shape, BF16),
+            pltpu.SemaphoreType.DMA((2,)),
         ],
-        out_specs=pl.BlockSpec((HALO, width), lambda i: (i * last, 0)),
-        input_output_aliases={0: 0},
-        compiler_params=pltpu.CompilerParams(vmem_limit_bytes=8 * 2**20),
-    )(grad, edge, same, other)
+        anywhere=(0, 1),
+    )
     message = (members, 2, share, LANES)
     (planed,) = call(
         functools.partial(plane_kernel, fields), [shape(message, BF16)], [parts], 10**6, 8

time: 95.9 us -> 95.1 us (level)
  waiting for transfers between devices: 15.4 us -> 13.2 us
  Pallas kernels: 16.4 us -> 18 us
    pallas_call x9 -> x10, Pallas kernels: 15.5 us -> 18 us  [call(): pl.pallas_call(kernel, out_shape=[pltpu.HBM(o.shape, o.dtype) if i in sto...]
    all_to_all x1, waiting for transfers between devices: 7.11 us -> 4.95 us  [per_device(): parts = lax.all_to_all(folded, BAND + MEM, 0, 0, axis_index_groups=groups)]
  transfers between devices with their start and end apart: 7 -> 7, of which waited for: 3 -> 3; matrix products, arithmetic and copies ran while one was open for 0% -> 0% of each run, Pallas kernels for 10% -> 12%
where the time goes in v4:
time: 95.1 us; the launch traced here: 94.6 us
  blocking collectives  41.4 us (44%)
  starting transfers between devices  21.1 us (22%)
  Pallas kernels  18 us (19%)
  waiting for transfers between devices  13.2 us (14%)
    all_to_all x1, blocking collectives, per_device(): parts = lax.all_to_all(mine, PLANE, 0, 0)  24 us
    pallas_call x10, Pallas kernels, call(): pl.pallas_call(kernel, out_shape=[pltpu.HBM(o.shape, o.dtype) if i in sto...  18 us
    all_to_all x1, blocking collectives, per_device(): lax.all_to_all(copies, BAND + MEM, 0, 0, axis_index_groups=groups)  17.4 us
    all_to_all x1, starting transfers between devices, per_device(): parts = lax.all_to_all(planed, 'z', 0, 0)  9.71 us
    ppermute x2, starting transfers between devices, per_device(): other = lax.ppermute(rim_other, BAND, chips)  7.72 us
    all_to_all x1, waiting for transfers between devices, per_device(): parts = lax.all_to_all(planed, 'z', 0, 0)  5.61 us
    all_to_all x1, waiting for transfers between devices, per_device(): parts = lax.all_to_all(folded, BAND + MEM, 0, 0, axis_index_groups=groups)  4.95 us
    all_to_all x1, starting transfers between devices, per_device(): parts = lax.all_to_all(folded, BAND + MEM, 0, 0, axis_index_groups=groups)  3.37 us
  transfers between devices with their start and end apart: 7, of which 3 were waited for; matrix products, arithmetic and copies ran while one was open for 0% of the time, Pallas kernels for 12%

profile of v4, /device:TPU:2, one launch (start us, length us, event | category | flops | bytes accessed | tf_op | source)
XLA Modules:
  0.0 94.6 jit_solution(1032340554356016707)
XLA Ops:
  0.6 1.1 %shard_map.102 = (bf16[128,1024]{1,0:T(8,128)(2,1)S(1)}, bf16[128,1024]{1,0:T(8,128)(2,1)S(1)}) custom-call(bf16[512,1024]{1,0:T(8,128)(2,1)} %bitcast.7), custom_call_target="tpu_custom_call" | custom-call | tf_op jit(solution)/shard_map/pallas_call | solution.py:33
  1.7 0.1 collective-permute-start.1
  1.8 4.3 %collective-permute-start = (bf16[128,1024]{1,0:T(8,128)(2,1)S(1)}, bf16[128,1024]{1,0:T(8,128)(2,1)S(1)}, u32[]{:S(2)}, u32[]{:S(2)}) collective-permute-start(bf16[128,1024]{1,0:T(8,128)(2,1)S(1)} %get-tuple-element.38), channel_id=1, source_target_pairs={{8,16},{24,32},{40,48},{56,64},{72,80},{88,96},{104,112},{120,128}... | collective-permute-start | bytes 786440 | tf_op jit(solution)/shard_map/ppermute | solution.py:418
  6.1 0.0 collective-permute-done.1.same_ref
  6.1 4.2 %shard_map.103 = (bf16[100,384]{1,0:T(8,128)(2,1)S(1)}, bf16[384,1024]{1,0:T(8,128)(2,1)S(1)}, bf16[384,1024]{1,0:T(8,128)(2,1)S(1)}, bf16[384,1024]{1,0:T(8,128...) custom-call(bf16[128,1024]{1,0:T(8,128)(2,1)S(1)} %collective-permut, ...), custom_call_target="tpu_custom_call" | custom-call | flops 1000000000 | bytes 12794880 | tf_op jit(solution)/shard_map/pallas_call | solution.py:33
  10.3 2.6 %collective-permute-done.other_ref = bf16[128,1024]{1,0:T(8,128)(2,1)S(1)} collective-permute-done((bf16[128,1024]{1,0:T(8,128)(2,1)S(1)}, bf16[128,1024]{1,0:T(8,128)(2,1)S(1)}, u32[]{:S(2)}, u32[]{:S(2)}) %collective-permute-start) | collective-permute-done | bytes 262176 | tf_op jit(solution)/shard_map/ppermute | solution.py:418
  12.9 1.2 %shard_map.104 = (bf16[8,100,512]{2,1,0:T(8,128)(2,1)S(1)}, bf16[512,1024]{1,0:T(8,128)(2,1)S(1)}, bf16[512,1024]{1,0:T(8,128)(2,1)S(1)}, bf16[512,1024]{1,0:T(8,128)(2,1)S(1)}, f32[512,128]{1,0:T(8,128)S(1)}) custom-call(bf16[128,1024]{1,0:T(8,128)(2,1)S(1)} %collective-permute-done.other_ref, f32[128,1024]{1,0:T(8,128)S(1)} %get-tuple-element.40.partial_ref, ...), custom_call_target="tpu_custom_call" | custom-call | flops 1000000000 | bytes 9985024 | tf_op jit(solution)/shard_map/pallas_call | solution.py:33
  14.2 0.0 copy-start
  14.2 0.0 copy-start.1
  14.2 17.4 %all_to_all.20.everyone_ref = bf16[8,100,512]{2,1,0:T(8,128)(2,1)S(1)} all-to-all(bf16[8,100,512]{2,1,0:T(8,128)(2,1)S(1)} %get-tuple-element.50), channel_id=1, replica_groups={{0,1,2,3,4,5,6,7},{15,14,13,12,11,10,9,8},{16,17,18,19,20,21,22,23},{31..., dimensions={0} | all-to-all | bytes 1638400 | tf_op jit(solution)/shard_map/all_to_all | solution.py:457
  31.6 0.0 copy-done
  31.6 0.0 copy-done.1
  31.6 2.7 %shard_map.105 = (bf16[16,9,32,128]{3,2,1,0:T(8,128)(2,1)S(1)}, bf16[16,9,32,128]{3,2,1,0:T(8,128)(2,1)S(1)}, bf16[512,1024]{1,0:T(8,128)(2,1)S(1)}) custom-call(bf16[8,100,512]{2,1,0:T(8,128)(2,1)S(1)} %all_to_all.20.everyone_ref, f32[100,512]{1,0:T(8,128)S(1)} %copy-done, s32[1,512]{1,0:T(1,128)S(1)} %bitcast.6, ...), custom_call_target="tpu_custom_call" | custom-call | flops 2000000000 | bytes 7784448 | tf_op jit(solution)/shard_map/pallas_call | solution.py:33
  34.3 0.1 collective-permute-start.2
  34.4 3.2 %shard_map.106 = (bf16[512,1024]{1,0:T(8,128)(2,1)}, bf16[128,1024]{1,0:T(8,128)(2,1)}, bf16[128,1024]{1,0:T(8,128)(2,1)}) custom-call(bf16[1024,1024]{1,0:T(8,128)(2,1)S(1)} %get-tuple-element.56.first_ref, bf16[512,1024]{1,0:T(8,128)(2,1)S(1)} %get-tuple-element.57.dpre_ref, bf16[512,1024]{1,0:T(8,128)(2,1)S(1)} %get-tuple-element.53.normed_ref, ...), custom_call_target="tpu_custom_call" | custom-call | flops 2000000000 | bytes 6819840 | tf_op jit(solution)/shard_map/pallas_call | solution.py:33
  37.6 0.0 collective-permute-done.2.got_ref
  37.6 0.4 shard_map.107
  38.0 24.0 %all_to_all.21.parts_ref = bf16[16,9,32,128]{3,2,1,0:T(8,128)(2,1)S(1)} all-to-all(bf16[16,9,32,128]{3,2,1,0:T(8,128)(2,1)S(1)} %shard_map.107), channel_id=1, replica_groups=mesh['z'=8,'xl'=2,'co'=2,'xh'=2,'y'=4] {'y','xh','xl'}, dimensions={0} | all-to-all | bytes 2359296 | tf_op jit(solution)/shard_map/all_to_all | solution.py:489
  62.0 0.0 copy-start.3
  62.0 0.0 copy-start.2
  62.0 0.8 shard_map.108
  62.8 9.7 %all-to-all-start.2 = ((bf16[8,2,32,128]{3,2,1,0:T(8,128)(2,1)}), bf16[8,2,32,128]{3,2,1,0:T(8,128)(2,1)S(1)}, u32[]{:S(2)}, u32[]{:S(2)}) async-start(bf16[8,2,32,128]{3,2,1,0:T(8,128)(2,1)} %shard_map.108), calls=%async_computation.2 | async-start | bytes 262144 | tf_op jit(solution)/shard_map/all_to_all | solution.py:510
  72.6 0.0 copy-done.3
  72.6 0.1 collective-permute-start.3
  72.7 0.0 copy-done.2
  72.7 3.5 %collective-permute-start.4 = (bf16[128,1024]{1,0:T(8,128)(2,1)S(1)}, bf16[128,1024]{1,0:T(8,128)(2,1)S(1)}, u32[]{:S(2)}, u32[]{:S(2)}) collective-permute-start(bf16[128,1024]{1,0:T(8,128)(2,1)S(1)} %copy-done.2), channel_id=1, source_target_pairs={{8,16},{24,32},{40,48},{56,64},{72,80},{88,96},{104,112},{120,128}... | collective-permute-start | bytes 786440 | tf_op jit(solution)/shard_map/ppermute | solution.py:492
  76.1 5.6 %all-to-all-done.2.parts_ref = bf16[8,2,32,128]{3,2,1,0:T(8,128)(2,1)S(1)} async-done(((bf16[8,2,32,128]{3,2,1,0:T(8,128)(2,1)}), bf16[8,2,32,128]{3,2,1,0:T(8,128)(2,1)S(1)}, u32[]{:S(2)}, u32[]{:S(2)}) %all-to-all-start.2) | async-done | bytes 131104 | tf_op jit(solution)/shard_map/all_to_all | solution.py:510
  81.7 0.8 shard_map.109
  82.5 3.4 %all-to-all-start.3 = ((bf16[8,2,32,128]{3,2,1,0:T(8,128)(2,1)}), bf16[8,2,32,128]{3,2,1,0:T(8,128)(2,1)S(1)}, u32[]{:S(2)}, u32[]{:S(2)}) async-start(bf16[8,2,32,128]{3,2,1,0:T(8,128)(2,1)} %shard_map.109), calls=%async_computation.3 | async-start | bytes 262144 | tf_op jit(solution)/shard_map/all_to_all | solution.py:514
  85.9 0.0 collective-permute-done.3.same_ref
  85.9 0.0 collective-permute-done.4.other_ref
  85.9 3.0 %shard_map.111 = bf16[512,1024]{1,0:T(8,128)(2,1)} custom-call(bf16[512,1024]{1,0:T(8,128)(2,1)} %get-tuple-element.66.low_hbm, bf16[768,512]{1,0:T(8,128)(2,1)} %get-tuple-element.67.turned_hbm, bf16[128,1024]{1,0:T(8,128)(2,1)S(1)} %collective-permute-done.3.same_ref, bf16[128,1024]{1,0:T(8,128)(2,1)S(1)} %collective-permute-done.4.other_ref), custom_call_target="tpu_custom_call" | custom-call | tf_op jit(solution)/shard_map/pallas_call | solution.py:33
  88.9 5.0 %all-to-all-done.3.parts_ref = bf16[8,2,32,128]{3,2,1,0:T(8,128)(2,1)S(1)} async-done(((bf16[8,2,32,128]{3,2,1,0:T(8,128)(2,1)}), bf16[8,2,32,128]{3,2,1,0:T(8,128)(2,1)S(1)}, u32[]{:S(2)}, u32[]{:S(2)}) %all-to-all-start.3) | async-done | bytes 131104 | tf_op jit(solution)/shard_map/all_to_all | solution.py:514
  93.9 0.7 shard_map.110
Async XLA Ops:
  1.7 4.4 %collective-permute-start.1 = (bf16[128,1024]{1,0:T(8,128)(2,1)S(1)}, bf16[128,1024]{1,0:T(8,128)(2,1)S(1)}, u32[]{:S(2)}, u32[]{:S(2)}) collective-permute-start(bf16[128,1024]{1,0:T(8,128)(2,1)S(1)} %get-tuple-element.39), channel_id=1, source_target_pairs={{0,8},{8,0},{1,9},{9,1},{2,10},{10,2},{3,11},{11,3},{4,12},{12,4},... | collective-permute-start | bytes 786440 | tf_op jit(solution)/shard_map/ppermute | solution.py:417
  1.8 11.1 %collective-permute-start = (bf16[128,1024]{1,0:T(8,128)(2,1)S(1)}, bf16[128,1024]{1,0:T(8,128)(2,1)S(1)}, u32[]{:S(2)}, u32[]{:S(2)}) collective-permute-start(bf16[128,1024]{1,0:T(8,128)(2,1)S(1)} %get-tuple-element.38), channel_id=1, source_target_pairs={{8,16},{24,32},{40,48},{56,64},{72,80},{88,96},{104,112},{120,128}... | collective-permute-start | bytes 786440 | tf_op jit(solution)/shard_map/ppermute | solution.py:418
  14.2 17.4 %copy-start = (f32[100,512]{1,0:T(8,128)S(1)}, f32[100,512]{1,0:T(8,128)}, u32[]{:S(2)}) copy-start(f32[100,512]{1,0:T(8,128)} %target_ref.1) | copy-start | bytes 614404
  14.2 17.4 %copy-start.1 = (s32[512]{0:T(512)S(1)}, s32[512]{0:T(512)}, u32[]{:S(2)}) copy-start(s32[512]{0:T(512)} %param.12) | copy-start | bytes 6148
  34.3 3.3 %collective-permute-start.2 = (bf16[16,9,32,128]{3,2,1,0:T(8,128)(2,1)S(1)}, bf16[16,9,32,128]{3,2,1,0:T(8,128)(2,1)S(1)}, u32[]{:S(2)}, u32[]{:S(2)}) collective-permute-start(bf16[16,9,32,128]{3,2,1,0:T(8,128)(2,1)S(1)} %get-tuple-element.55), channel_id=1, source_target_pairs={{0,8},{8,0},{1,9},{9,1},{2,10},{10,2},{3,11},{11,3},{4,12},{12,4},... | collective-permute-start | bytes 3538952 | tf_op jit(solution)/shard_map/ppermute | solution.py:466
  62.0 10.5 %copy-start.3 = (bf16[128,1024]{1,0:T(8,128)(2,1)S(1)}, bf16[128,1024]{1,0:T(8,128)(2,1)}, u32[]{:S(2)}) copy-start(bf16[128,1024]{1,0:T(8,128)(2,1)} %get-tuple-element.68) | copy-start | bytes 786436
  62.0 10.7 %copy-start.2 = (bf16[128,1024]{1,0:T(8,128)(2,1)S(1)}, bf16[128,1024]{1,0:T(8,128)(2,1)}, u32[]{:S(2)}) copy-start(bf16[128,1024]{1,0:T(8,128)(2,1)} %get-tuple-element.69) | copy-start | bytes 786436
  62.8 18.9 %all-to-all-start.2 = ((bf16[8,2,32,128]{3,2,1,0:T(8,128)(2,1)}), bf16[8,2,32,128]{3,2,1,0:T(8,128)(2,1)S(1)}, u32[]{:S(2)}, u32[]{:S(2)}) async-start(bf16[8,2,32,128]{3,2,1,0:T(8,128)(2,1)} %shard_map.108), calls=%async_computation.2 | async-start | bytes 262144 | tf_op jit(solution)/shard_map/all_to_all | solution.py:510
  72.6 13.3 %collective-permute-start.3 = (bf16[128,1024]{1,0:T(8,128)(2,1)S(1)}, bf16[128,1024]{1,0:T(8,128)(2,1)S(1)}, u32[]{:S(2)}, u32[]{:S(2)}) collective-permute-start(bf16[128,1024]{1,0:T(8,128)(2,1)S(1)} %copy-done.3), channel_id=1, source_target_pairs={{0,8},{8,0},{1,9},{9,1},{2,10},{10,2},{3,11},{11,3},{4,12},{12,4},... | collective-permute-start | bytes 786440 | tf_op jit(solution)/shard_map/ppermute | solution.py:491
  72.7 13.2 %collective-permute-start.4 = (bf16[128,1024]{1,0:T(8,128)(2,1)S(1)}, bf16[128,1024]{1,0:T(8,128)(2,1)S(1)}, u32[]{:S(2)}, u32[]{:S(2)}) collective-permute-start(bf16[128,1024]{1,0:T(8,128)(2,1)S(1)} %copy-done.2), channel_id=1, source_target_pairs={{8,16},{24,32},{40,48},{56,64},{72,80},{88,96},{104,112},{120,128}... | collective-permute-start | bytes 786440 | tf_op jit(solution)/shard_map/ppermute | solution.py:492
  82.5 11.4 %all-to-all-start.3 = ((bf16[8,2,32,128]{3,2,1,0:T(8,128)(2,1)}), bf16[8,2,32,128]{3,2,1,0:T(8,128)(2,1)S(1)}, u32[]{:S(2)}, u32[]{:S(2)}) async-start(bf16[8,2,32,128]{3,2,1,0:T(8,128)(2,1)} %shard_map.109), calls=%async_computation.3 | async-start | bytes 262144 | tf_op jit(solution)/shard_map/all_to_all | solution.py:514

commit v5 on v4

--- a/solution.py
+++ b/solution.py
@@ -330,11 +330,11 @@
         for k in range(1, parts_ref.shape[0]):
             total = total + parts_ref[k, j].astype(F32)
         if j < blocks:
-            out_ref[j, 0] = total.astype(BF16)
+            out_ref[member_place(j, blocks), 0] = total.astype(BF16)
     loss = read_loss(total, fields)
     for j in range(blocks):
         tile = jnp.where(me == j, total, 0.0)
-        out_ref[j, 1] = split_loss(tile, loss, fields).astype(BF16)
+        out_ref[member_place(j, blocks), 1] = split_loss(tile, loss, fields).astype(BF16)
 
 
 def fold_kernel(fields, parts_ref, out_ref):
@@ -388,6 +388,14 @@
     for band in range(bands):
         group = [band * members + m for m in range(members)]
         groups.append(group if band % 2 == 0 else group[::-1])
+    return groups
+
+
+def height_groups(bands, members):
+    groups = []
+    for i in range(4 * members):
+        group = [(z * 4 + i // members) * members + i % members for z in range(bands // 4)]
+        groups.append(group if i // members % 2 == 0 else group[::-1])
     return groups
 
 
@@ -507,7 +515,8 @@
     (planed,) = call(
         functools.partial(plane_kernel, fields), [shape(message, BF16)], [parts], 10**6, 8
     )
-    parts = lax.all_to_all(planed, "z", 0, 0)
+    heights = height_groups(bands, members)
+    parts = lax.all_to_all(planed, BAND + MEM, 0, 0, axis_index_groups=heights)
     (folded,) = call(
         functools.partial(fold_kernel, fields), [shape(message, BF16)], [parts], 10**6, 8
     )

time: 95.1 us -> 95.1 us (level)
  no operation moved by 1% of the time
where the time goes in v5:
time: 95.1 us; the launch traced here: 94.6 us
  blocking collectives  41.4 us (44%)
  starting transfers between devices  21.1 us (22%)
  Pallas kernels  18 us (19%)
  waiting for transfers between devices  13.2 us (14%)
    all_to_all x1, blocking collectives, per_device(): parts = lax.all_to_all(mine, PLANE, 0, 0)  24 us
    pallas_call x10, Pallas kernels, call(): pl.pallas_call(kernel, out_shape=[pltpu.HBM(o.shape, o.dtype) if i in sto...  18 us
    all_to_all x1, blocking collectives, per_device(): lax.all_to_all(copies, BAND + MEM, 0, 0, axis_index_groups=groups)  17.4 us
    all_to_all x1, starting transfers between devices, per_device(): parts = lax.all_to_all(planed, BAND + MEM, 0, 0, axis_index_groups=heights)  9.71 us
    ppermute x2, starting transfers between devices, per_device(): other = lax.ppermute(rim_other, BAND, chips)  7.72 us
    all_to_all x1, waiting for transfers between devices, per_device(): parts = lax.all_to_all(planed, BAND + MEM, 0, 0, axis_index_groups=heights)  5.61 us
    all_to_all x1, waiting for transfers between devices, per_device(): parts = lax.all_to_all(folded, BAND + MEM, 0, 0, axis_index_groups=groups)  4.95 us
    all_to_all x1, starting transfers between devices, per_device(): parts = lax.all_to_all(folded, BAND + MEM, 0, 0, axis_index_groups=groups)  3.37 us
  transfers between devices with their start and end apart: 7, of which 3 were waited for; matrix products, arithmetic and copies ran while one was open for 0% of the time, Pallas kernels for 12%

profile of v5, /device:TPU:2, one launch (start us, length us, event | category | flops | bytes accessed | tf_op | source)
XLA Modules:
  0.0 94.6 jit_solution(18247253294927066624)
XLA Ops:
  0.6 1.1 %shard_map.102 = (bf16[128,1024]{1,0:T(8,128)(2,1)S(1)}, bf16[128,1024]{1,0:T(8,128)(2,1)S(1)}) custom-call(bf16[512,1024]{1,0:T(8,128)(2,1)} %bitcast.7), custom_call_target="tpu_custom_call" | custom-call | tf_op jit(solution)/shard_map/pallas_call | solution.py:33
  1.7 0.1 collective-permute-start.1
  1.8 4.3 %collective-permute-start = (bf16[128,1024]{1,0:T(8,128)(2,1)S(1)}, bf16[128,1024]{1,0:T(8,128)(2,1)S(1)}, u32[]{:S(2)}, u32[]{:S(2)}) collective-permute-start(bf16[128,1024]{1,0:T(8,128)(2,1)S(1)} %get-tuple-element.38), channel_id=1, source_target_pairs={{8,16},{24,32},{40,48},{56,64},{72,80},{88,96},{104,112},{120,128}... | collective-permute-start | bytes 786440 | tf_op jit(solution)/shard_map/ppermute | solution.py:426
  6.1 0.0 collective-permute-done.1.same_ref
  6.1 4.2 %shard_map.103 = (bf16[100,384]{1,0:T(8,128)(2,1)S(1)}, bf16[384,1024]{1,0:T(8,128)(2,1)S(1)}, bf16[384,1024]{1,0:T(8,128)(2,1)S(1)}, bf16[384,1024]{1,0:T(8,128...) custom-call(bf16[128,1024]{1,0:T(8,128)(2,1)S(1)} %collective-permut, ...), custom_call_target="tpu_custom_call" | custom-call | flops 1000000000 | bytes 12794880 | tf_op jit(solution)/shard_map/pallas_call | solution.py:33
  10.3 2.6 %collective-permute-done.other_ref = bf16[128,1024]{1,0:T(8,128)(2,1)S(1)} collective-permute-done((bf16[128,1024]{1,0:T(8,128)(2,1)S(1)}, bf16[128,1024]{1,0:T(8,128)(2,1)S(1)}, u32[]{:S(2)}, u32[]{:S(2)}) %collective-permute-start) | collective-permute-done | bytes 262176 | tf_op jit(solution)/shard_map/ppermute | solution.py:426
  12.9 1.2 %shard_map.104 = (bf16[8,100,512]{2,1,0:T(8,128)(2,1)S(1)}, bf16[512,1024]{1,0:T(8,128)(2,1)S(1)}, bf16[512,1024]{1,0:T(8,128)(2,1)S(1)}, bf16[512,1024]{1,0:T(8,128)(2,1)S(1)}, f32[512,128]{1,0:T(8,128)S(1)}) custom-call(bf16[128,1024]{1,0:T(8,128)(2,1)S(1)} %collective-permute-done.other_ref, f32[128,1024]{1,0:T(8,128)S(1)} %get-tuple-element.40.partial_ref, ...), custom_call_target="tpu_custom_call" | custom-call | flops 1000000000 | bytes 9985024 | tf_op jit(solution)/shard_map/pallas_call | solution.py:33
  14.2 0.0 copy-start
  14.2 0.0 copy-start.1
  14.2 17.4 %all_to_all.20.everyone_ref = bf16[8,100,512]{2,1,0:T(8,128)(2,1)S(1)} all-to-all(bf16[8,100,512]{2,1,0:T(8,128)(2,1)S(1)} %get-tuple-element.50), channel_id=1, replica_groups={{0,1,2,3,4,5,6,7},{15,14,13,12,11,10,9,8},{16,17,18,19,20,21,22,23},{31..., dimensions={0} | all-to-all | bytes 1638400 | tf_op jit(solution)/shard_map/all_to_all | solution.py:465
  31.6 0.0 copy-done
  31.6 0.0 copy-done.1
  31.6 2.7 %shard_map.105 = (bf16[16,9,32,128]{3,2,1,0:T(8,128)(2,1)S(1)}, bf16[16,9,32,128]{3,2,1,0:T(8,128)(2,1)S(1)}, bf16[512,1024]{1,0:T(8,128)(2,1)S(1)}) custom-call(bf16[8,100,512]{2,1,0:T(8,128)(2,1)S(1)} %all_to_all.20.everyone_ref, f32[100,512]{1,0:T(8,128)S(1)} %copy-done, s32[1,512]{1,0:T(1,128)S(1)} %bitcast.6, ...), custom_call_target="tpu_custom_call" | custom-call | flops 2000000000 | bytes 7784448 | tf_op jit(solution)/shard_map/pallas_call | solution.py:33
  34.3 0.1 collective-permute-start.2
  34.4 3.2 %shard_map.106 = (bf16[512,1024]{1,0:T(8,128)(2,1)}, bf16[128,1024]{1,0:T(8,128)(2,1)}, bf16[128,1024]{1,0:T(8,128)(2,1)}) custom-call(bf16[1024,1024]{1,0:T(8,128)(2,1)S(1)} %get-tuple-element.56.first_ref, bf16[512,1024]{1,0:T(8,128)(2,1)S(1)} %get-tuple-element.57.dpre_ref, bf16[512,1024]{1,0:T(8,128)(2,1)S(1)} %get-tuple-element.53.normed_ref, ...), custom_call_target="tpu_custom_call" | custom-call | flops 2000000000 | bytes 6819840 | tf_op jit(solution)/shard_map/pallas_call | solution.py:33
  37.6 0.0 collective-permute-done.2.got_ref
  37.6 0.4 shard_map.107
  38.0 24.0 %all_to_all.21.parts_ref = bf16[16,9,32,128]{3,2,1,0:T(8,128)(2,1)S(1)} all-to-all(bf16[16,9,32,128]{3,2,1,0:T(8,128)(2,1)S(1)} %shard_map.107), channel_id=1, replica_groups=mesh['z'=8,'xl'=2,'co'=2,'xh'=2,'y'=4] {'y','xh','xl'}, dimensions={0} | all-to-all | bytes 2359296 | tf_op jit(solution)/shard_map/all_to_all | solution.py:497
  62.0 0.0 copy-start.3
  62.0 0.0 copy-start.2
  62.0 0.8 shard_map.108
  62.8 9.7 %all-to-all-start.2 = ((bf16[8,2,32,128]{3,2,1,0:T(8,128)(2,1)}), bf16[8,2,32,128]{3,2,1,0:T(8,128)(2,1)S(1)}, u32[]{:S(2)}, u32[]{:S(2)}) async-start(bf16[8,2,32,128]{3,2,1,0:T(8,128)(2,1)} %shard_map.108), calls=%async_computation.2 | async-start | bytes 262144 | tf_op jit(solution)/shard_map/all_to_all | solution.py:519
  72.6 0.0 copy-done.3
  72.6 0.1 collective-permute-start.3
  72.7 0.0 copy-done.2
  72.7 3.5 %collective-permute-start.4 = (bf16[128,1024]{1,0:T(8,128)(2,1)S(1)}, bf16[128,1024]{1,0:T(8,128)(2,1)S(1)}, u32[]{:S(2)}, u32[]{:S(2)}) collective-permute-start(bf16[128,1024]{1,0:T(8,128)(2,1)S(1)} %copy-done.2), channel_id=1, source_target_pairs={{8,16},{24,32},{40,48},{56,64},{72,80},{88,96},{104,112},{120,128}... | collective-permute-start | bytes 786440 | tf_op jit(solution)/shard_map/ppermute | solution.py:500
  76.1 5.6 %all-to-all-done.2.parts_ref = bf16[8,2,32,128]{3,2,1,0:T(8,128)(2,1)S(1)} async-done(((bf16[8,2,32,128]{3,2,1,0:T(8,128)(2,1)}), bf16[8,2,32,128]{3,2,1,0:T(8,128)(2,1)S(1)}, u32[]{:S(2)}, u32[]{:S(2)}) %all-to-all-start.2) | async-done | bytes 131104 | tf_op jit(solution)/shard_map/all_to_all | solution.py:519
  81.7 0.8 shard_map.109
  82.5 3.4 %all-to-all-start.3 = ((bf16[8,2,32,128]{3,2,1,0:T(8,128)(2,1)}), bf16[8,2,32,128]{3,2,1,0:T(8,128)(2,1)S(1)}, u32[]{:S(2)}, u32[]{:S(2)}) async-start(bf16[8,2,32,128]{3,2,1,0:T(8,128)(2,1)} %shard_map.109), calls=%async_computation.3 | async-start | bytes 262144 | tf_op jit(solution)/shard_map/all_to_all | solution.py:523
  85.9 0.0 collective-permute-done.3.same_ref
  85.9 0.0 collective-permute-done.4.other_ref
  85.9 3.0 %shard_map.111 = bf16[512,1024]{1,0:T(8,128)(2,1)} custom-call(bf16[512,1024]{1,0:T(8,128)(2,1)} %get-tuple-element.66.low_hbm, bf16[768,512]{1,0:T(8,128)(2,1)} %get-tuple-element.67.turned_hbm, bf16[128,1024]{1,0:T(8,128)(2,1)S(1)} %collective-permute-done.3.same_ref, bf16[128,1024]{1,0:T(8,128)(2,1)S(1)} %collective-permute-done.4.other_ref), custom_call_target="tpu_custom_call" | custom-call | tf_op jit(solution)/shard_map/pallas_call | solution.py:33
  88.9 5.0 %all-to-all-done.3.parts_ref = bf16[8,2,32,128]{3,2,1,0:T(8,128)(2,1)S(1)} async-done(((bf16[8,2,32,128]{3,2,1,0:T(8,128)(2,1)}), bf16[8,2,32,128]{3,2,1,0:T(8,128)(2,1)S(1)}, u32[]{:S(2)}, u32[]{:S(2)}) %all-to-all-start.3) | async-done | bytes 131104 | tf_op jit(solution)/shard_map/all_to_all | solution.py:523
  93.9 0.7 shard_map.110
Async XLA Ops:
  1.7 4.4 %collective-permute-start.1 = (bf16[128,1024]{1,0:T(8,128)(2,1)S(1)}, bf16[128,1024]{1,0:T(8,128)(2,1)S(1)}, u32[]{:S(2)}, u32[]{:S(2)}) collective-permute-start(bf16[128,1024]{1,0:T(8,128)(2,1)S(1)} %get-tuple-element.39), channel_id=1, source_target_pairs={{0,8},{8,0},{1,9},{9,1},{2,10},{10,2},{3,11},{11,3},{4,12},{12,4},... | collective-permute-start | bytes 786440 | tf_op jit(solution)/shard_map/ppermute | solution.py:425
  1.8 11.1 %collective-permute-start = (bf16[128,1024]{1,0:T(8,128)(2,1)S(1)}, bf16[128,1024]{1,0:T(8,128)(2,1)S(1)}, u32[]{:S(2)}, u32[]{:S(2)}) collective-permute-start(bf16[128,1024]{1,0:T(8,128)(2,1)S(1)} %get-tuple-element.38), channel_id=1, source_target_pairs={{8,16},{24,32},{40,48},{56,64},{72,80},{88,96},{104,112},{120,128}... | collective-permute-start | bytes 786440 | tf_op jit(solution)/shard_map/ppermute | solution.py:426
  14.2 17.4 %copy-start = (f32[100,512]{1,0:T(8,128)S(1)}, f32[100,512]{1,0:T(8,128)}, u32[]{:S(2)}) copy-start(f32[100,512]{1,0:T(8,128)} %target_ref.1) | copy-start | bytes 614404
  14.2 17.4 %copy-start.1 = (s32[512]{0:T(512)S(1)}, s32[512]{0:T(512)}, u32[]{:S(2)}) copy-start(s32[512]{0:T(512)} %param.12) | copy-start | bytes 6148
  34.3 3.3 %collective-permute-start.2 = (bf16[16,9,32,128]{3,2,1,0:T(8,128)(2,1)S(1)}, bf16[16,9,32,128]{3,2,1,0:T(8,128)(2,1)S(1)}, u32[]{:S(2)}, u32[]{:S(2)}) collective-permute-start(bf16[16,9,32,128]{3,2,1,0:T(8,128)(2,1)S(1)} %get-tuple-element.55), channel_id=1, source_target_pairs={{0,8},{8,0},{1,9},{9,1},{2,10},{10,2},{3,11},{11,3},{4,12},{12,4},... | collective-permute-start | bytes 3538952 | tf_op jit(solution)/shard_map/ppermute | solution.py:474
  62.0 10.5 %copy-start.3 = (bf16[128,1024]{1,0:T(8,128)(2,1)S(1)}, bf16[128,1024]{1,0:T(8,128)(2,1)}, u32[]{:S(2)}) copy-start(bf16[128,1024]{1,0:T(8,128)(2,1)} %get-tuple-element.68) | copy-start | bytes 786436
  62.0 10.7 %copy-start.2 = (bf16[128,1024]{1,0:T(8,128)(2,1)S(1)}, bf16[128,1024]{1,0:T(8,128)(2,1)}, u32[]{:S(2)}) copy-start(bf16[128,1024]{1,0:T(8,128)(2,1)} %get-tuple-element.69) | copy-start | bytes 786436
  62.8 18.9 %all-to-all-start.2 = ((bf16[8,2,32,128]{3,2,1,0:T(8,128)(2,1)}), bf16[8,2,32,128]{3,2,1,0:T(8,128)(2,1)S(1)}, u32[]{:S(2)}, u32[]{:S(2)}) async-start(bf16[8,2,32,128]{3,2,1,0:T(8,128)(2,1)} %shard_map.108), calls=%async_computation.2 | async-start | bytes 262144 | tf_op jit(solution)/shard_map/all_to_all | solution.py:519
  72.6 13.3 %collective-permute-start.3 = (bf16[128,1024]{1,0:T(8,128)(2,1)S(1)}, bf16[128,1024]{1,0:T(8,128)(2,1)S(1)}, u32[]{:S(2)}, u32[]{:S(2)}) collective-permute-start(bf16[128,1024]{1,0:T(8,128)(2,1)S(1)} %copy-done.3), channel_id=1, source_target_pairs={{0,8},{8,0},{1,9},{9,1},{2,10},{10,2},{3,11},{11,3},{4,12},{12,4},... | collective-permute-start | bytes 786440 | tf_op jit(solution)/shard_map/ppermute | solution.py:499
  72.7 13.2 %collective-permute-start.4 = (bf16[128,1024]{1,0:T(8,128)(2,1)S(1)}, bf16[128,1024]{1,0:T(8,128)(2,1)S(1)}, u32[]{:S(2)}, u32[]{:S(2)}) collective-permute-start(bf16[128,1024]{1,0:T(8,128)(2,1)S(1)} %copy-done.2), channel_id=1, source_target_pairs={{8,16},{24,32},{40,48},{56,64},{72,80},{88,96},{104,112},{120,128}... | collective-permute-start | bytes 786440 | tf_op jit(solution)/shard_map/ppermute | solution.py:500
  82.5 11.4 %all-to-all-start.3 = ((bf16[8,2,32,128]{3,2,1,0:T(8,128)(2,1)}), bf16[8,2,32,128]{3,2,1,0:T(8,128)(2,1)S(1)}, u32[]{:S(2)}, u32[]{:S(2)}) async-start(bf16[8,2,32,128]{3,2,1,0:T(8,128)(2,1)} %shard_map.109), calls=%async_computation.3 | async-start | bytes 262144 | tf_op jit(solution)/shard_map/all_to_all | solution.py:523

commit v6 on v5

--- a/solution.py
+++ b/solution.py
@@ -278,7 +278,10 @@
             [
                 (rim_ref.at[0], same_hbm),
                 (rim_ref.at[1], other_hbm),
-                (low_ref, low_hbm),
+                *(
+                    (low_ref.at[i : i + HALO], low_hbm.at[i : i + HALO])
+                    for i in range(0, cells, HALO)
+                ),
             ]
         )
     ]
@@ -302,13 +305,15 @@
             along[own] * (1.0 / width)
         )
         low_ref[own, :] = (inv_ref[own, :1] * (total_ref[own, :] - inner)).astype(BF16)
-    saves[2].start()
-    up = dot(turned_ref[:HALO, :HALO], low_ref[:HALO, :]) * (1.0 / NEIGH)
-    rim_ref[1 - core] = up.astype(BF16)
-    down = dot(turned_ref[cells + HALO :, cells - HALO :], low_ref[cells - HALO :, :]) * (1.0 / NEIGH)
-    rim_ref[core] = down.astype(BF16)
-    saves[0].start()
-    saves[1].start()
+        saves[2 + block].start()
+        if block == 0:
+            up = dot(turned_ref[:HALO, :HALO], low_ref[own, :]) * (1.0 / NEIGH)
+            rim_ref[1 - core] = up.astype(BF16)
+        if block == blocks - 1:
+            down = dot(turned_ref[cells + HALO :, own], low_ref[own, :]) * (1.0 / NEIGH)
+            rim_ref[core] = down.astype(BF16)
+            saves[0].start()
+            saves[1].start()
     for save in saves:
         save.wait()
 
@@ -486,7 +491,7 @@
             pltpu.VMEM((cells, width), F32),
             pltpu.VMEM((cells, width), BF16),
             pltpu.VMEM((2, HALO, width), BF16),
-            pltpu.SemaphoreType.DMA((3,)),
+            pltpu.SemaphoreType.DMA((2 + cells // HALO,)),
         ],
         stored=(0, 1, 2),
     )

time: 95.1 us -> 95.1 us (level)
  no operation moved by 1% of the time
where the time goes in v6:
time: 95.1 us; the launch traced here: 94.5 us
  blocking collectives  41.4 us (44%)
  starting transfers between devices  21.1 us (22%)
  Pallas kernels  18 us (19%)
  waiting for transfers between devices  13.2 us (14%)
    all_to_all x1, blocking collectives, per_device(): parts = lax.all_to_all(mine, PLANE, 0, 0)  24 us
    pallas_call x10, Pallas kernels, call(): pl.pallas_call(kernel, out_shape=[pltpu.HBM(o.shape, o.dtype) if i in sto...  18 us
    all_to_all x1, blocking collectives, per_device(): lax.all_to_all(copies, BAND + MEM, 0, 0, axis_index_groups=groups)  17.4 us
    all_to_all x1, starting transfers between devices, per_device(): parts = lax.all_to_all(planed, BAND + MEM, 0, 0, axis_index_groups=heights)  9.74 us
    ppermute x2, starting transfers between devices, per_device(): other = lax.ppermute(rim_other, BAND, chips)  7.72 us
    all_to_all x1, waiting for transfers between devices, per_device(): parts = lax.all_to_all(planed, BAND + MEM, 0, 0, axis_index_groups=heights)  5.6 us
    all_to_all x1, waiting for transfers between devices, per_device(): parts = lax.all_to_all(folded, BAND + MEM, 0, 0, axis_index_groups=groups)  4.95 us
    all_to_all x1, starting transfers between devices, per_device(): parts = lax.all_to_all(folded, BAND + MEM, 0, 0, axis_index_groups=groups)  3.37 us
  transfers between devices with their start and end apart: 7, of which 3 were waited for; matrix products, arithmetic and copies ran while one was open for 0% of the time, Pallas kernels for 12%

profile of v6, /device:TPU:2, one launch (start us, length us, event | category | flops | bytes accessed | tf_op | source)
XLA Modules:
  0.0 94.5 jit_solution(1117609723813994389)
XLA Ops:
  0.6 1.1 %shard_map.102 = (bf16[128,1024]{1,0:T(8,128)(2,1)S(1)}, bf16[128,1024]{1,0:T(8,128)(2,1)S(1)}) custom-call(bf16[512,1024]{1,0:T(8,128)(2,1)} %bitcast.7), custom_call_target="tpu_custom_call" | custom-call | tf_op jit(solution)/shard_map/pallas_call | solution.py:33
  1.7 0.1 collective-permute-start.1
  1.8 4.3 %collective-permute-start = (bf16[128,1024]{1,0:T(8,128)(2,1)S(1)}, bf16[128,1024]{1,0:T(8,128)(2,1)S(1)}, u32[]{:S(2)}, u32[]{:S(2)}) collective-permute-start(bf16[128,1024]{1,0:T(8,128)(2,1)S(1)} %get-tuple-element.38), channel_id=1, source_target_pairs={{8,16},{24,32},{40,48},{56,64},{72,80},{88,96},{104,112},{120,128}... | collective-permute-start | bytes 786440 | tf_op jit(solution)/shard_map/ppermute | solution.py:431
  6.1 0.0 collective-permute-done.1.same_ref
  6.1 4.2 %shard_map.103 = (bf16[100,384]{1,0:T(8,128)(2,1)S(1)}, bf16[384,1024]{1,0:T(8,128)(2,1)S(1)}, bf16[384,1024]{1,0:T(8,128)(2,1)S(1)}, bf16[384,1024]{1,0:T(8,128...) custom-call(bf16[128,1024]{1,0:T(8,128)(2,1)S(1)} %collective-permut, ...), custom_call_target="tpu_custom_call" | custom-call | flops 1000000000 | bytes 12794880 | tf_op jit(solution)/shard_map/pallas_call | solution.py:33
  10.3 2.6 %collective-permute-done.other_ref = bf16[128,1024]{1,0:T(8,128)(2,1)S(1)} collective-permute-done((bf16[128,1024]{1,0:T(8,128)(2,1)S(1)}, bf16[128,1024]{1,0:T(8,128)(2,1)S(1)}, u32[]{:S(2)}, u32[]{:S(2)}) %collective-permute-start) | collective-permute-done | bytes 262176 | tf_op jit(solution)/shard_map/ppermute | solution.py:431
  12.9 1.2 %shard_map.104 = (bf16[8,100,512]{2,1,0:T(8,128)(2,1)S(1)}, bf16[512,1024]{1,0:T(8,128)(2,1)S(1)}, bf16[512,1024]{1,0:T(8,128)(2,1)S(1)}, bf16[512,1024]{1,0:T(8,128)(2,1)S(1)}, f32[512,128]{1,0:T(8,128)S(1)}) custom-call(bf16[128,1024]{1,0:T(8,128)(2,1)S(1)} %collective-permute-done.other_ref, f32[128,1024]{1,0:T(8,128)S(1)} %get-tuple-element.40.partial_ref, ...), custom_call_target="tpu_custom_call" | custom-call | flops 1000000000 | bytes 9985024 | tf_op jit(solution)/shard_map/pallas_call | solution.py:33
  14.2 0.0 copy-start
  14.2 0.0 copy-start.1
  14.2 17.4 %all_to_all.20.everyone_ref = bf16[8,100,512]{2,1,0:T(8,128)(2,1)S(1)} all-to-all(bf16[8,100,512]{2,1,0:T(8,128)(2,1)S(1)} %get-tuple-element.50), channel_id=1, replica_groups={{0,1,2,3,4,5,6,7},{15,14,13,12,11,10,9,8},{16,17,18,19,20,21,22,23},{31..., dimensions={0} | all-to-all | bytes 1638400 | tf_op jit(solution)/shard_map/all_to_all | solution.py:470
  31.6 0.0 copy-done
  31.6 0.0 copy-done.1
  31.6 2.7 %shard_map.105 = (bf16[16,9,32,128]{3,2,1,0:T(8,128)(2,1)S(1)}, bf16[16,9,32,128]{3,2,1,0:T(8,128)(2,1)S(1)}, bf16[512,1024]{1,0:T(8,128)(2,1)S(1)}) custom-call(bf16[8,100,512]{2,1,0:T(8,128)(2,1)S(1)} %all_to_all.20.everyone_ref, f32[100,512]{1,0:T(8,128)S(1)} %copy-done, s32[1,512]{1,0:T(1,128)S(1)} %bitcast.6, ...), custom_call_target="tpu_custom_call" | custom-call | flops 2000000000 | bytes 7784448 | tf_op jit(solution)/shard_map/pallas_call | solution.py:33
  34.3 0.1 collective-permute-start.2
  34.4 3.1 %shard_map.106 = (bf16[512,1024]{1,0:T(8,128)(2,1)}, bf16[128,1024]{1,0:T(8,128)(2,1)}, bf16[128,1024]{1,0:T(8,128)(2,1)}) custom-call(bf16[1024,1024]{1,0:T(8,128)(2,1)S(1)} %get-tuple-element.56.first_ref, bf16[512,1024]{1,0:T(8,128)(2,1)S(1)} %get-tuple-element.57.dpre_ref, bf16[512,1024]{1,0:T(8,128)(2,1)S(1)} %get-tuple-element.53.normed_ref, ...), custom_call_target="tpu_custom_call" | custom-call | flops 2000000000 | bytes 6819840 | tf_op jit(solution)/shard_map/pallas_call | solution.py:33
  37.5 0.0 collective-permute-done.2.got_ref
  37.5 0.4 shard_map.107
  37.9 24.0 %all_to_all.21.parts_ref = bf16[16,9,32,128]{3,2,1,0:T(8,128)(2,1)S(1)} all-to-all(bf16[16,9,32,128]{3,2,1,0:T(8,128)(2,1)S(1)} %shard_map.107), channel_id=1, replica_groups=mesh['z'=8,'xl'=2,'co'=2,'xh'=2,'y'=4] {'y','xh','xl'}, dimensions={0} | all-to-all | bytes 2359296 | tf_op jit(solution)/shard_map/all_to_all | solution.py:502
  61.9 0.0 copy-start.3
  61.9 0.0 copy-start.2
  61.9 0.8 shard_map.108
  62.8 9.7 %all-to-all-start.2 = ((bf16[8,2,32,128]{3,2,1,0:T(8,128)(2,1)}), bf16[8,2,32,128]{3,2,1,0:T(8,128)(2,1)S(1)}, u32[]{:S(2)}, u32[]{:S(2)}) async-start(bf16[8,2,32,128]{3,2,1,0:T(8,128)(2,1)} %shard_map.108), calls=%async_computation.2 | async-start | bytes 262144 | tf_op jit(solution)/shard_map/all_to_all | solution.py:524
  72.5 0.0 copy-done.3
  72.5 0.1 collective-permute-start.3
  72.6 0.0 copy-done.2
  72.6 3.5 %collective-permute-start.4 = (bf16[128,1024]{1,0:T(8,128)(2,1)S(1)}, bf16[128,1024]{1,0:T(8,128)(2,1)S(1)}, u32[]{:S(2)}, u32[]{:S(2)}) collective-permute-start(bf16[128,1024]{1,0:T(8,128)(2,1)S(1)} %copy-done.2), channel_id=1, source_target_pairs={{8,16},{24,32},{40,48},{56,64},{72,80},{88,96},{104,112},{120,128}... | collective-permute-start | bytes 786440 | tf_op jit(solution)/shard_map/ppermute | solution.py:505
  76.1 5.6 %all-to-all-done.2.parts_ref = bf16[8,2,32,128]{3,2,1,0:T(8,128)(2,1)S(1)} async-done(((bf16[8,2,32,128]{3,2,1,0:T(8,128)(2,1)}), bf16[8,2,32,128]{3,2,1,0:T(8,128)(2,1)S(1)}, u32[]{:S(2)}, u32[]{:S(2)}) %all-to-all-start.2) | async-done | bytes 131104 | tf_op jit(solution)/shard_map/all_to_all | solution.py:524
  81.7 0.8 shard_map.109
  82.4 3.4 %all-to-all-start.3 = ((bf16[8,2,32,128]{3,2,1,0:T(8,128)(2,1)}), bf16[8,2,32,128]{3,2,1,0:T(8,128)(2,1)S(1)}, u32[]{:S(2)}, u32[]{:S(2)}) async-start(bf16[8,2,32,128]{3,2,1,0:T(8,128)(2,1)} %shard_map.109), calls=%async_computation.3 | async-start | bytes 262144 | tf_op jit(solution)/shard_map/all_to_all | solution.py:528
  85.8 0.0 collective-permute-done.3.same_ref
  85.8 0.0 collective-permute-done.4.other_ref
  85.8 3.0 %shard_map.111 = bf16[512,1024]{1,0:T(8,128)(2,1)} custom-call(bf16[512,1024]{1,0:T(8,128)(2,1)} %get-tuple-element.66.low_hbm, bf16[768,512]{1,0:T(8,128)(2,1)} %get-tuple-element.67.turned_hbm, bf16[128,1024]{1,0:T(8,128)(2,1)S(1)} %collective-permute-done.3.same_ref, bf16[128,1024]{1,0:T(8,128)(2,1)S(1)} %collective-permute-done.4.other_ref), custom_call_target="tpu_custom_call" | custom-call | tf_op jit(solution)/shard_map/pallas_call | solution.py:33
  88.9 4.9 %all-to-all-done.3.parts_ref = bf16[8,2,32,128]{3,2,1,0:T(8,128)(2,1)S(1)} async-done(((bf16[8,2,32,128]{3,2,1,0:T(8,128)(2,1)}), bf16[8,2,32,128]{3,2,1,0:T(8,128)(2,1)S(1)}, u32[]{:S(2)}, u32[]{:S(2)}) %all-to-all-start.3) | async-done | bytes 131104 | tf_op jit(solution)/shard_map/all_to_all | solution.py:528
  93.8 0.7 shard_map.110
Async XLA Ops:
  1.7 4.4 %collective-permute-start.1 = (bf16[128,1024]{1,0:T(8,128)(2,1)S(1)}, bf16[128,1024]{1,0:T(8,128)(2,1)S(1)}, u32[]{:S(2)}, u32[]{:S(2)}) collective-permute-start(bf16[128,1024]{1,0:T(8,128)(2,1)S(1)} %get-tuple-element.39), channel_id=1, source_target_pairs={{0,8},{8,0},{1,9},{9,1},{2,10},{10,2},{3,11},{11,3},{4,12},{12,4},... | collective-permute-start | bytes 786440 | tf_op jit(solution)/shard_map/ppermute | solution.py:430
  1.8 11.1 %collective-permute-start = (bf16[128,1024]{1,0:T(8,128)(2,1)S(1)}, bf16[128,1024]{1,0:T(8,128)(2,1)S(1)}, u32[]{:S(2)}, u32[]{:S(2)}) collective-permute-start(bf16[128,1024]{1,0:T(8,128)(2,1)S(1)} %get-tuple-element.38), channel_id=1, source_target_pairs={{8,16},{24,32},{40,48},{56,64},{72,80},{88,96},{104,112},{120,128}... | collective-permute-start | bytes 786440 | tf_op jit(solution)/shard_map/ppermute | solution.py:431
  14.2 17.4 %copy-start = (f32[100,512]{1,0:T(8,128)S(1)}, f32[100,512]{1,0:T(8,128)}, u32[]{:S(2)}) copy-start(f32[100,512]{1,0:T(8,128)} %target_ref.1) | copy-start | bytes 614404
  14.2 17.4 %copy-start.1 = (s32[512]{0:T(512)S(1)}, s32[512]{0:T(512)}, u32[]{:S(2)}) copy-start(s32[512]{0:T(512)} %param.12) | copy-start | bytes 6148
  34.3 3.2 %collective-permute-start.2 = (bf16[16,9,32,128]{3,2,1,0:T(8,128)(2,1)S(1)}, bf16[16,9,32,128]{3,2,1,0:T(8,128)(2,1)S(1)}, u32[]{:S(2)}, u32[]{:S(2)}) collective-permute-start(bf16[16,9,32,128]{3,2,1,0:T(8,128)(2,1)S(1)} %get-tuple-element.55), channel_id=1, source_target_pairs={{0,8},{8,0},{1,9},{9,1},{2,10},{10,2},{3,11},{11,3},{4,12},{12,4},... | collective-permute-start | bytes 3538952 | tf_op jit(solution)/shard_map/ppermute | solution.py:479
  61.9 10.6 %copy-start.3 = (bf16[128,1024]{1,0:T(8,128)(2,1)S(1)}, bf16[128,1024]{1,0:T(8,128)(2,1)}, u32[]{:S(2)}) copy-start(bf16[128,1024]{1,0:T(8,128)(2,1)} %get-tuple-element.68) | copy-start | bytes 786436
  61.9 10.7 %copy-start.2 = (bf16[128,1024]{1,0:T(8,128)(2,1)S(1)}, bf16[128,1024]{1,0:T(8,128)(2,1)}, u32[]{:S(2)}) copy-start(bf16[128,1024]{1,0:T(8,128)(2,1)} %get-tuple-element.69) | copy-start | bytes 786436
  62.8 18.9 %all-to-all-start.2 = ((bf16[8,2,32,128]{3,2,1,0:T(8,128)(2,1)}), bf16[8,2,32,128]{3,2,1,0:T(8,128)(2,1)S(1)}, u32[]{:S(2)}, u32[]{:S(2)}) async-start(bf16[8,2,32,128]{3,2,1,0:T(8,128)(2,1)} %shard_map.108), calls=%async_computation.2 | async-start | bytes 262144 | tf_op jit(solution)/shard_map/all_to_all | solution.py:524
  72.5 13.3 %collective-permute-start.3 = (bf16[128,1024]{1,0:T(8,128)(2,1)S(1)}, bf16[128,1024]{1,0:T(8,128)(2,1)S(1)}, u32[]{:S(2)}, u32[]{:S(2)}) collective-permute-start(bf16[128,1024]{1,0:T(8,128)(2,1)S(1)} %copy-done.3), channel_id=1, source_target_pairs={{0,8},{8,0},{1,9},{9,1},{2,10},{10,2},{3,11},{11,3},{4,12},{12,4},... | collective-permute-start | bytes 786440 | tf_op jit(solution)/shard_map/ppermute | solution.py:504
  72.6 13.2 %collective-permute-start.4 = (bf16[128,1024]{1,0:T(8,128)(2,1)S(1)}, bf16[128,1024]{1,0:T(8,128)(2,1)S(1)}, u32[]{:S(2)}, u32[]{:S(2)}) collective-permute-start(bf16[128,1024]{1,0:T(8,128)(2,1)S(1)} %copy-done.2), channel_id=1, source_target_pairs={{8,16},{24,32},{40,48},{56,64},{72,80},{88,96},{104,112},{120,128}... | collective-permute-start | bytes 786440 | tf_op jit(solution)/shard_map/ppermute | solution.py:505
  82.4 11.4 %all-to-all-start.3 = ((bf16[8,2,32,128]{3,2,1,0:T(8,128)(2,1)}), bf16[8,2,32,128]{3,2,1,0:T(8,128)(2,1)S(1)}, u32[]{:S(2)}, u32[]{:S(2)}) async-start(bf16[8,2,32,128]{3,2,1,0:T(8,128)(2,1)} %shard_map.109), calls=%async_computation.3 | async-start | bytes 262144 | tf_op jit(solution)/shard_map/all_to_all | solution.py:528
